TPU v7x, 256 devices: a whole 4x4x8 slice. The times are simulated.
256 devices in a mesh: grp: 2 (over x_lo), ctx: 16 (over z, x_hi), tp: 8 (over y, core).
Axes of the slice: x: 4 (x_hi: 2, x_lo: 2; x = x_hi * 2 + x_lo), y: 4, z: 8, core: 2. Of those that a mesh axis runs over, the one named last changes fastest.
Arguments:
- key_value_cache: bfloat16 [2, 32, 3072, 2048], P('grp', 'ctx', None, 'tp'), may hold values from -6 to 6
- new_kv: bfloat16 [2, 32, 2048], P('grp', 'ctx', 'tp'), may hold values from -6 to 6
- final_query: bfloat16 [2, 32, 8192], P('grp', 'ctx', 'tp'), may hold values from -484 to 484
- out_weight: bfloat16 [2, 8192, 2560], P('grp', 'tp'), may hold values from -0.25 to 0.25
- lengths: int32 [32], replicated, may hold values from 1 to 3072, as said below
- block_plan: int32 [192], replicated, may hold values from 0 to 15, as said below
- queries: bfloat16 [2, 3072, 8192], P('grp', 'ctx', 'tp'), may hold values from -480 to 480
- output_gradient: bfloat16 [2, 3072, 8192], P('grp', 'ctx', 'tp'), may hold values from -6 to 6
Outputs:
- decoded: bfloat16 [2, 32, 2560], P('grp', 'ctx')
- attn_out: bfloat16 [2, 3072, 8192], P('grp', 'ctx', 'tp')
- grad_query: bfloat16 [2, 3072, 8192], P('grp', 'ctx', 'tp')
- grad_kv: bfloat16 [2, 3072, 2048], P('grp', 'ctx', 'tp')
Inputs may be any that keep to these rules, and one draw needn't show every extreme that they name: `lengths`: exactly one row has length 3072. `block_plan`: each shard number is given to exactly 12 blocks.
All inputs are finite; a program needn't handle non-finite values.
Results may differ from a plain program's by a relative error of at most 0.024.
Values may be sent and summed in bfloat16 or wider, within the bound.
No kernel may reach another device: no remote copies, remote signals or barrier semaphores. Data moves between devices by JAX's collectives and lax.ppermute only.
A program may use at most 128 MiB of HBM per device.

v0:
```python
import functools
import math

import jax
import jax.numpy as jnp
from jax import lax
from jax.experimental import pallas as pl
from jax.experimental.pallas import tpu as pltpu
from jax.sharding import PartitionSpec as P

HEAD = 128
TOKENS = 64
KEYS = 512
neg_big = -1e30


def attention_kernel(heads, blk, order_ref, meta_ref, *refs):
    kv_ref, q_ref, do_ref, o_ref, dq_ref, g_ref, kt_s, vt_s, s_s, p_s, dk_s, dv_s = refs
    total = kv_ref.shape[0]
    toks = q_ref.shape[0]
    gt, kc = TOKENS, KEYS
    rows = gt * heads
    sub = gt // blk
    me = meta_ref[0]
    learner = meta_ref[1]
    scale = HEAD ** -0.5
    factor = scale * math.log2(math.e)

    @pl.when(learner == 0)
    def _():
        o_ref[...] = jnp.zeros_like(o_ref)
        dq_ref[...] = jnp.zeros_like(dq_ref)
        g_ref[...] = jnp.zeros_like(g_ref)

    @pl.when(learner == 1)
    def _():
        for c in range(total // 256):
            part = pl.ds(c * 256, 256)
            kt_s[:, part] = kv_ref[part, :HEAD].T
            vt_s[:, part] = kv_ref[part, HEAD:].T
        dk_s[...] = jnp.zeros_like(dk_s)
        dv_s[...] = jnp.zeros_like(dv_s)

        def stacked(ref, base):
            return jnp.concatenate([ref[pl.ds(base, gt), h * HEAD:(h + 1) * HEAD] for h in range(heads)], axis=0)

        def spread(ref, base, value):
            for h in range(heads):
                ref[pl.ds(base, gt), h * HEAD:(h + 1) * HEAD] = value[h * gt:(h + 1) * gt]

        def group(g, _):
            base = pl.multiple_of(g * gt, gt)
            firsts = [order_ref[me * (toks // blk) + g * sub + s] * blk for s in range(sub)]
            lane = lax.rem(lax.broadcasted_iota(jnp.int32, (1, rows), 1), gt)
            pos = firsts[0] + lane
            for s in range(1, sub):
                pos = jnp.where(lane >= s * blk, firsts[s] + lane - s * blk, pos)
            full = lax.div(firsts[0] + 1, kc)
            last = lax.div(firsts[-1] + blk + kc - 1, kc)
            q = stacked(q_ref, base)
            qt = q.T
            dot_t = stacked(do_ref, base).T

            def scores(masked, c, m):
                part = pl.ds(pl.multiple_of(c * kc, kc), kc)
                s = jnp.dot(kv_ref[part, :HEAD], qt, preferred_element_type=jnp.float32)
                if masked:
                    kpos = c * kc + lax.broadcasted_iota(jnp.int32, (kc, rows), 0)
                    s = jnp.where(kpos <= pos, s, neg_big)
                s_s[part, :] = s
                return jnp.maximum(m, jnp.max(s.reshape(kc // 8, 8, rows), axis=0))

            m = jnp.full((8, rows), neg_big, jnp.float32)
            m = lax.fori_loop(0, full, functools.partial(scores, False), m)
            m = lax.fori_loop(full, last, functools.partial(scores, True), m)
            m = jnp.max(m, axis=0, keepdims=True)

            def weigh(c, carry):
                l, acc = carry
                part = pl.ds(pl.multiple_of(c * kc, kc), kc)
                p = jnp.exp2((s_s[part, :] - m) * factor)
                l = l + jnp.sum(p.reshape(kc // 8, 8, rows), axis=0)
                pb = p.astype(jnp.bfloat16)
                p_s[part, :] = pb
                acc = acc + jnp.dot(vt_s[:, part], pb, preferred_element_type=jnp.float32)
                return l, acc

            l, acc = lax.fori_loop(
                0, last, weigh, (jnp.zeros((8, rows), jnp.float32), jnp.zeros((HEAD, rows), jnp.float32))
            )
            inv = 1.0 / jnp.sum(l, axis=0, keepdims=True)
            ob = (acc * inv).astype(jnp.bfloat16)
            spread(o_ref, base, ob.T)
            dot_f = dot_t.astype(jnp.float32)
            delta = jnp.sum(dot_f * ob.astype(jnp.float32), axis=0, keepdims=True) * inv
            dots = (dot_f * inv).astype(jnp.bfloat16)
            dos = dots.T

            def back(c, acc):
                part = pl.ds(pl.multiple_of(c * kc, kc), kc)
                dp = jnp.dot(kv_ref[part, HEAD:], dots, preferred_element_type=jnp.float32)
                pb = p_s[part, :]
                ds = (pb.astype(jnp.float32) * (dp - delta)).astype(jnp.bfloat16)
                dv_s[part, :] += jnp.dot(pb, dos, preferred_element_type=jnp.float32)
                dk_s[part, :] += jnp.dot(ds, q, preferred_element_type=jnp.float32)
                return acc + jnp.dot(kt_s[:, part], ds, preferred_element_type=jnp.float32)

            acc = lax.fori_loop(0, last, back, jnp.zeros((HEAD, rows), jnp.float32))
            spread(dq_ref, base, (acc * scale).astype(jnp.bfloat16).T)
            return 0

        lax.fori_loop(0, toks // gt, group, 0)

        def put(i, _):
            src = pl.ds(pl.multiple_of(order_ref[i] * blk, blk), blk)
            dst = pl.ds(pl.multiple_of(i * blk, blk), blk)
            g_ref[dst, :HEAD] = (dk_s[src, :] * scale).astype(jnp.bfloat16)
            g_ref[dst, HEAD:] = dv_s[src, :].astype(jnp.bfloat16)
            return 0

        lax.fori_loop(0, total // blk, put, 0)


def attention(order, meta, kv, q, do):
    total = kv.shape[0]
    heads = q.shape[1] // HEAD
    rows = TOKENS * heads
    vmem = pl.BlockSpec(memory_space=pltpu.VMEM)
    smem = pl.BlockSpec(memory_space=pltpu.SMEM)
    rows_like = jax.ShapeDtypeStruct(q.shape, jnp.bfloat16)
    return pl.pallas_call(
        functools.partial(attention_kernel, heads, total // order.shape[0]),
        out_shape=(rows_like, rows_like, jax.ShapeDtypeStruct((total, 2 * HEAD), jnp.bfloat16)),
        in_specs=[smem, smem] + [vmem] * 3,
        out_specs=(vmem, vmem, vmem),
        scratch_shapes=[
            pltpu.VMEM((HEAD, total), jnp.bfloat16),
            pltpu.VMEM((HEAD, total), jnp.bfloat16),
            pltpu.VMEM((total, rows), jnp.float32),
            pltpu.VMEM((total, rows), jnp.bfloat16),
            pltpu.VMEM((total, HEAD), jnp.float32),
            pltpu.VMEM((total, HEAD), jnp.float32),
        ],
        compiler_params=pltpu.CompilerParams(vmem_limit_bytes=48 * 2**20),
    )(order, meta, kv, q, do)


def decode_rows(operands):
    cached, new_pair, final_query, row_lengths, weight_rows = operands
    row_count, total, _ = cached.shape
    heads = final_query.shape[1] // HEAD
    positions = jnp.arange(total, dtype=jnp.int32)
    is_last = (positions[None, :] == (row_lengths - 1)[:, None])[:, None, :]
    query = final_query.reshape(row_count, heads, HEAD)
    scores = jnp.einsum("rgd,rld->rgl", query, cached[:, :, :HEAD], preferred_element_type=jnp.float32)
    new_score = jnp.einsum("rgd,rd->rg", query, new_pair[:, :HEAD], preferred_element_type=jnp.float32)
    scores = jnp.where(is_last, new_score[:, :, None], scores) * HEAD ** -0.5
    valid = (positions[None, :] < row_lengths[:, None])[:, None, :]
    scores = jnp.where(valid, scores, neg_big)
    weights = jnp.where(valid, jnp.exp(scores - jnp.max(scores, axis=-1, keepdims=True)), 0.0)
    rounded = weights.astype(jnp.bfloat16)
    old = jnp.where(is_last, jnp.zeros_like(rounded), rounded)
    new = jnp.sum(jnp.where(is_last, rounded.astype(jnp.float32), 0.0), axis=-1)
    mixed = jnp.einsum("rgl,rld->rgd", old, cached[:, :, HEAD:], preferred_element_type=jnp.float32)
    mixed = mixed + new[:, :, None] * new_pair[:, None, HEAD:].astype(jnp.float32)
    attended = (mixed / jnp.sum(weights, axis=-1)[..., None]).astype(jnp.bfloat16)
    return jnp.dot(attended.reshape(row_count, heads * HEAD), weight_rows, preferred_element_type=jnp.float32)


def shards(
    key_value_cache, new_kv, final_query, out_weight, lengths, block_plan, queries, output_gradient
):
    grp_index = lax.axis_index("grp")
    ctx_index = lax.axis_index("ctx")
    ctx_size = lax.axis_size("ctx")
    tp_size = lax.axis_size("tp")
    ring = ctx_size // 2
    z_index = ctx_index // 2
    cached = key_value_cache[0]
    row_count, total, width = cached.shape
    run = total // ring
    row_ids = jnp.arange(lengths.shape[0], dtype=jnp.int32)
    finished = jnp.sum(jnp.where(lengths == total, row_ids, 0))
    owner = finished // row_count
    owner_z = owner // 2
    picked = finished % row_count
    new_row = lax.dynamic_index_in_dim(new_kv[0], picked, 0, keepdims=True)

    def own_run(i):
        part = lax.dynamic_slice(cached, (picked, i * run, 0), (1, run, width))[0]
        at = i * run + jnp.arange(run, dtype=jnp.int32)
        return jnp.where((at == total - 1)[:, None], new_row, part)

    runs = [own_run((z_index + step) % ring) for step in range(ring)]

    def scatter_from(first):
        def scatter(parts):
            got = parts[0]
            for step in range(1, ring):
                route = [
                    (z * 2 + column, (z + step) % ring * 2 + column)
                    for z in range(first, ring, classes)
                    for column in range(2)
                ]
                arrived = lax.ppermute(parts[step], ("grp", "ctx"), route)
                got = jnp.where((z_index - owner_z) % ring == step, arrived, got)
            return got

        return scatter

    classes = ring // 2
    held = lax.switch(owner_z % classes, [scatter_from(first) for first in range(classes)], runs)

    same = [(i, ctx_size + i) for i in range(ctx_size)]
    flipped = [(i, ctx_size + (i ^ 1)) for i in range(ctx_size)]
    from_same = lax.ppermute(held, ("grp", "ctx"), same)
    from_flipped = lax.ppermute(held, ("grp", "ctx"), flipped)
    mine = jnp.where(owner % 2 == ctx_index % 2, from_same, from_flipped)
    columns = [list(range(column, ctx_size, 2)) for column in range(2)]
    kv = lax.all_gather(mine, "ctx", axis=0, tiled=True, axis_index_groups=columns)

    block_count = block_plan.shape[0]
    order = jnp.argsort(block_plan, stable=True).astype(jnp.int32)
    meta = jnp.stack([ctx_index, grp_index]).astype(jnp.int32)
    attn_out, grad_query, grads = attention(
        order, meta, kv, queries[0], output_gradient[0]
    )
    piece = total // ctx_size
    spread = lax.all_to_all(grads.reshape(ctx_size, piece, width), "ctx", 0, 0)
    grad_pairs = jnp.sum(spread.astype(jnp.float32), axis=0).astype(jnp.bfloat16)

    row_lengths = lax.dynamic_slice_in_dim(lengths, ctx_index * row_count, row_count)
    held_query, _ = lax.optimization_barrier((final_query[0], held))
    partial_out = lax.cond(
        grp_index == 0,
        decode_rows,
        lambda operands: jnp.zeros((row_count, out_weight.shape[2]), jnp.float32),
        (cached, new_kv[0], held_query, row_lengths, out_weight[0]),
    )
    step = 1
    while step < tp_size:
        partial_out = partial_out + lax.ppermute(
            partial_out, ("grp", "tp"), [(i, i ^ step) for i in range(tp_size)]
        )
        step *= 2
    decoded = partial_out.astype(jnp.bfloat16)
    return (decoded[None], attn_out[None], grad_query[None], grad_pairs[None])


def solution(mesh):
    return jax.shard_map(
        shards,
        mesh=mesh,
        in_specs=(
            P("grp", "ctx", None, "tp"),
            P("grp", "ctx", "tp"),
            P("grp", "ctx", "tp"),
            P("grp", "tp", None),
            P(),
            P(),
            P("grp", "ctx", "tp"),
            P("grp", "ctx", "tp"),
        ),
        out_specs=(
            P("grp", "ctx", None),
            P("grp", "ctx", "tp"),
            P("grp", "ctx", "tp"),
            P("grp", "ctx", "tp"),
        ),
        check_vma=False,
    )
```

profile of v0, /device:TPU:2, one launch (start us, length us, event | category | flops | bytes accessed | tf_op | source)
XLA Modules:
  0.0 163.9 jit_solution(1557682550488295525)
XLA Ops:
  7.2 0.0 all-gather.2.cloned.1.call-start
  7.4 1.3 fusion.38
  11.4 0.7 fusion.37
  12.1 2.0 %bitcast_select_fusion = (bf16[384,256]{1,0:T(8,128)(2,1)S(1)}, bf16[384,256]{1,0:T(8,128)(2,1)S(1)}, bf16[384,256]{1,0:T(8,128)(2,1)S(1)}, bf16[384,256]{1,0:T(...) fusion(bf16[1,2,3072,256]{3,2,1,0:T(8,128)(2,1)} %param.14, ...), kind=kLoop, calls=%fused_computation.39 | loop fusion | flops 786432 | bytes 3149348 | tf_op jit(solution)/shard_map/jit(_where)/select_n | solution.py:192
  14.1 0.0 copy-start.4
  14.1 5.1 %conditional.2 = (bf16[384,256]{1,0:T(8,128)(2,1)S(1)}) conditional(s32[]{:T(128)} %clamp.3, (s32[]{:T(128)}, s32[]{:T(128)}, bf16[384,256]{1,0:T(8,128)(2,1)S(1)}, bf16[384,256]{1,0:T(8,128)(2,1)S(1)}, bf16[384,256]{1,0:T(8,128)(2,1)S(1)}, /*index=5*/bf16[384,256]{1,0:T(8,128)(2,1)S(1)}, ...), branch_computations={%region_1.2_spmd, %region_2.3_spmd, %region_3.4_spmd, %region_4.5_... | conditional | flops 688147 | bytes 7274975 | solution.py:212
  14.2 0.8 collective-permute-start.21
  15.0 0.7 collective-permute-start.22
  15.7 0.7 collective-permute-start.23
  16.4 0.7 collective-permute-start.24
  17.0 0.7 collective-permute-start.25
  17.7 0.7 collective-permute-start.26
  18.4 0.7 collective-permute-start.27
  19.2 0.1 select_select_fusion.3
  19.3 1.3 collective-permute-start.32
  20.6 1.3 collective-permute-start.31
  21.9 26.8 %collective-permute-done.32 = bf16[384,256]{1,0:T(8,128)(2,1)S(1)} collective-permute-done((bf16[384,256]{1,0:T(8,128)(2,1)S(1)}, bf16[384,256]{1,0:T(8,128)(2,1)S(1)}, u32[]{:S(2)}, u32[]{:S(2)}) %collective-permute-start.32) | collective-permute-done | bytes 196640 | tf_op jit(solution)/shard_map/ppermute | solution.py:217
  48.8 0.4 collective-permute-done.31
  49.1 0.7 broadcast_select_fusion
  49.8 0.0 all-gather.2.cloned.1.call-update
  49.9 3.2 %sort.17 = (s32[192]{0:T(256)}, s32[192]{0:T(256)S(1)}) sort(s32[192]{0:T(256)S(1)} %copy-done.4, s32[192]{0:T(256)S(1)} %iota.69), dimensions={0}, to_apply=%region_10.11 | sort | flops 1536 | bytes 3072 | tf_op jit(solution)/shard_map/jit(argsort)/sort | solution.py:223
  53.0 0.1 pad_add_fusion.meta_ref
  53.1 38.1 %all-gather.2.cloned.1.call-done.refs_0_ = bf16[3072,256]{1,0:T(8,128)(2,1)} async-done(((bf16[384,256]{1,0:T(8,128)(2,1)}), bf16[3072,256]{1,0:T(8,128)(2,1)}) %all-gather.2.cloned.1.call-update) | async-done | bytes 1572880 | tf_op jit(solution)/shard_map/all_gather | solution.py:220
  91.2 1.4 copy-done
  92.6 22.3 %shard_map.112 = (bf16[192,1024]{1,0:T(8,128)(2,1)}, bf16[192,1024]{1,0:T(8,128)(2,1)}, bf16[3072,256]{1,0:T(8,128)(2,1)}) custom-call(s32[192]{0:T(256)S(1)} %get-tuple-element.185.order_ref, s32[2]{0:T(128)S(1)} %pad_add_fusion.meta_ref, bf16[3072,256]{1,0:T(8,128)(2,1)S(1)} %copy-done, bf16[192,1024]{1,0:T(8,128)(2,1)S(1)} %bitcast.49, ...), custom_call_target="tpu_custom_call" | custom-call | tf_op jit(solution)/shard_map/pallas_call | solution.py:131
  114.9 5.9 %all-to-all-start = ((bf16[16,192,256]{2,1,0:T(8,128)(2,1)}), bf16[16,192,256]{2,1,0:T(8,128)(2,1)S(1)}, u32[]{:S(2)}, u32[]{:S(2)}) async-start(bf16[16,192,256]{2,1,0:T(8,128)(2,1)} %bitcast.22), calls=%async_computation | async-start | bytes 3145728 | tf_op jit(solution)/shard_map/all_to_all | solution.py:229
  120.9 0.7 collective-permute-start.28
  121.6 0.7 collective-permute-start.29
  122.3 0.7 collective-permute-start.30
  123.0 0.6 fusion.36
  123.6 32.6 %all-to-all-done = bf16[16,192,256]{2,1,0:T(8,128)(2,1)S(1)} async-done(((bf16[16,192,256]{2,1,0:T(8,128)(2,1)}), bf16[16,192,256]{2,1,0:T(8,128)(2,1)S(1)}, u32[]{:S(2)}, u32[]{:S(2)}) %all-to-all-start) | async-done | bytes 1572896 | tf_op jit(solution)/shard_map/all_to_all | solution.py:229
  156.2 0.9 reduce_sum.42
  (31 shorter events, 0.2 us)
Async XLA Ops:
  7.2 84.0 %all-gather.2.cloned.1.call-start = ((), (), s32[]{:S(2)}) async-start(), calls=%async_computation.1 | async-start | bytes 1769472 | tf_op jit(solution)/shard_map/all_gather | solution.py:220
  14.1 35.8 %copy-start.4 = (s32[192]{0:T(256)S(1)}, s32[192]{0:T(256)}, u32[]{:S(2)}) copy-start(s32[192]{0:T(256)} %param.19) | copy-start | bytes 2308
  14.1 77.1 %copy-start.1 = (bf16[1,192,1024]{2,1,0:T(8,128)(2,1)S(1)}, bf16[1,192,1024]{2,1,0:T(8,128)(2,1)}, u32[]{:S(2)}) copy-start(bf16[1,192,1024]{2,1,0:T(8,128)(2,1)} %param.20) | copy-start | bytes 1179652
  14.1 77.0 %copy-start.2 = (bf16[1,192,1024]{2,1,0:T(8,128)(2,1)S(1)}, bf16[1,192,1024]{2,1,0:T(8,128)(2,1)}, u32[]{:S(2)}) copy-start(bf16[1,192,1024]{2,1,0:T(8,128)(2,1)} %param.21) | copy-start | bytes 1179652
  14.2 3.5 %collective-permute-start.21 = (bf16[384,256]{1,0:T(8,128)(2,1)S(1)}, bf16[384,256]{1,0:T(8,128)(2,1)S(1)}, u32[]{:S(2)}, u32[]{:S(2)}) collective-permute-start(bf16[384,256]{1,0:T(8,128)(2,1)S(1)} %get-tuple-element.161), channel_id=1, source_target_pairs={{48,32},{56,40},{112,96},{120,104},{49,33},{57,41},{113,97},{121,1... | collective-permute-start | bytes 589832 | tf_op jit(solution)/shard_map/cond/branch_3_fun/ppermute | solution.py:205
  15.0 3.4 %collective-permute-start.22 = (bf16[384,256]{1,0:T(8,128)(2,1)S(1)}, bf16[384,256]{1,0:T(8,128)(2,1)S(1)}, u32[]{:S(2)}, u32[]{:S(2)}) collective-permute-start(bf16[384,256]{1,0:T(8,128)(2,1)S(1)} %get-tuple-element.162), channel_id=1, source_target_pairs={{48,16},{56,24},{112,80},{120,88},{49,17},{57,25},{113,81},{121,89... | collective-permute-start | bytes 589832 | tf_op jit(solution)/shard_map/cond/branch_3_fun/ppermute | solution.py:205
  15.7 3.5 %collective-permute-start.23 = (bf16[384,256]{1,0:T(8,128)(2,1)S(1)}, bf16[384,256]{1,0:T(8,128)(2,1)S(1)}, u32[]{:S(2)}, u32[]{:S(2)}) collective-permute-start(bf16[384,256]{1,0:T(8,128)(2,1)S(1)} %get-tuple-element.163), channel_id=1, source_target_pairs={{48,0},{56,8},{112,64},{120,72},{49,1},{57,9},{113,65},{121,73},{5... | collective-permute-start | bytes 589832 | tf_op jit(solution)/shard_map/cond/branch_3_fun/ppermute | solution.py:205
  16.4 2.8 %collective-permute-start.24 = (bf16[384,256]{1,0:T(8,128)(2,1)S(1)}, bf16[384,256]{1,0:T(8,128)(2,1)S(1)}, u32[]{:S(2)}, u32[]{:S(2)}) collective-permute-start(bf16[384,256]{1,0:T(8,128)(2,1)S(1)} %get-tuple-element.164), channel_id=1, source_target_pairs={{48,112},{56,120},{112,48},{120,56},{49,113},{57,121},{113,49},{12... | collective-permute-start | bytes 589832 | tf_op jit(solution)/shard_map/cond/branch_3_fun/ppermute | solution.py:205
  17.0 2.1 %collective-permute-start.25 = (bf16[384,256]{1,0:T(8,128)(2,1)S(1)}, bf16[384,256]{1,0:T(8,128)(2,1)S(1)}, u32[]{:S(2)}, u32[]{:S(2)}) collective-permute-start(bf16[384,256]{1,0:T(8,128)(2,1)S(1)} %get-tuple-element.165), channel_id=1, source_target_pairs={{48,96},{56,104},{112,32},{120,40},{49,97},{57,105},{113,33},{121,... | collective-permute-start | bytes 589832 | tf_op jit(solution)/shard_map/cond/branch_3_fun/ppermute | solution.py:205
  17.7 1.4 collective-permute-start.26
  18.4 0.8 collective-permute-start.27
  19.3 29.5 %collective-permute-start.32 = (bf16[384,256]{1,0:T(8,128)(2,1)S(1)}, bf16[384,256]{1,0:T(8,128)(2,1)S(1)}, u32[]{:S(2)}, u32[]{:S(2)}) collective-permute-start(bf16[384,256]{1,0:T(8,128)(2,1)S(1)} %get-tuple-element.221), channel_id=1, source_target_pairs={{0,136},{8,128},{16,152},{24,144},{32,168},{40,160},{48,184},{56,1... | collective-permute-start | bytes 589832 | tf_op jit(solution)/shard_map/ppermute | solution.py:217
  20.6 28.6 %collective-permute-start.31 = (bf16[384,256]{1,0:T(8,128)(2,1)S(1)}, bf16[384,256]{1,0:T(8,128)(2,1)S(1)}, u32[]{:S(2)}, u32[]{:S(2)}) collective-permute-start(bf16[384,256]{1,0:T(8,128)(2,1)S(1)} %get-tuple-element.221), channel_id=1, source_target_pairs={{0,128},{8,136},{16,144},{24,152},{32,160},{40,168},{48,176},{56,1... | collective-permute-start | bytes 589832 | tf_op jit(solution)/shard_map/ppermute | solution.py:216
  21.9 98.9 %copy-start.3 = (bf16[1,2,256]{2,1,0:T(2,128)(2,1)S(1)}, bf16[1,2,256]{2,1,0:T(2,128)(2,1)}, u32[]{:S(2)}) copy-start(bf16[1,2,256]{2,1,0:T(2,128)(2,1)} %param.15) | copy-start | bytes 3076
  21.9 98.9 %copy-start.5 = (s32[32]{0:T(128)S(1)}, s32[32]{0:T(128)}, u32[]{:S(2)}) copy-start(s32[32]{0:T(128)} %param.18) | copy-start | bytes 388
  21.9 98.9 %copy-start.6 = (bf16[1,2,1024]{2,1,0:T(2,128)(2,1)S(1)}, bf16[1,2,1024]{2,1,0:T(2,128)(2,1)}, u32[]{:S(2)}) copy-start(bf16[1,2,1024]{2,1,0:T(2,128)(2,1)} %param.16) | copy-start | bytes 12292
  91.2 1.4 copy-start
  114.9 41.3 %all-to-all-start = ((bf16[16,192,256]{2,1,0:T(8,128)(2,1)}), bf16[16,192,256]{2,1,0:T(8,128)(2,1)S(1)}, u32[]{:S(2)}, u32[]{:S(2)}) async-start(bf16[16,192,256]{2,1,0:T(8,128)(2,1)} %bitcast.22), calls=%async_computation | async-start | bytes 3145728 | tf_op jit(solution)/shard_map/all_to_all | solution.py:229
  120.9 0.7 collective-permute-start.28
  121.6 0.7 collective-permute-start.29
  122.3 0.7 collective-permute-start.30
Sparse Core Ops, SparseCore 0:
  50.0 41.1 all-gather.1
where the time goes:
time: 166 us; the launch traced here: 164 us
  waiting for transfers between devices  97.9 us (59%)
  Pallas kernels  22.3 us (13%)
  between operations  17.2 us (10%)
  starting transfers between devices  15.4 us (9%)
  other arithmetic  8.8 us (5%)
  local copies, waits for them, and re-layouts  2.16 us (1%)
    all_gather x1, waiting for transfers between devices, shards(): lax.all_gather(mine, 'ctx', axis=0, tiled=True, axis_index_groups=columns)  38.1 us
    all_to_all x1, waiting for transfers between devices, shards(): spread = lax.all_to_all(grads.reshape(ctx_size, piece, width), 'ctx', 0, 0)  32.6 us
    ppermute x1, waiting for transfers between devices, shards(): from_flipped = lax.ppermute(held, ('grp', 'ctx'), flipped)  26.8 us
    pallas_call x1, Pallas kernels, attention(): pl.pallas_call(functools.partial(attention_kernel, heads, total // order....  22.3 us
    all_to_all x1, starting transfers between devices, shards(): spread = lax.all_to_all(grads.reshape(ctx_size, piece, width), 'ctx', 0, 0)  5.92 us
    ppermute x7, starting transfers between devices, scatter(): arrived = lax.ppermute(parts[step], ('grp', 'ctx'), route)  4.84 us
  transfers between devices with their start and end apart: 14, of which 4 were waited for; matrix products, arithmetic and copies ran while one was open for 2% of the time, Pallas kernels for 0%

commit v1 on v0

--- a/solution.py
+++ b/solution.py
@@ -1,4 +1,5 @@
 import functools
+import itertools
 import math
 
 import jax
@@ -15,25 +16,45 @@
 
 
 def attention_kernel(heads, blk, order_ref, meta_ref, *refs):
-    kv_ref, q_ref, do_ref, o_ref, dq_ref, g_ref, kt_s, vt_s, s_s, p_s, dk_s, dv_s = refs
+    pieces, refs = refs[:6], refs[6:]
+    in_ref, out_ref, keep_ref, send_ref, kv_ref, kt_s, vt_s, s_s, p_s, dk_s, dv_s = refs
     total = kv_ref.shape[0]
-    toks = q_ref.shape[0]
+    toks = in_ref.shape[1]
     gt, kc = TOKENS, KEYS
     rows = gt * heads
     sub = gt // blk
     me = meta_ref[0]
     learner = meta_ref[1]
+    core = meta_ref[2]
     scale = HEAD ** -0.5
     factor = scale * math.log2(math.e)
 
     @pl.when(learner == 0)
     def _():
-        o_ref[...] = jnp.zeros_like(o_ref)
-        dq_ref[...] = jnp.zeros_like(dq_ref)
-        g_ref[...] = jnp.zeros_like(g_ref)
+        out_ref[...] = jnp.zeros_like(out_ref)
+        keep_ref[...] = jnp.zeros_like(keep_ref)
+        send_ref[...] = jnp.zeros_like(send_ref)
 
     @pl.when(learner == 1)
     def _():
+        run = pieces[0].shape[0]
+        half = run // 2
+        ring = total // run
+        z = lax.div(me, 2)
+        turn = 1 - 2 * core
+
+        def place(ref, first, size, steps, offset):
+            start = lax.rem(z + steps + ring, ring) * run + offset
+            for r in range(0, size, half):
+                kv_ref[pl.ds(pl.multiple_of(start + r, half), half), :] = ref[pl.ds(first + r, half), :]
+
+        place(pieces[0], 0, run, 0, 0)
+        for i in range(3):
+            place(pieces[1 + i], 0, run, -turn * (i + 1), 0)
+            place(pieces[5], i * run, run, turn * (i + 1), 0)
+        place(pieces[4], 0, half, 4, core * half)
+        place(pieces[5], 3 * run, half, 4, (1 - core) * half)
+
         for c in range(total // 256):
             part = pl.ds(c * 256, 256)
             kt_s[:, part] = kv_ref[part, :HEAD].T
@@ -41,12 +62,12 @@
         dk_s[...] = jnp.zeros_like(dk_s)
         dv_s[...] = jnp.zeros_like(dv_s)
 
-        def stacked(ref, base):
-            return jnp.concatenate([ref[pl.ds(base, gt), h * HEAD:(h + 1) * HEAD] for h in range(heads)], axis=0)
-
-        def spread(ref, base, value):
+        def stacked(which, base):
+            return jnp.concatenate([in_ref[which, pl.ds(base, gt), h * HEAD:(h + 1) * HEAD] for h in range(heads)], axis=0)
+
+        def spread(which, base, value):
             for h in range(heads):
-                ref[pl.ds(base, gt), h * HEAD:(h + 1) * HEAD] = value[h * gt:(h + 1) * gt]
+                out_ref[which, pl.ds(base, gt), h * HEAD:(h + 1) * HEAD] = value[h * gt:(h + 1) * gt]
 
         def group(g, _):
             base = pl.multiple_of(g * gt, gt)
@@ -57,9 +78,9 @@
                 pos = jnp.where(lane >= s * blk, firsts[s] + lane - s * blk, pos)
             full = lax.div(firsts[0] + 1, kc)
             last = lax.div(firsts[-1] + blk + kc - 1, kc)
-            q = stacked(q_ref, base)
+            q = stacked(0, base)
             qt = q.T
-            dot_t = stacked(do_ref, base).T
+            dot_t = stacked(1, base).T
 
             def scores(masked, c, m):
                 part = pl.ds(pl.multiple_of(c * kc, kc), kc)
@@ -90,7 +111,7 @@
             )
             inv = 1.0 / jnp.sum(l, axis=0, keepdims=True)
             ob = (acc * inv).astype(jnp.bfloat16)
-            spread(o_ref, base, ob.T)
+            spread(0, base, ob.T)
             dot_f = dot_t.astype(jnp.float32)
             delta = jnp.sum(dot_f * ob.astype(jnp.float32), axis=0, keepdims=True) * inv
             dots = (dot_f * inv).astype(jnp.bfloat16)
@@ -106,34 +127,41 @@
                 return acc + jnp.dot(kt_s[:, part], ds, preferred_element_type=jnp.float32)
 
             acc = lax.fori_loop(0, last, back, jnp.zeros((HEAD, rows), jnp.float32))
-            spread(dq_ref, base, (acc * scale).astype(jnp.bfloat16).T)
+            spread(1, base, (acc * scale).astype(jnp.bfloat16).T)
             return 0
 
         lax.fori_loop(0, toks // gt, group, 0)
 
-        def put(i, _):
-            src = pl.ds(pl.multiple_of(order_ref[i] * blk, blk), blk)
+        per = toks // blk
+
+        def put(parity, ref, i, _):
+            shard = lax.div(i, per) * 2 + parity
+            src = pl.ds(pl.multiple_of(order_ref[shard * per + lax.rem(i, per)] * blk, blk), blk)
             dst = pl.ds(pl.multiple_of(i * blk, blk), blk)
-            g_ref[dst, :HEAD] = (dk_s[src, :] * scale).astype(jnp.bfloat16)
-            g_ref[dst, HEAD:] = dv_s[src, :].astype(jnp.bfloat16)
+            ref[dst, :HEAD] = (dk_s[src, :] * scale).astype(ref.dtype)
+            ref[dst, HEAD:] = dv_s[src, :].astype(ref.dtype)
             return 0
 
-        lax.fori_loop(0, total // blk, put, 0)
-
-
-def attention(order, meta, kv, q, do):
-    total = kv.shape[0]
-    heads = q.shape[1] // HEAD
+        lax.fori_loop(0, total // blk // 2, functools.partial(put, core, keep_ref), 0)
+        lax.fori_loop(0, total // blk // 2, functools.partial(put, 1 - core, send_ref), 0)
+
+
+def attention(order, meta, pieces, token_rows, total):
+    heads = token_rows.shape[2] // HEAD
     rows = TOKENS * heads
     vmem = pl.BlockSpec(memory_space=pltpu.VMEM)
     smem = pl.BlockSpec(memory_space=pltpu.SMEM)
-    rows_like = jax.ShapeDtypeStruct(q.shape, jnp.bfloat16)
     return pl.pallas_call(
         functools.partial(attention_kernel, heads, total // order.shape[0]),
-        out_shape=(rows_like, rows_like, jax.ShapeDtypeStruct((total, 2 * HEAD), jnp.bfloat16)),
-        in_specs=[smem, smem] + [vmem] * 3,
+        out_shape=(
+            jax.ShapeDtypeStruct(token_rows.shape, jnp.bfloat16),
+            jax.ShapeDtypeStruct((total // 2, 2 * HEAD), jnp.float32),
+            jax.ShapeDtypeStruct((total // 2, 2 * HEAD), jnp.bfloat16),
+        ),
+        in_specs=[smem, smem] + [vmem] * 7,
         out_specs=(vmem, vmem, vmem),
         scratch_shapes=[
+            pltpu.VMEM((total, 2 * HEAD), jnp.bfloat16),
             pltpu.VMEM((HEAD, total), jnp.bfloat16),
             pltpu.VMEM((HEAD, total), jnp.bfloat16),
             pltpu.VMEM((total, rows), jnp.float32),
@@ -142,7 +170,7 @@
             pltpu.VMEM((total, HEAD), jnp.float32),
         ],
         compiler_params=pltpu.CompilerParams(vmem_limit_bytes=48 * 2**20),
-    )(order, meta, kv, q, do)
+    )(order, meta, *pieces, token_rows)
 
 
 def decode_rows(operands):
@@ -175,23 +203,47 @@
     ctx_size = lax.axis_size("ctx")
     tp_size = lax.axis_size("tp")
     ring = ctx_size // 2
-    z_index = ctx_index // 2
+    z_index, column = ctx_index >> 1, ctx_index & 1
+    core = lax.axis_index("tp") & 1
+
+    def route(groups, move):
+        pairs = []
+        for at in itertools.product(groups, range(ring), range(2), range(tp_size // 2), range(2)):
+            to = move(*at)
+            if to is not None and to != at:
+                pairs.append(tuple((((g * ring + z) * 2 + h) * tp_size) + y * 2 + c for g, z, h, y, c in (at, to)))
+        return pairs
+
+    def sent(x, pairs):
+        return lax.ppermute(x, ("grp", "ctx", "tp"), pairs)
+
+    swap = route((1,), lambda g, z, h, y, c: (g, z, c, y, h))
+    cores = route((0, 1), lambda g, z, h, y, c: (g, z, h, y, 1 - c))
+    around = route((1,), lambda g, z, h, y, c: (g, (z + 1 - 2 * c) % ring, h, y, c))
+    across = route((0,), lambda g, z, h, y, c: (1, z, c, y, h))
+
+    stays = column == core
+    token_rows = jnp.stack([queries[0], output_gradient[0]])
+    token_rows = jnp.where(stays, token_rows, sent(token_rows, swap))
     cached = key_value_cache[0]
     row_count, total, width = cached.shape
     run = total // ring
     row_ids = jnp.arange(lengths.shape[0], dtype=jnp.int32)
     finished = jnp.sum(jnp.where(lengths == total, row_ids, 0))
-    owner = finished // row_count
-    owner_z = owner // 2
-    picked = finished % row_count
-    new_row = lax.dynamic_index_in_dim(new_kv[0], picked, 0, keepdims=True)
+    owner = lax.div(finished, row_count)
+    owner_z = owner >> 1
+    picked = lax.rem(finished, row_count)
+    distance = lax.rem(z_index + ring - owner_z, ring)
+    new_row = lax.dynamic_slice(new_kv[0], (picked, 0), (1, width), allow_negative_indices=False)
 
     def own_run(i):
-        part = lax.dynamic_slice(cached, (picked, i * run, 0), (1, run, width))[0]
+        part = lax.dynamic_slice(
+            cached, (picked, i * run, 0), (1, run, width), allow_negative_indices=False
+        )[0]
         at = i * run + jnp.arange(run, dtype=jnp.int32)
         return jnp.where((at == total - 1)[:, None], new_row, part)
 
-    runs = [own_run((z_index + step) % ring) for step in range(ring)]
+    runs = [own_run(lax.rem(z_index + step, ring)) for step in range(ring)]
 
     def scatter_from(first):
         def scatter(parts):
@@ -203,31 +255,41 @@
                     for column in range(2)
                 ]
                 arrived = lax.ppermute(parts[step], ("grp", "ctx"), route)
-                got = jnp.where((z_index - owner_z) % ring == step, arrived, got)
+                got = jnp.where(distance == step, arrived, got)
             return got
 
         return scatter
 
     classes = ring // 2
-    held = lax.switch(owner_z % classes, [scatter_from(first) for first in range(classes)], runs)
-
-    same = [(i, ctx_size + i) for i in range(ctx_size)]
-    flipped = [(i, ctx_size + (i ^ 1)) for i in range(ctx_size)]
-    from_same = lax.ppermute(held, ("grp", "ctx"), same)
-    from_flipped = lax.ppermute(held, ("grp", "ctx"), flipped)
-    mine = jnp.where(owner % 2 == ctx_index % 2, from_same, from_flipped)
-    columns = [list(range(column, ctx_size, 2)) for column in range(2)]
-    kv = lax.all_gather(mine, "ctx", axis=0, tiled=True, axis_index_groups=columns)
-
-    block_count = block_plan.shape[0]
-    order = jnp.argsort(block_plan, stable=True).astype(jnp.int32)
-    meta = jnp.stack([ctx_index, grp_index]).astype(jnp.int32)
-    attn_out, grad_query, grads = attention(
-        order, meta, kv, queries[0], output_gradient[0]
+    held = lax.switch(lax.rem(owner_z, classes), [scatter_from(first) for first in range(classes)], runs)
+
+    landed = sent(held, across)
+    landed, token_rows, order = lax.optimization_barrier(
+        (landed, token_rows, jnp.argsort(block_plan, stable=True).astype(jnp.int32))
     )
-    piece = total // ctx_size
-    spread = lax.all_to_all(grads.reshape(ctx_size, piece, width), "ctx", 0, 0)
-    grad_pairs = jnp.sum(spread.astype(jnp.float32), axis=0).astype(jnp.bfloat16)
+    own = jnp.where(core == (owner & 1), landed, sent(landed, cores))
+    half = run // 2
+    passing, arrived = own, []
+    for step in range(4):
+        if step == 3:
+            passing = jnp.where(core == 0, passing[:half], passing[half:])
+        passing = sent(passing, around)
+        arrived.append(passing)
+    other = sent(jnp.concatenate(arrived, axis=0), cores)
+    pieces = [own] + arrived + [other]
+
+    meta = jnp.stack([z_index * 2 + core, grp_index, core]).astype(jnp.int32)
+    result_rows, kept, passed = attention(order, meta, pieces, token_rows, total)
+    summed = (kept + sent(passed, cores).astype(jnp.float32)).astype(jnp.bfloat16)
+    columns = [list(range(h, ctx_size, 2)) for h in range(2)]
+    spread = lax.all_to_all(
+        summed.reshape(ring, total // ctx_size, width), "ctx", 0, 0, axis_index_groups=columns
+    )
+    grads = jnp.sum(spread.astype(jnp.float32), axis=0).astype(jnp.bfloat16)
+    returned = sent(result_rows, swap)
+    attn_out = jnp.where(stays, result_rows[0], returned[0])
+    grad_query = jnp.where(stays, result_rows[1], returned[1])
+    grad_pairs = jnp.where(stays, grads, sent(grads, swap))
 
     row_lengths = lax.dynamic_slice_in_dim(lengths, ctx_index * row_count, row_count)
     held_query, _ = lax.optimization_barrier((final_query[0], held))
@@ -237,12 +299,9 @@
         lambda operands: jnp.zeros((row_count, out_weight.shape[2]), jnp.float32),
         (cached, new_kv[0], held_query, row_lengths, out_weight[0]),
     )
-    step = 1
-    while step < tp_size:
-        partial_out = partial_out + lax.ppermute(
-            partial_out, ("grp", "tp"), [(i, i ^ step) for i in range(tp_size)]
-        )
-        step *= 2
+    partial_out = partial_out + sent(partial_out, cores)
+    partial_out = partial_out + sent(partial_out, route((0,), lambda g, z, h, y, c: (g, z, h, y ^ 1, c)))
+    partial_out = partial_out + sent(partial_out, route((0,), lambda g, z, h, y, c: (g, z, h, y ^ 2, c)))
     decoded = partial_out.astype(jnp.bfloat16)
     return (decoded[None], attn_out[None], grad_query[None], grad_pairs[None])
 

time: 166 us -> 146 us (0.88)
  the two profiles are of different devices: /device:TPU:2 before, /device:TPU:11 now
where the time goes in v1:
time: 146 us
  waiting for transfers between devices  63 us (43%)
  starting transfers between devices  46 us (32%)
  Pallas kernels  21 us (14%)
  other arithmetic  10.2 us (7%)
  between operations  2.9 us (2%)
  local copies, waits for them, and re-layouts  2.78 us (2%)
    ppermute x14, waiting for transfers between devices, sent(): return lax.ppermute(x, ('grp', 'ctx', 'tp'), pairs)  44.7 us
    ppermute x14, starting transfers between devices, sent(): return lax.ppermute(x, ('grp', 'ctx', 'tp'), pairs)  36.2 us
    pallas_call x1, Pallas kernels, attention(): pl.pallas_call(functools.partial(attention_kernel, heads, total // order....  21 us
    all_to_all x1, waiting for transfers between devices, shards(): lax.all_to_all(summed.reshape(ring, total // ctx_size, width), 'ctx', 0,...  18.3 us
    all_to_all x1, starting transfers between devices, shards(): lax.all_to_all(summed.reshape(ring, total // ctx_size, width), 'ctx', 0,...  5.07 us
    ppermute x7, starting transfers between devices, scatter(): arrived = lax.ppermute(parts[step], ('grp', 'ctx'), route)  4.71 us
    sort x1, other arithmetic, shards(): jnp.argsort(block_plan, stable=True).astype(jnp.int32)  3.17 us
  transfers between devices with their start and end apart: 22, of which 12 were waited for; matrix products, arithmetic and copies ran while one was open for 3% of the time, Pallas kernels for 0%

profile of v1, /device:TPU:11, one launch (start us, length us, event | category | flops | bytes accessed | tf_op | source)
XLA Modules:
  0.0 146.1 jit_solution(4514762215158795999)
XLA Ops:
  0.6 1.3 fusion.38
  3.9 1.0 constant_dynamic-update-slice_fusion.1
  4.9 0.7 fusion.37
  5.7 1.0 constant_dynamic-update-slice_fusion
  6.7 2.0 %bitcast_select_fusion = (bf16[384,256]{1,0:T(8,128)(2,1)S(1)}, bf16[384,256]{1,0:T(8,128)(2,1)S(1)}, bf16[384,256]{1,0:T(8,128)(2,1)S(1)}, bf16[384,256]{1,0:T(...) fusion(bf16[1,2,3072,256]{3,2,1,0:T(8,128)(2,1)} %param.14, ...), kind=kLoop, calls=%fused_computation.44 | loop fusion | flops 786432 | bytes 3149348 | tf_op jit(solution)/shard_map/jit(_where)/select_n | solution.py:244
  8.7 5.0 %conditional.2 = (bf16[384,256]{1,0:T(8,128)(2,1)S(1)}) conditional(s32[]{:T(128)} %clamp.3, (s32[]{:T(128)}, bf16[384,256]{1,0:T(8,128)(2,1)S(1)}, bf16[384,256]{1,0:T(8,128)(2,1)S(1)}, bf16[384,256]{1,0:T(8,128)(2,1)S(1)}, bf16[384,256]{1,0:T(8,128)(2,1)S(1)}, /*index=5*/bf16[384,256]{1,0:T(8,128)(2,1)S(1)}, ...), branch_computations={%region_1.2_spmd, %region_2.3_spmd, %region_3.4_spmd, %region_4.5_... | conditional | flops 688135 | bytes 7274854 | solution.py:264
  13.7 4.3 %collective-permute-start.32 = (bf16[2,192,1024]{2,1,0:T(8,128)(2,1)S(1)}, bf16[2,192,1024]{2,1,0:T(8,128)(2,1)S(1)}, u32[]{:S(2)}, u32[]{:S(2)}) collective-permute-start(bf16[2,192,1024]{2,1,0:T(8,128)(2,1)S(1)} %constant_dynamic-update-slice_fusion), channel_id=1, source_target_pairs={{129,136},{131,138},{133,140},{135,142},{136,129},{138,131},{140,1... | collective-permute-start | bytes 2359304 | tf_op jit(solution)/shard_map/ppermute | solution.py:218
  18.0 1.3 collective-permute-start.31
  19.3 3.2 %sort.17 = (s32[192]{0:T(256)}, s32[192]{0:T(256)S(1)}) sort(s32[192]{0:T(256)S(1)} %copy-done.1, s32[192]{0:T(256)S(1)} %iota.69), dimensions={0}, to_apply=%region_10.11 | sort | flops 1536 | bytes 3072 | tf_op jit(solution)/shard_map/jit(argsort)/sort | solution.py:268
  22.5 6.0 %collective-permute-done.32 = bf16[2,192,1024]{2,1,0:T(8,128)(2,1)S(1)} collective-permute-done((bf16[2,192,1024]{2,1,0:T(8,128)(2,1)S(1)}, bf16[2,192,1024]{2,1,0:T(8,128)(2,1)S(1)}, u32[]{:S(2)}, u32[]{:S(2)}) %collective-permute-start.32) | collective-permute-done | bytes 786464 | tf_op jit(solution)/shard_map/ppermute | solution.py:218
  28.6 18.5 %collective-permute-done.31 = bf16[384,256]{1,0:T(8,128)(2,1)S(1)} collective-permute-done((bf16[384,256]{1,0:T(8,128)(2,1)S(1)}, bf16[384,256]{1,0:T(8,128)(2,1)S(1)}, u32[]{:S(2)}, u32[]{:S(2)}) %collective-permute-start.31) | collective-permute-done | bytes 196640 | tf_op jit(solution)/shard_map/ppermute | solution.py:218
  47.2 1.4 collective-permute-done.33
  48.6 4.9 %collective-permute-start.34 = (bf16[384,256]{1,0:T(8,128)(2,1)S(1)}, bf16[384,256]{1,0:T(8,128)(2,1)S(1)}, u32[]{:S(2)}, u32[]{:S(2)}) collective-permute-start(bf16[384,256]{1,0:T(8,128)(2,1)S(1)} %broadcast_select_fusion.1.refs_0_), channel_id=1, source_target_pairs={{128,144},{129,241},{130,146},{131,243},{132,148},{133,245},{134,1... | collective-permute-start | bytes 589832 | tf_op jit(solution)/shard_map/ppermute | solution.py:218
  53.6 2.6 %collective-permute-done.34.refs_1_ = bf16[384,256]{1,0:T(8,128)(2,1)S(1)} collective-permute-done((bf16[384,256]{1,0:T(8,128)(2,1)S(1)}, bf16[384,256]{1,0:T(8,128)(2,1)S(1)}, u32[]{:S(2)}, u32[]{:S(2)}) %collective-permute-start.34) | collective-permute-done | bytes 196640 | tf_op jit(solution)/shard_map/ppermute | solution.py:218
  56.2 5.0 %collective-permute-start.35 = (bf16[384,256]{1,0:T(8,128)(2,1)S(1)}, bf16[384,256]{1,0:T(8,128)(2,1)S(1)}, u32[]{:S(2)}, u32[]{:S(2)}) collective-permute-start(bf16[384,256]{1,0:T(8,128)(2,1)S(1)} %collective-permute-done.34.refs_1_), channel_id=1, source_target_pairs={{128,144},{129,241},{130,146},{131,243},{132,148},{133,245},{134,1... | collective-permute-start | bytes 589832 | tf_op jit(solution)/shard_map/ppermute | solution.py:218
  61.2 2.6 %collective-permute-done.35.refs_2_ = bf16[384,256]{1,0:T(8,128)(2,1)S(1)} collective-permute-done((bf16[384,256]{1,0:T(8,128)(2,1)S(1)}, bf16[384,256]{1,0:T(8,128)(2,1)S(1)}, u32[]{:S(2)}, u32[]{:S(2)}) %collective-permute-start.35) | collective-permute-done | bytes 196640 | tf_op jit(solution)/shard_map/ppermute | solution.py:218
  63.8 5.0 %collective-permute-start.36 = (bf16[384,256]{1,0:T(8,128)(2,1)S(1)}, bf16[384,256]{1,0:T(8,128)(2,1)S(1)}, u32[]{:S(2)}, u32[]{:S(2)}) collective-permute-start(bf16[384,256]{1,0:T(8,128)(2,1)S(1)} %collective-permute-done.35.refs_2_), channel_id=1, source_target_pairs={{128,144},{129,241},{130,146},{131,243},{132,148},{133,245},{134,1... | collective-permute-start | bytes 589832 | tf_op jit(solution)/shard_map/ppermute | solution.py:218
  68.8 2.6 %collective-permute-done.36.refs_3_ = bf16[384,256]{1,0:T(8,128)(2,1)S(1)} collective-permute-done((bf16[384,256]{1,0:T(8,128)(2,1)S(1)}, bf16[384,256]{1,0:T(8,128)(2,1)S(1)}, u32[]{:S(2)}, u32[]{:S(2)}) %collective-permute-start.36) | collective-permute-done | bytes 196640 | tf_op jit(solution)/shard_map/ppermute | solution.py:218
  71.4 5.0 %collective-permute-start.37 = (bf16[192,256]{1,0:T(8,128)(2,1)S(1)}, bf16[192,256]{1,0:T(8,128)(2,1)S(1)}, u32[]{:S(2)}, u32[]{:S(2)}) collective-permute-start(bf16[192,256]{1,0:T(8,128)(2,1)S(1)} %slice_select_fusion.2), channel_id=1, source_target_pairs={{128,144},{129,241},{130,146},{131,243},{132,148},{133,245},{134,1... | collective-permute-start | bytes 294920 | tf_op jit(solution)/shard_map/ppermute | solution.py:218
  76.4 1.6 %collective-permute-done.37.refs_4_ = bf16[192,256]{1,0:T(8,128)(2,1)S(1)} collective-permute-done((bf16[192,256]{1,0:T(8,128)(2,1)S(1)}, bf16[192,256]{1,0:T(8,128)(2,1)S(1)}, u32[]{:S(2)}, u32[]{:S(2)}) %collective-permute-start.37) | collective-permute-done | bytes 98336 | tf_op jit(solution)/shard_map/ppermute | solution.py:218
  78.1 4.9 %collective-permute-start.38 = (bf16[1344,256]{1,0:T(8,128)(2,1)S(1)}, bf16[1344,256]{1,0:T(8,128)(2,1)S(1)}, u32[]{:S(2)}, u32[]{:S(2)}) collective-permute-start(bf16[1344,256]{1,0:T(8,128)(2,1)S(1)} %pad_maximum_fusion), channel_id=1, source_target_pairs={{0,1},{1,0},{2,3},{3,2},{4,5},{5,4},{6,7},{7,6},{8,9},{9,8},{10,11... | collective-permute-start | bytes 2064392 | tf_op jit(solution)/shard_map/ppermute | solution.py:218
  83.1 1.7 %collective-permute-done.38.refs_5_ = bf16[1344,256]{1,0:T(8,128)(2,1)S(1)} collective-permute-done((bf16[1344,256]{1,0:T(8,128)(2,1)S(1)}, bf16[1344,256]{1,0:T(8,128)(2,1)S(1)}, u32[]{:S(2)}, u32[]{:S(2)}) %collective-permute-start.38) | collective-permute-done | bytes 688160 | tf_op jit(solution)/shard_map/ppermute | solution.py:218
  84.8 21.0 %shard_map.112 = (bf16[2,192,1024]{2,1,0:T(8,128)(2,1)S(1)}, f32[1536,256]{1,0:T(8,128)S(1)}, bf16[1536,256]{1,0:T(8,128)(2,1)S(1)}) custom-call(s32[192]{0:T(256)S(1)} %get-tuple-element.177.order_ref, s32[3]{0:T(128)S(1)} %pad_add_fusion.meta_ref, bf16[384,256]{1,0:T(8,128)(2,1)S(1)} %broadcast_select_fusion.1.refs_0_, ...), custom_call_target="tpu_custom_call" | custom-call | tf_op jit(solution)/shard_map/pallas_call | solution.py:154
  106.2 1.9 %collective-permute-done.40 = bf16[1536,256]{1,0:T(8,128)(2,1)S(1)} collective-permute-done((bf16[1536,256]{1,0:T(8,128)(2,1)S(1)}, bf16[1536,256]{1,0:T(8,128)(2,1)S(1)}, u32[]{:S(2)}, u32[]{:S(2)}) %collective-permute-start.40) | collective-permute-done | bytes 786464 | tf_op jit(solution)/shard_map/ppermute | solution.py:218
  108.2 1.1 add_convert_fusion
  109.3 5.1 %all-to-all-start = ((bf16[8,192,256]{2,1,0:T(8,128)(2,1)}), bf16[8,192,256]{2,1,0:T(8,128)(2,1)S(1)}, u32[]{:S(2)}, u32[]{:S(2)}) async-start(bf16[8,192,256]{2,1,0:T(8,128)(2,1)} %bitcast.19), calls=%async_computation | async-start | bytes 1572864 | tf_op jit(solution)/shard_map/all_to_all | solution.py:285
  114.3 1.9 %collective-permute-start.39 = (bf16[2,192,1024]{2,1,0:T(8,128)(2,1)S(1)}, bf16[2,192,1024]{2,1,0:T(8,128)(2,1)S(1)}, u32[]{:S(2)}, u32[]{:S(2)}) collective-permute-start(bf16[2,192,1024]{2,1,0:T(8,128)(2,1)S(1)} %get-tuple-element.180), channel_id=1, source_target_pairs={{129,136},{131,138},{133,140},{135,142},{136,129},{138,131},{140,1... | collective-permute-start | bytes 2359304 | tf_op jit(solution)/shard_map/ppermute | solution.py:218
  116.4 1.2 collective-permute-done.28
  119.6 18.3 %all-to-all-done = bf16[8,192,256]{2,1,0:T(8,128)(2,1)S(1)} async-done(((bf16[8,192,256]{2,1,0:T(8,128)(2,1)}), bf16[8,192,256]{2,1,0:T(8,128)(2,1)S(1)}, u32[]{:S(2)}, u32[]{:S(2)}) %all-to-all-start) | async-done | bytes 786464 | tf_op jit(solution)/shard_map/all_to_all | solution.py:285
  138.0 1.9 %collective-permute-start.41 = (bf16[192,256]{1,0:T(8,128)(2,1)S(1)}, bf16[192,256]{1,0:T(8,128)(2,1)S(1)}, u32[]{:S(2)}, u32[]{:S(2)}) collective-permute-start(bf16[192,256]{1,0:T(8,128)(2,1)S(1)} %reduce_sum.42), channel_id=1, source_target_pairs={{129,136},{131,138},{133,140},{135,142},{136,129},{138,131},{140,1... | collective-permute-start | bytes 294920 | tf_op jit(solution)/shard_map/ppermute | solution.py:218
  139.9 1.0 slice_select_fusion
  140.9 4.5 %collective-permute-done.41 = bf16[192,256]{1,0:T(8,128)(2,1)S(1)} collective-permute-done((bf16[192,256]{1,0:T(8,128)(2,1)S(1)}, bf16[192,256]{1,0:T(8,128)(2,1)S(1)}, u32[]{:S(2)}, u32[]{:S(2)}) %collective-permute-start.41) | collective-permute-done | bytes 98336 | tf_op jit(solution)/shard_map/ppermute | solution.py:218
  (48 shorter events, 8.4 us)
Async XLA Ops:
  8.7 10.6 %copy-start.1 = (s32[192]{0:T(256)S(1)}, s32[192]{0:T(256)}, u32[]{:S(2)}) copy-start(s32[192]{0:T(256)} %param.19) | copy-start | bytes 2308
  8.7 3.4 %collective-permute-start.14 = (bf16[384,256]{1,0:T(8,128)(2,1)S(1)}, bf16[384,256]{1,0:T(8,128)(2,1)S(1)}, u32[]{:S(2)}, u32[]{:S(2)}) collective-permute-start(bf16[384,256]{1,0:T(8,128)(2,1)S(1)} %get-tuple-element.140), channel_id=1, source_target_pairs={{32,16},{40,24},{96,80},{104,88},{33,17},{41,25},{97,81},{105,89},... | collective-permute-start | bytes 589832 | tf_op jit(solution)/shard_map/cond/branch_2_fun/ppermute | solution.py:257
  9.4 3.4 %collective-permute-start.15 = (bf16[384,256]{1,0:T(8,128)(2,1)S(1)}, bf16[384,256]{1,0:T(8,128)(2,1)S(1)}, u32[]{:S(2)}, u32[]{:S(2)}) collective-permute-start(bf16[384,256]{1,0:T(8,128)(2,1)S(1)} %get-tuple-element.141), channel_id=1, source_target_pairs={{32,0},{40,8},{96,64},{104,72},{33,1},{41,9},{97,65},{105,73},{34,... | collective-permute-start | bytes 589832 | tf_op jit(solution)/shard_map/cond/branch_2_fun/ppermute | solution.py:257
  10.1 3.4 %collective-permute-start.16 = (bf16[384,256]{1,0:T(8,128)(2,1)S(1)}, bf16[384,256]{1,0:T(8,128)(2,1)S(1)}, u32[]{:S(2)}, u32[]{:S(2)}) collective-permute-start(bf16[384,256]{1,0:T(8,128)(2,1)S(1)} %get-tuple-element.142), channel_id=1, source_target_pairs={{32,112},{40,120},{96,48},{104,56},{33,113},{41,121},{97,49},{105,... | collective-permute-start | bytes 589832 | tf_op jit(solution)/shard_map/cond/branch_2_fun/ppermute | solution.py:257
  10.8 2.8 %collective-permute-start.17 = (bf16[384,256]{1,0:T(8,128)(2,1)S(1)}, bf16[384,256]{1,0:T(8,128)(2,1)S(1)}, u32[]{:S(2)}, u32[]{:S(2)}) collective-permute-start(bf16[384,256]{1,0:T(8,128)(2,1)S(1)} %get-tuple-element.143), channel_id=1, source_target_pairs={{32,96},{40,104},{96,32},{104,40},{33,97},{41,105},{97,33},{105,41... | collective-permute-start | bytes 589832 | tf_op jit(solution)/shard_map/cond/branch_2_fun/ppermute | solution.py:257
  11.5 2.1 %collective-permute-start.18 = (bf16[384,256]{1,0:T(8,128)(2,1)S(1)}, bf16[384,256]{1,0:T(8,128)(2,1)S(1)}, u32[]{:S(2)}, u32[]{:S(2)}) collective-permute-start(bf16[384,256]{1,0:T(8,128)(2,1)S(1)} %get-tuple-element.144), channel_id=1, source_target_pairs={{32,80},{40,88},{96,16},{104,24},{33,81},{41,89},{97,17},{105,25},... | collective-permute-start | bytes 589832 | tf_op jit(solution)/shard_map/cond/branch_2_fun/ppermute | solution.py:257
  12.2 1.4 collective-permute-start.19
  12.9 0.7 collective-permute-start.20
  13.7 14.8 %collective-permute-start.32 = (bf16[2,192,1024]{2,1,0:T(8,128)(2,1)S(1)}, bf16[2,192,1024]{2,1,0:T(8,128)(2,1)S(1)}, u32[]{:S(2)}, u32[]{:S(2)}) collective-permute-start(bf16[2,192,1024]{2,1,0:T(8,128)(2,1)S(1)} %constant_dynamic-update-slice_fusion), channel_id=1, source_target_pairs={{129,136},{131,138},{133,140},{135,142},{136,129},{138,131},{140,1... | collective-permute-start | bytes 2359304 | tf_op jit(solution)/shard_map/ppermute | solution.py:218
  18.0 29.1 %collective-permute-start.31 = (bf16[384,256]{1,0:T(8,128)(2,1)S(1)}, bf16[384,256]{1,0:T(8,128)(2,1)S(1)}, u32[]{:S(2)}, u32[]{:S(2)}) collective-permute-start(bf16[384,256]{1,0:T(8,128)(2,1)S(1)} %get-tuple-element.217), channel_id=1, source_target_pairs={{0,128},{1,136},{2,130},{3,138},{4,132},{5,140},{6,134},{7,142},{8... | collective-permute-start | bytes 589832 | tf_op jit(solution)/shard_map/ppermute | solution.py:218
  47.2 1.4 collective-permute-start.33
  48.6 7.5 %collective-permute-start.34 = (bf16[384,256]{1,0:T(8,128)(2,1)S(1)}, bf16[384,256]{1,0:T(8,128)(2,1)S(1)}, u32[]{:S(2)}, u32[]{:S(2)}) collective-permute-start(bf16[384,256]{1,0:T(8,128)(2,1)S(1)} %broadcast_select_fusion.1.refs_0_), channel_id=1, source_target_pairs={{128,144},{129,241},{130,146},{131,243},{132,148},{133,245},{134,1... | collective-permute-start | bytes 589832 | tf_op jit(solution)/shard_map/ppermute | solution.py:218
  56.2 7.6 %collective-permute-start.35 = (bf16[384,256]{1,0:T(8,128)(2,1)S(1)}, bf16[384,256]{1,0:T(8,128)(2,1)S(1)}, u32[]{:S(2)}, u32[]{:S(2)}) collective-permute-start(bf16[384,256]{1,0:T(8,128)(2,1)S(1)} %collective-permute-done.34.refs_1_), channel_id=1, source_target_pairs={{128,144},{129,241},{130,146},{131,243},{132,148},{133,245},{134,1... | collective-permute-start | bytes 589832 | tf_op jit(solution)/shard_map/ppermute | solution.py:218
  63.8 7.6 %collective-permute-start.36 = (bf16[384,256]{1,0:T(8,128)(2,1)S(1)}, bf16[384,256]{1,0:T(8,128)(2,1)S(1)}, u32[]{:S(2)}, u32[]{:S(2)}) collective-permute-start(bf16[384,256]{1,0:T(8,128)(2,1)S(1)} %collective-permute-done.35.refs_2_), channel_id=1, source_target_pairs={{128,144},{129,241},{130,146},{131,243},{132,148},{133,245},{134,1... | collective-permute-start | bytes 589832 | tf_op jit(solution)/shard_map/ppermute | solution.py:218
  71.4 6.7 %collective-permute-start.37 = (bf16[192,256]{1,0:T(8,128)(2,1)S(1)}, bf16[192,256]{1,0:T(8,128)(2,1)S(1)}, u32[]{:S(2)}, u32[]{:S(2)}) collective-permute-start(bf16[192,256]{1,0:T(8,128)(2,1)S(1)} %slice_select_fusion.2), channel_id=1, source_target_pairs={{128,144},{129,241},{130,146},{131,243},{132,148},{133,245},{134,1... | collective-permute-start | bytes 294920 | tf_op jit(solution)/shard_map/ppermute | solution.py:218
  78.1 6.7 %collective-permute-start.38 = (bf16[1344,256]{1,0:T(8,128)(2,1)S(1)}, bf16[1344,256]{1,0:T(8,128)(2,1)S(1)}, u32[]{:S(2)}, u32[]{:S(2)}) collective-permute-start(bf16[1344,256]{1,0:T(8,128)(2,1)S(1)} %pad_maximum_fusion), channel_id=1, source_target_pairs={{0,1},{1,0},{2,3},{3,2},{4,5},{5,4},{6,7},{7,6},{8,9},{9,8},{10,11... | collective-permute-start | bytes 2064392 | tf_op jit(solution)/shard_map/ppermute | solution.py:218
  105.8 2.4 %collective-permute-start.40 = (bf16[1536,256]{1,0:T(8,128)(2,1)S(1)}, bf16[1536,256]{1,0:T(8,128)(2,1)S(1)}, u32[]{:S(2)}, u32[]{:S(2)}) collective-permute-start(bf16[1536,256]{1,0:T(8,128)(2,1)S(1)} %get-tuple-element.182), channel_id=1, source_target_pairs={{0,1},{1,0},{2,3},{3,2},{4,5},{5,4},{6,7},{7,6},{8,9},{9,8},{10,11... | collective-permute-start | bytes 2359304 | tf_op jit(solution)/shard_map/ppermute | solution.py:218
  109.2 7.0 %copy-start = (bf16[1,2,256]{2,1,0:T(2,128)(2,1)S(1)}, bf16[1,2,256]{2,1,0:T(2,128)(2,1)}, u32[]{:S(2)}) copy-start(bf16[1,2,256]{2,1,0:T(2,128)(2,1)} %param.15) | copy-start | bytes 3076
  109.2 7.0 %copy-start.2 = (s32[32]{0:T(128)S(1)}, s32[32]{0:T(128)}, u32[]{:S(2)}) copy-start(s32[32]{0:T(128)} %param.18) | copy-start | bytes 388
  109.2 7.0 %copy-start.3 = (bf16[1,2,1024]{2,1,0:T(2,128)(2,1)S(1)}, bf16[1,2,1024]{2,1,0:T(2,128)(2,1)}, u32[]{:S(2)}) copy-start(bf16[1,2,1024]{2,1,0:T(2,128)(2,1)} %param.16) | copy-start | bytes 12292
  109.3 28.6 %all-to-all-start = ((bf16[8,192,256]{2,1,0:T(8,128)(2,1)}), bf16[8,192,256]{2,1,0:T(8,128)(2,1)S(1)}, u32[]{:S(2)}, u32[]{:S(2)}) async-start(bf16[8,192,256]{2,1,0:T(8,128)(2,1)} %bitcast.19), calls=%async_computation | async-start | bytes 1572864 | tf_op jit(solution)/shard_map/all_to_all | solution.py:285
  114.3 25.6 %collective-permute-start.39 = (bf16[2,192,1024]{2,1,0:T(8,128)(2,1)S(1)}, bf16[2,192,1024]{2,1,0:T(8,128)(2,1)S(1)}, u32[]{:S(2)}, u32[]{:S(2)}) collective-permute-start(bf16[2,192,1024]{2,1,0:T(8,128)(2,1)S(1)} %get-tuple-element.180), channel_id=1, source_target_pairs={{129,136},{131,138},{133,140},{135,142},{136,129},{138,131},{140,1... | collective-permute-start | bytes 2359304 | tf_op jit(solution)/shard_map/ppermute | solution.py:218
  116.3 1.3 collective-permute-start.28
  117.6 0.7 collective-permute-start.29
  118.3 0.7 collective-permute-start.30
  138.0 7.4 %collective-permute-start.41 = (bf16[192,256]{1,0:T(8,128)(2,1)S(1)}, bf16[192,256]{1,0:T(8,128)(2,1)S(1)}, u32[]{:S(2)}, u32[]{:S(2)}) collective-permute-start(bf16[192,256]{1,0:T(8,128)(2,1)S(1)} %reduce_sum.42), channel_id=1, source_target_pairs={{129,136},{131,138},{133,140},{135,142},{136,129},{138,131},{140,1... | collective-permute-start | bytes 294920 | tf_op jit(solution)/shard_map/ppermute | solution.py:218

commit v2 on v1

--- a/solution.py
+++ b/solution.py
@@ -10,16 +10,15 @@
 from jax.sharding import PartitionSpec as P
 
 HEAD = 128
-TOKENS = 64
-KEYS = 512
+TOKENS = 96
+KEYS = 768
 neg_big = -1e30
 
 
 def attention_kernel(heads, blk, order_ref, meta_ref, *refs):
-    pieces, refs = refs[:6], refs[6:]
-    in_ref, out_ref, keep_ref, send_ref, kv_ref, kt_s, vt_s, s_s, p_s, dk_s, dv_s = refs
+    mine_ref, other_ref, q_ref, do_ref, o_ref, dq_ref, keep_ref, send_ref, kv_ref, kt_s, vt_s, s_s, p_s, dk_s, dv_s = refs
     total = kv_ref.shape[0]
-    toks = in_ref.shape[1]
+    toks = q_ref.shape[0]
     gt, kc = TOKENS, KEYS
     rows = gt * heads
     sub = gt // blk
@@ -31,29 +30,18 @@
 
     @pl.when(learner == 0)
     def _():
-        out_ref[...] = jnp.zeros_like(out_ref)
+        o_ref[...] = jnp.zeros_like(o_ref)
+        dq_ref[...] = jnp.zeros_like(dq_ref)
         keep_ref[...] = jnp.zeros_like(keep_ref)
         send_ref[...] = jnp.zeros_like(send_ref)
 
     @pl.when(learner == 1)
     def _():
-        run = pieces[0].shape[0]
-        half = run // 2
-        ring = total // run
-        z = lax.div(me, 2)
-        turn = 1 - 2 * core
-
-        def place(ref, first, size, steps, offset):
-            start = lax.rem(z + steps + ring, ring) * run + offset
-            for r in range(0, size, half):
-                kv_ref[pl.ds(pl.multiple_of(start + r, half), half), :] = ref[pl.ds(first + r, half), :]
-
-        place(pieces[0], 0, run, 0, 0)
-        for i in range(3):
-            place(pieces[1 + i], 0, run, -turn * (i + 1), 0)
-            place(pieces[5], i * run, run, turn * (i + 1), 0)
-        place(pieces[4], 0, half, 4, core * half)
-        place(pieces[5], 3 * run, half, 4, (1 - core) * half)
+        half = toks
+        for r in range(total // half // 2):
+            for ref, which in ((mine_ref, core), (other_ref, 1 - core)):
+                start = pl.multiple_of((2 * r + which) * half, half)
+                kv_ref[pl.ds(start, half), :] = ref[r * half:(r + 1) * half, :]
 
         for c in range(total // 256):
             part = pl.ds(c * 256, 256)
@@ -62,12 +50,12 @@
         dk_s[...] = jnp.zeros_like(dk_s)
         dv_s[...] = jnp.zeros_like(dv_s)
 
-        def stacked(which, base):
-            return jnp.concatenate([in_ref[which, pl.ds(base, gt), h * HEAD:(h + 1) * HEAD] for h in range(heads)], axis=0)
-
-        def spread(which, base, value):
+        def stacked(ref, base):
+            return jnp.concatenate([ref[pl.ds(base, gt), h * HEAD:(h + 1) * HEAD] for h in range(heads)], axis=0)
+
+        def spread(ref, base, value):
             for h in range(heads):
-                out_ref[which, pl.ds(base, gt), h * HEAD:(h + 1) * HEAD] = value[h * gt:(h + 1) * gt]
+                ref[pl.ds(base, gt), h * HEAD:(h + 1) * HEAD] = value[h * gt:(h + 1) * gt]
 
         def group(g, _):
             base = pl.multiple_of(g * gt, gt)
@@ -78,9 +66,9 @@
                 pos = jnp.where(lane >= s * blk, firsts[s] + lane - s * blk, pos)
             full = lax.div(firsts[0] + 1, kc)
             last = lax.div(firsts[-1] + blk + kc - 1, kc)
-            q = stacked(0, base)
+            q = stacked(q_ref, base)
             qt = q.T
-            dot_t = stacked(1, base).T
+            dot_t = stacked(do_ref, base).T
 
             def scores(masked, c, m):
                 part = pl.ds(pl.multiple_of(c * kc, kc), kc)
@@ -111,7 +99,7 @@
             )
             inv = 1.0 / jnp.sum(l, axis=0, keepdims=True)
             ob = (acc * inv).astype(jnp.bfloat16)
-            spread(0, base, ob.T)
+            spread(o_ref, base, ob.T)
             dot_f = dot_t.astype(jnp.float32)
             delta = jnp.sum(dot_f * ob.astype(jnp.float32), axis=0, keepdims=True) * inv
             dots = (dot_f * inv).astype(jnp.bfloat16)
@@ -127,7 +115,7 @@
                 return acc + jnp.dot(kt_s[:, part], ds, preferred_element_type=jnp.float32)
 
             acc = lax.fori_loop(0, last, back, jnp.zeros((HEAD, rows), jnp.float32))
-            spread(1, base, (acc * scale).astype(jnp.bfloat16).T)
+            spread(dq_ref, base, (acc * scale).astype(jnp.bfloat16).T)
             return 0
 
         lax.fori_loop(0, toks // gt, group, 0)
@@ -142,24 +130,26 @@
             ref[dst, HEAD:] = dv_s[src, :].astype(ref.dtype)
             return 0
 
-        lax.fori_loop(0, total // blk // 2, functools.partial(put, core, keep_ref), 0)
-        lax.fori_loop(0, total // blk // 2, functools.partial(put, 1 - core, send_ref), 0)
-
-
-def attention(order, meta, pieces, token_rows, total):
-    heads = token_rows.shape[2] // HEAD
+        lax.fori_loop(0, total // blk // 2, functools.partial(put, core, keep_ref), 0, unroll=8)
+        lax.fori_loop(0, total // blk // 2, functools.partial(put, 1 - core, send_ref), 0, unroll=8)
+
+
+def attention(order, meta, mine, other, q, do):
+    total = mine.shape[0] * 2
+    heads = q.shape[1] // HEAD
     rows = TOKENS * heads
     vmem = pl.BlockSpec(memory_space=pltpu.VMEM)
     smem = pl.BlockSpec(memory_space=pltpu.SMEM)
     return pl.pallas_call(
         functools.partial(attention_kernel, heads, total // order.shape[0]),
         out_shape=(
-            jax.ShapeDtypeStruct(token_rows.shape, jnp.bfloat16),
+            jax.ShapeDtypeStruct(q.shape, jnp.bfloat16),
+            jax.ShapeDtypeStruct(q.shape, jnp.bfloat16),
             jax.ShapeDtypeStruct((total // 2, 2 * HEAD), jnp.float32),
             jax.ShapeDtypeStruct((total // 2, 2 * HEAD), jnp.bfloat16),
         ),
-        in_specs=[smem, smem] + [vmem] * 7,
-        out_specs=(vmem, vmem, vmem),
+        in_specs=[smem, smem] + [vmem] * 4,
+        out_specs=(vmem, vmem, vmem, vmem),
         scratch_shapes=[
             pltpu.VMEM((total, 2 * HEAD), jnp.bfloat16),
             pltpu.VMEM((HEAD, total), jnp.bfloat16),
@@ -170,7 +160,51 @@
             pltpu.VMEM((total, HEAD), jnp.float32),
         ],
         compiler_params=pltpu.CompilerParams(vmem_limit_bytes=48 * 2**20),
-    )(order, meta, *pieces, token_rows)
+    )(order, meta, mine, other, q, do)
+
+
+def runs_kernel(lengths_ref, z_ref, cached_ref, new_ref, owner_ref, *refs):
+    run_refs, sems = refs[:-1], refs[-1]
+    ring = len(run_refs)
+    run = run_refs[0].shape[0]
+    row_count, total, _ = cached_ref.shape
+    finished = jnp.int32(0)
+    for r in range(lengths_ref.shape[0]):
+        finished = jnp.where(lengths_ref[r] == total, r, finished)
+    picked = lax.rem(finished, row_count)
+    owner_ref[0] = lax.div(finished, row_count)
+    copies = []
+    for step, ref in enumerate(run_refs):
+        start = pl.multiple_of(lax.rem(z_ref[0] + step, ring) * run, run)
+        copies.append(pltpu.make_async_copy(cached_ref.at[picked, pl.ds(start, run)], ref, sems.at[step]))
+    for copy in copies:
+        copy.start()
+    new_row = new_ref[0:1, :]
+    for r in range(1, row_count):
+        new_row = jnp.where(picked == r, new_ref[r:r + 1, :], new_row)
+    for copy in copies:
+        copy.wait()
+    for step, ref in enumerate(run_refs):
+        @pl.when(lax.rem(z_ref[0] + step, ring) == ring - 1)
+        def _(ref=ref):
+            at = lax.broadcasted_iota(jnp.int32, (16, ref.shape[1]), 0)
+            tail = pl.ds(run - 16, 16)
+            ref[tail, :] = jnp.where(at == 15, new_row, ref[tail, :])
+
+
+def finished_runs(lengths, z_index, cached, new_pairs, ring):
+    total, width = cached.shape[1:]
+    vmem = pl.BlockSpec(memory_space=pltpu.VMEM)
+    smem = pl.BlockSpec(memory_space=pltpu.SMEM)
+    return pl.pallas_call(
+        runs_kernel,
+        out_shape=[jax.ShapeDtypeStruct((1,), jnp.int32)]
+        + [jax.ShapeDtypeStruct((total // ring, width), cached.dtype)] * ring,
+        in_specs=[smem, smem, pl.BlockSpec(memory_space=pl.ANY), vmem],
+        out_specs=[smem] + [vmem] * ring,
+        scratch_shapes=[pltpu.SemaphoreType.DMA((ring,))],
+        compiler_params=pltpu.CompilerParams(vmem_limit_bytes=16 * 2**20),
+    )(lengths, z_index.reshape(1), cached, new_pairs)
 
 
 def decode_rows(operands):
@@ -206,11 +240,11 @@
     z_index, column = ctx_index >> 1, ctx_index & 1
     core = lax.axis_index("tp") & 1
 
-    def route(groups, move):
+    def route(groups, move, stay=False):
         pairs = []
         for at in itertools.product(groups, range(ring), range(2), range(tp_size // 2), range(2)):
             to = move(*at)
-            if to is not None and to != at:
+            if stay or to != at:
                 pairs.append(tuple((((g * ring + z) * 2 + h) * tp_size) + y * 2 + c for g, z, h, y, c in (at, to)))
         return pairs
 
@@ -218,32 +252,18 @@
         return lax.ppermute(x, ("grp", "ctx", "tp"), pairs)
 
     swap = route((1,), lambda g, z, h, y, c: (g, z, c, y, h))
+    swap_all = route((1,), lambda g, z, h, y, c: (g, z, c, y, h), True)
     cores = route((0, 1), lambda g, z, h, y, c: (g, z, h, y, 1 - c))
-    around = route((1,), lambda g, z, h, y, c: (g, (z + 1 - 2 * c) % ring, h, y, c))
     across = route((0,), lambda g, z, h, y, c: (1, z, c, y, h))
 
-    stays = column == core
-    token_rows = jnp.stack([queries[0], output_gradient[0]])
-    token_rows = jnp.where(stays, token_rows, sent(token_rows, swap))
     cached = key_value_cache[0]
     row_count, total, width = cached.shape
     run = total // ring
-    row_ids = jnp.arange(lengths.shape[0], dtype=jnp.int32)
-    finished = jnp.sum(jnp.where(lengths == total, row_ids, 0))
-    owner = lax.div(finished, row_count)
+    half = run // 2
+    owner, *runs = finished_runs(lengths, z_index, cached, new_kv[0], ring)
+    owner = owner[0]
     owner_z = owner >> 1
-    picked = lax.rem(finished, row_count)
     distance = lax.rem(z_index + ring - owner_z, ring)
-    new_row = lax.dynamic_slice(new_kv[0], (picked, 0), (1, width), allow_negative_indices=False)
-
-    def own_run(i):
-        part = lax.dynamic_slice(
-            cached, (picked, i * run, 0), (1, run, width), allow_negative_indices=False
-        )[0]
-        at = i * run + jnp.arange(run, dtype=jnp.int32)
-        return jnp.where((at == total - 1)[:, None], new_row, part)
-
-    runs = [own_run(lax.rem(z_index + step, ring)) for step in range(ring)]
 
     def scatter_from(first):
         def scatter(parts):
@@ -263,33 +283,31 @@
     classes = ring // 2
     held = lax.switch(lax.rem(owner_z, classes), [scatter_from(first) for first in range(classes)], runs)
 
+    stays = column == core
+    query_rows = sent(queries[0], swap_all)
+    gradient_rows = sent(output_gradient[0], swap)
+    gradient_rows = jnp.where(stays, output_gradient[0], gradient_rows)
     landed = sent(held, across)
-    landed, token_rows, order = lax.optimization_barrier(
-        (landed, token_rows, jnp.argsort(block_plan, stable=True).astype(jnp.int32))
+    landed, query_rows, gradient_rows, order = lax.optimization_barrier(
+        (landed, query_rows, gradient_rows, jnp.argsort(block_plan, stable=True).astype(jnp.int32))
     )
-    own = jnp.where(core == (owner & 1), landed, sent(landed, cores))
-    half = run // 2
-    passing, arrived = own, []
-    for step in range(4):
-        if step == 3:
-            passing = jnp.where(core == 0, passing[:half], passing[half:])
-        passing = sent(passing, around)
-        arrived.append(passing)
-    other = sent(jnp.concatenate(arrived, axis=0), cores)
-    pieces = [own] + arrived + [other]
+    low, high = landed[:half], landed[half:]
+    handed = sent(jnp.where(core == 0, high, low), cores)
+    own = jnp.where(core == (owner & 1), jnp.where(core == 0, low, high), handed)
+    columns = [list(range(h, ctx_size, 2)) for h in range(2)]
+    mine = lax.all_gather(own, "ctx", axis=0, tiled=True, axis_index_groups=columns)
+    other = sent(mine, cores)
 
     meta = jnp.stack([z_index * 2 + core, grp_index, core]).astype(jnp.int32)
-    result_rows, kept, passed = attention(order, meta, pieces, token_rows, total)
+    attn_rows, grad_rows, kept, passed = attention(order, meta, mine, other, query_rows, gradient_rows)
     summed = (kept + sent(passed, cores).astype(jnp.float32)).astype(jnp.bfloat16)
-    columns = [list(range(h, ctx_size, 2)) for h in range(2)]
     spread = lax.all_to_all(
         summed.reshape(ring, total // ctx_size, width), "ctx", 0, 0, axis_index_groups=columns
     )
+    attn_out = sent(attn_rows, swap_all)
+    grad_query = jnp.where(stays, grad_rows, sent(grad_rows, swap))
     grads = jnp.sum(spread.astype(jnp.float32), axis=0).astype(jnp.bfloat16)
-    returned = sent(result_rows, swap)
-    attn_out = jnp.where(stays, result_rows[0], returned[0])
-    grad_query = jnp.where(stays, result_rows[1], returned[1])
-    grad_pairs = jnp.where(stays, grads, sent(grads, swap))
+    grad_pairs = sent(grads, swap_all)
 
     row_lengths = lax.dynamic_slice_in_dim(lengths, ctx_index * row_count, row_count)
     held_query, _ = lax.optimization_barrier((final_query[0], held))

time: 146 us -> 137 us (0.938); the launches traced: 146 us -> 139 us
  blocking collectives: 0 us -> 21.4 us
  waiting for transfers between devices: 63 us -> 43.6 us
  starting transfers between devices: 46 us -> 41.3 us
  other arithmetic: 10.2 us -> 6.01 us
  Pallas kernels: 21 us -> 23.1 us
    all_gather x0 -> x1, blocking collectives: none -> 21.4 us  [shards(): lax.all_gather(own, 'ctx', axis=0, tiled=True, axis_index_groups=columns)]
    ppermute x14 -> x12, waiting for transfers between devices: 44.7 us -> 30.7 us  [sent(): return lax.ppermute(x, ('grp', 'ctx', 'tp'), pairs)]
    ppermute x14 -> x12, starting transfers between devices: 36.2 us -> 28.9 us  [sent(): return lax.ppermute(x, ('grp', 'ctx', 'tp'), pairs)]
    all_to_all x1, waiting for transfers between devices: 18.3 us -> 12.8 us  [shards(): lax.all_to_all(summed.reshape(ring, total // ctx_size, width), 'ctx', 0,...]
    select_n x5 -> x3, other arithmetic: 3.06 us -> 0.08 us  [the longest x1 0.06 us: shards(): gradient_rows = jnp.where(stays, output_gradient[0], gradient_rows)]
    pallas_call x0 -> x1, Pallas kernels: none -> 2.78 us  [finished_runs(): pl.pallas_call(runs_kernel, out_shape=[jax.ShapeDtypeStruct((1,), jnp.int...]
    all_to_all x1, starting transfers between devices: 5.07 us -> 7.59 us  [shards(): lax.all_to_all(summed.reshape(ring, total // ctx_size, width), 'ctx', 0,...]
  transfers between devices with their start and end apart: 22 -> 20, of which waited for: 12 -> 7; matrix products, arithmetic and copies ran while one was open for 3% -> 3% of each run, Pallas kernels for 0% -> 0%
where the time goes in v2:
time: 137 us; the launch traced here: 139 us
  waiting for transfers between devices  43.6 us (32%)
  starting transfers between devices  41.3 us (30%)
  Pallas kernels  23.1 us (17%)
  blocking collectives  21.4 us (16%)
  other arithmetic  6.01 us (4%)
  between operations  2.05 us (1%)
  local copies, waits for them, and re-layouts  1.43 us (1%)
    ppermute x12, waiting for transfers between devices, sent(): return lax.ppermute(x, ('grp', 'ctx', 'tp'), pairs)  30.7 us
    ppermute x12, starting transfers between devices, sent(): return lax.ppermute(x, ('grp', 'ctx', 'tp'), pairs)  28.9 us
    all_gather x1, blocking collectives, shards(): lax.all_gather(own, 'ctx', axis=0, tiled=True, axis_index_groups=columns)  21.4 us
    pallas_call x1, Pallas kernels, attention(): pl.pallas_call(functools.partial(attention_kernel, heads, total // order....  20.3 us
    all_to_all x1, waiting for transfers between devices, shards(): lax.all_to_all(summed.reshape(ring, total // ctx_size, width), 'ctx', 0,...  12.8 us
    all_to_all x1, starting transfers between devices, shards(): lax.all_to_all(summed.reshape(ring, total // ctx_size, width), 'ctx', 0,...  7.59 us
    ppermute x7, starting transfers between devices, scatter(): arrived = lax.ppermute(parts[step], ('grp', 'ctx'), route)  4.84 us
    sort x1, other arithmetic, shards(): jnp.argsort(block_plan, stable=True).astype(jnp.int32)  3.17 us
  transfers between devices with their start and end apart: 20, of which 7 were waited for; matrix products, arithmetic and copies ran while one was open for 3% of the time, Pallas kernels for 0%

profile of v2, /device:TPU:11, one launch (start us, length us, event | category | flops | bytes accessed | tf_op | source)
XLA Modules:
  0.0 139.1 jit_solution(1709034971961203680)
XLA Ops:
  0.6 2.8 %shard_map.112 = (s32[1]{0:T(128)}, bf16[384,256]{1,0:T(8,128)(2,1)S(1)}, bf16[384,256]{1,0:T(8,128)(2,1)S(1)}, bf16[384,256]{1,0:T(8,128)(2,1)S(1)}, bf16[384,2...) custom-call(s32[32]{0:T(128)} %lengths_ref.1, ...), custom_call_target="tpu_custom_call" | custom-call | tf_op jit(solution)/shard_map/pallas_call | solution.py:199
  4.1 5.1 %conditional.2 = (bf16[384,256]{1,0:T(8,128)(2,1)S(1)}) conditional(s32[]{:T(128)} %clamp.3, (s32[]{:T(128)}, bf16[384,256]{1,0:T(8,128)(2,1)S(1)}, bf16[384,256]{1,0:T(8,128)(2,1)S(1)}, bf16[384,256]{1,0:T(8,128)(2,1)S(1)}, bf16[384,256]{1,0:T(8,128)(2,1)S(1)}, /*index=5*/bf16[384,256]{1,0:T(8,128)(2,1)S(1)}, ...), branch_computations={%region_0.1_spmd, %region_1.2_spmd, %region_2.3_spmd, %region_3.4_... | conditional | flops 688135 | bytes 7274854 | solution.py:284
  4.1 0.8 collective-permute-start
  4.9 0.7 collective-permute-start.1
  5.6 0.7 collective-permute-start.2
  6.2 0.7 collective-permute-start.3
  6.9 0.7 collective-permute-start.4
  7.6 0.7 collective-permute-start.5
  8.3 0.7 collective-permute-start.6
  9.2 4.3 %collective-permute-start.33 = (bf16[192,1024]{1,0:T(8,128)(2,1)S(1)}, bf16[192,1024]{1,0:T(8,128)(2,1)S(1)}, u32[]{:S(2)}, u32[]{:S(2)}) collective-permute-start(bf16[192,1024]{1,0:T(8,128)(2,1)S(1)} %bitcast.42), channel_id=1, source_target_pairs={{129,136},{131,138},{133,140},{135,142},{136,129},{138,131},{140,1... | collective-permute-start | bytes 1179656 | tf_op jit(solution)/shard_map/ppermute | solution.py:252
  13.5 2.8 %collective-permute-start.32 = (bf16[192,1024]{1,0:T(8,128)(2,1)S(1)}, bf16[192,1024]{1,0:T(8,128)(2,1)S(1)}, u32[]{:S(2)}, u32[]{:S(2)}) collective-permute-start(bf16[192,1024]{1,0:T(8,128)(2,1)S(1)} %bitcast.46), channel_id=1, source_target_pairs={{128,128},{129,136},{130,130},{131,138},{132,132},{133,140},{134,1... | collective-permute-start | bytes 1179656 | tf_op jit(solution)/shard_map/ppermute | solution.py:252
  16.3 1.3 collective-permute-start.31
  17.6 3.2 %sort.17 = (s32[192]{0:T(256)}, s32[192]{0:T(256)S(1)}) sort(s32[192]{0:T(256)S(1)} %copy-done.3, s32[192]{0:T(256)S(1)} %iota.17), dimensions={0}, to_apply=%region_9.10 | sort | flops 1536 | bytes 3072 | tf_op jit(solution)/shard_map/jit(argsort)/sort | solution.py:292
  20.8 21.5 %collective-permute-done.31 = bf16[384,256]{1,0:T(8,128)(2,1)S(1)} collective-permute-done((bf16[384,256]{1,0:T(8,128)(2,1)S(1)}, bf16[384,256]{1,0:T(8,128)(2,1)S(1)}, u32[]{:S(2)}, u32[]{:S(2)}) %collective-permute-start.31) | collective-permute-done | bytes 196640 | tf_op jit(solution)/shard_map/ppermute | solution.py:252
  43.1 0.7 collective-permute-done.34
  43.8 21.4 %all_gather.3.refs_0_ = bf16[1536,256]{1,0:T(8,128)(2,1)S(1)} all-gather(bf16[192,256]{1,0:T(8,128)(2,1)S(1)} %select_select_fusion.4), channel_id=1, replica_groups={{0,16,32,48,64,80,96,112},{8,24,40,56,72,88,104,120},{1,17,33,49,65,81,..., dimensions={0}, use_global_device_ids=true | all-gather | bytes 884736 | tf_op jit(solution)/shard_map/all_gather | solution.py:298
  65.2 5.2 %collective-permute-start.35 = (bf16[1536,256]{1,0:T(8,128)(2,1)S(1)}, bf16[1536,256]{1,0:T(8,128)(2,1)S(1)}, u32[]{:S(2)}, u32[]{:S(2)}) collective-permute-start(bf16[1536,256]{1,0:T(8,128)(2,1)S(1)} %all_gather.3.refs_0_), channel_id=1, source_target_pairs={{0,1},{1,0},{2,3},{3,2},{4,5},{5,4},{6,7},{7,6},{8,9},{9,8},{10,11... | collective-permute-start | bytes 2359304 | tf_op jit(solution)/shard_map/ppermute | solution.py:252
  70.5 1.8 %collective-permute-done.35.refs_1_ = bf16[1536,256]{1,0:T(8,128)(2,1)S(1)} collective-permute-done((bf16[1536,256]{1,0:T(8,128)(2,1)S(1)}, bf16[1536,256]{1,0:T(8,128)(2,1)S(1)}, u32[]{:S(2)}, u32[]{:S(2)}) %collective-permute-start.35) | collective-permute-done | bytes 786464 | tf_op jit(solution)/shard_map/ppermute | solution.py:252
  72.3 20.3 %shard_map.113 = (bf16[192,1024]{1,0:T(8,128)(2,1)S(1)}, bf16[192,1024]{1,0:T(8,128)(2,1)S(1)}, f32[1536,256]{1,0:T(8,128)S(1)}, bf16[1536,256]{1,0:T(8,128)(2,1)S(1)}) custom-call(s32[192]{0:T(256)S(1)} %get-tuple-element.195.order_ref, s32[3]{0:T(128)S(1)} %pad_add_fusion.meta_ref, bf16[1536,256]{1,0:T(8,128)(2,1)S(1)} %all_gather.3.refs_0_, ...), custom_call_target="tpu_custom_call" | custom-call | tf_op jit(solution)/shard_map/pallas_call | solution.py:143
  92.8 2.3 %collective-permute-done.38 = bf16[1536,256]{1,0:T(8,128)(2,1)S(1)} collective-permute-done((bf16[1536,256]{1,0:T(8,128)(2,1)S(1)}, bf16[1536,256]{1,0:T(8,128)(2,1)S(1)}, u32[]{:S(2)}, u32[]{:S(2)}) %collective-permute-start.38) | collective-permute-done | bytes 786464 | tf_op jit(solution)/shard_map/ppermute | solution.py:252
  95.1 1.1 add_convert_fusion
  96.1 7.6 %all-to-all-start = ((bf16[8,192,256]{2,1,0:T(8,128)(2,1)}), bf16[8,192,256]{2,1,0:T(8,128)(2,1)S(1)}, u32[]{:S(2)}, u32[]{:S(2)}) async-start(bf16[8,192,256]{2,1,0:T(8,128)(2,1)} %bitcast.18), calls=%async_computation | async-start | bytes 1572864 | tf_op jit(solution)/shard_map/all_to_all | solution.py:304
  103.8 0.7 collective-permute-start.28
  104.5 0.8 collective-permute-done.28
  105.4 0.7 collective-permute-start.29
  106.7 1.9 %collective-permute-start.36 = (bf16[192,1024]{1,0:T(8,128)(2,1)S(1)}, bf16[192,1024]{1,0:T(8,128)(2,1)S(1)}, u32[]{:S(2)}, u32[]{:S(2)}) collective-permute-start(bf16[192,1024]{1,0:T(8,128)(2,1)S(1)} %get-tuple-element.199), channel_id=1, source_target_pairs={{128,128},{129,136},{130,130},{131,138},{132,132},{133,140},{134,1... | collective-permute-start | bytes 1179656 | tf_op jit(solution)/shard_map/ppermute | solution.py:252
  108.7 5.1 %collective-permute-start.37 = (bf16[192,1024]{1,0:T(8,128)(2,1)S(1)}, bf16[192,1024]{1,0:T(8,128)(2,1)S(1)}, u32[]{:S(2)}, u32[]{:S(2)}) collective-permute-start(bf16[192,1024]{1,0:T(8,128)(2,1)S(1)} %get-tuple-element.200), channel_id=1, source_target_pairs={{129,136},{131,138},{133,140},{135,142},{136,129},{138,131},{140,1... | collective-permute-start | bytes 1179656 | tf_op jit(solution)/shard_map/ppermute | solution.py:252
  114.5 12.8 %all-to-all-done = bf16[8,192,256]{2,1,0:T(8,128)(2,1)S(1)} async-done(((bf16[8,192,256]{2,1,0:T(8,128)(2,1)}), bf16[8,192,256]{2,1,0:T(8,128)(2,1)S(1)}, u32[]{:S(2)}, u32[]{:S(2)}) %all-to-all-start) | async-done | bytes 786464 | tf_op jit(solution)/shard_map/all_to_all | solution.py:304
  127.4 6.0 %collective-permute-start.39 = (bf16[192,256]{1,0:T(8,128)(2,1)S(1)}, bf16[192,256]{1,0:T(8,128)(2,1)S(1)}, u32[]{:S(2)}, u32[]{:S(2)}) collective-permute-start(bf16[192,256]{1,0:T(8,128)(2,1)S(1)} %reduce_sum.32), channel_id=1, source_target_pairs={{128,128},{129,136},{130,130},{131,138},{132,132},{133,140},{134,1... | collective-permute-start | bytes 294920 | tf_op jit(solution)/shard_map/ppermute | solution.py:252
  133.4 0.8 select_bitcast_fusion
  134.2 3.5 %collective-permute-done.39 = bf16[192,256]{1,0:T(8,128)(2,1)S(1)} collective-permute-done((bf16[192,256]{1,0:T(8,128)(2,1)S(1)}, bf16[192,256]{1,0:T(8,128)(2,1)S(1)}, u32[]{:S(2)}, u32[]{:S(2)}) %collective-permute-start.39) | collective-permute-done | bytes 98336 | tf_op jit(solution)/shard_map/ppermute | solution.py:252
  137.7 0.7 copy.41
  (41 shorter events, 2.6 us)
Async XLA Ops:
  4.0 5.1 %copy-start = (bf16[1,192,1024]{2,1,0:T(8,128)(2,1)S(1)}, bf16[1,192,1024]{2,1,0:T(8,128)(2,1)}, u32[]{:S(2)}) copy-start(bf16[1,192,1024]{2,1,0:T(8,128)(2,1)} %param.21) | copy-start | bytes 1179652
  4.0 9.5 %copy-start.4 = (bf16[1,192,1024]{2,1,0:T(8,128)(2,1)S(1)}, bf16[1,192,1024]{2,1,0:T(8,128)(2,1)}, u32[]{:S(2)}) copy-start(bf16[1,192,1024]{2,1,0:T(8,128)(2,1)} %param.20) | copy-start | bytes 1179652
  4.0 13.5 %copy-start.3 = (s32[192]{0:T(256)S(1)}, s32[192]{0:T(256)}, u32[]{:S(2)}) copy-start(s32[192]{0:T(256)} %param.19) | copy-start | bytes 2308
  4.1 3.5 %collective-permute-start = (bf16[384,256]{1,0:T(8,128)(2,1)S(1)}, bf16[384,256]{1,0:T(8,128)(2,1)S(1)}, u32[]{:S(2)}, u32[]{:S(2)}) collective-permute-start(bf16[384,256]{1,0:T(8,128)(2,1)S(1)} %get-tuple-element.120), channel_id=1, source_target_pairs={{0,112},{8,120},{64,48},{72,56},{1,113},{9,121},{65,49},{73,57},{2... | collective-permute-start | bytes 589832 | tf_op jit(solution)/shard_map/cond/branch_0_fun/ppermute | solution.py:277
  4.9 3.4 %collective-permute-start.1 = (bf16[384,256]{1,0:T(8,128)(2,1)S(1)}, bf16[384,256]{1,0:T(8,128)(2,1)S(1)}, u32[]{:S(2)}, u32[]{:S(2)}) collective-permute-start(bf16[384,256]{1,0:T(8,128)(2,1)S(1)} %get-tuple-element.121), channel_id=1, source_target_pairs={{0,96},{8,104},{64,32},{72,40},{1,97},{9,105},{65,33},{73,41},{2,9... | collective-permute-start | bytes 589832 | tf_op jit(solution)/shard_map/cond/branch_0_fun/ppermute | solution.py:277
  5.6 3.4 %collective-permute-start.2 = (bf16[384,256]{1,0:T(8,128)(2,1)S(1)}, bf16[384,256]{1,0:T(8,128)(2,1)S(1)}, u32[]{:S(2)}, u32[]{:S(2)}) collective-permute-start(bf16[384,256]{1,0:T(8,128)(2,1)S(1)} %get-tuple-element.122), channel_id=1, source_target_pairs={{0,80},{8,88},{64,16},{72,24},{1,81},{9,89},{65,17},{73,25},{2,82}... | collective-permute-start | bytes 589832 | tf_op jit(solution)/shard_map/cond/branch_0_fun/ppermute | solution.py:277
  6.2 2.8 %collective-permute-start.3 = (bf16[384,256]{1,0:T(8,128)(2,1)S(1)}, bf16[384,256]{1,0:T(8,128)(2,1)S(1)}, u32[]{:S(2)}, u32[]{:S(2)}) collective-permute-start(bf16[384,256]{1,0:T(8,128)(2,1)S(1)} %get-tuple-element.123), channel_id=1, source_target_pairs={{0,64},{8,72},{64,0},{72,8},{1,65},{9,73},{65,1},{73,9},{2,66},{10... | collective-permute-start | bytes 589832 | tf_op jit(solution)/shard_map/cond/branch_0_fun/ppermute | solution.py:277
  6.9 2.1 %collective-permute-start.4 = (bf16[384,256]{1,0:T(8,128)(2,1)S(1)}, bf16[384,256]{1,0:T(8,128)(2,1)S(1)}, u32[]{:S(2)}, u32[]{:S(2)}) collective-permute-start(bf16[384,256]{1,0:T(8,128)(2,1)S(1)} %get-tuple-element.124), channel_id=1, source_target_pairs={{0,48},{8,56},{64,112},{72,120},{1,49},{9,57},{65,113},{73,121},{2... | collective-permute-start | bytes 589832 | tf_op jit(solution)/shard_map/cond/branch_0_fun/ppermute | solution.py:277
  7.6 1.4 %collective-permute-start.5 = (bf16[384,256]{1,0:T(8,128)(2,1)S(1)}, bf16[384,256]{1,0:T(8,128)(2,1)S(1)}, u32[]{:S(2)}, u32[]{:S(2)}) collective-permute-start(bf16[384,256]{1,0:T(8,128)(2,1)S(1)} %get-tuple-element.125), channel_id=1, source_target_pairs={{0,32},{8,40},{64,96},{72,104},{1,33},{9,41},{65,97},{73,105},{2,3... | collective-permute-start | bytes 589832 | tf_op jit(solution)/shard_map/cond/branch_0_fun/ppermute | solution.py:277
  8.3 0.7 collective-permute-start.6
  9.2 11.6 %collective-permute-start.33 = (bf16[192,1024]{1,0:T(8,128)(2,1)S(1)}, bf16[192,1024]{1,0:T(8,128)(2,1)S(1)}, u32[]{:S(2)}, u32[]{:S(2)}) collective-permute-start(bf16[192,1024]{1,0:T(8,128)(2,1)S(1)} %bitcast.42), channel_id=1, source_target_pairs={{129,136},{131,138},{133,140},{135,142},{136,129},{138,131},{140,1... | collective-permute-start | bytes 1179656 | tf_op jit(solution)/shard_map/ppermute | solution.py:252
  13.5 28.9 %collective-permute-start.32 = (bf16[192,1024]{1,0:T(8,128)(2,1)S(1)}, bf16[192,1024]{1,0:T(8,128)(2,1)S(1)}, u32[]{:S(2)}, u32[]{:S(2)}) collective-permute-start(bf16[192,1024]{1,0:T(8,128)(2,1)S(1)} %bitcast.46), channel_id=1, source_target_pairs={{128,128},{129,136},{130,130},{131,138},{132,132},{133,140},{134,1... | collective-permute-start | bytes 1179656 | tf_op jit(solution)/shard_map/ppermute | solution.py:252
  16.3 26.1 %collective-permute-start.31 = (bf16[384,256]{1,0:T(8,128)(2,1)S(1)}, bf16[384,256]{1,0:T(8,128)(2,1)S(1)}, u32[]{:S(2)}, u32[]{:S(2)}) collective-permute-start(bf16[384,256]{1,0:T(8,128)(2,1)S(1)} %get-tuple-element.227), channel_id=1, source_target_pairs={{0,128},{1,136},{2,130},{3,138},{4,132},{5,140},{6,134},{7,142},{8... | collective-permute-start | bytes 589832 | tf_op jit(solution)/shard_map/ppermute | solution.py:252
  42.4 1.4 collective-permute-start.34
  65.2 7.2 %collective-permute-start.35 = (bf16[1536,256]{1,0:T(8,128)(2,1)S(1)}, bf16[1536,256]{1,0:T(8,128)(2,1)S(1)}, u32[]{:S(2)}, u32[]{:S(2)}) collective-permute-start(bf16[1536,256]{1,0:T(8,128)(2,1)S(1)} %all_gather.3.refs_0_), channel_id=1, source_target_pairs={{0,1},{1,0},{2,3},{3,2},{4,5},{5,4},{6,7},{7,6},{8,9},{9,8},{10,11... | collective-permute-start | bytes 2359304 | tf_op jit(solution)/shard_map/ppermute | solution.py:252
  70.5 33.2 %copy-start.1 = (bf16[1,2,256]{2,1,0:T(2,128)(2,1)S(1)}, bf16[1,2,256]{2,1,0:T(2,128)(2,1)}, u32[]{:S(2)}) copy-start(bf16[1,2,256]{2,1,0:T(2,128)(2,1)} %param.15) | copy-start | bytes 3076
  70.5 33.2 %copy-start.2 = (s32[32]{0:T(128)S(1)}, s32[32]{0:T(128)}, u32[]{:S(2)}) copy-start(s32[32]{0:T(128)} %lengths_ref.1) | copy-start | bytes 388
  70.5 33.2 %copy-start.5 = (bf16[1,2,1024]{2,1,0:T(2,128)(2,1)S(1)}, bf16[1,2,1024]{2,1,0:T(2,128)(2,1)}, u32[]{:S(2)}) copy-start(bf16[1,2,1024]{2,1,0:T(2,128)(2,1)} %param.16) | copy-start | bytes 12292
  92.7 2.4 %collective-permute-start.38 = (bf16[1536,256]{1,0:T(8,128)(2,1)S(1)}, bf16[1536,256]{1,0:T(8,128)(2,1)S(1)}, u32[]{:S(2)}, u32[]{:S(2)}) collective-permute-start(bf16[1536,256]{1,0:T(8,128)(2,1)S(1)} %get-tuple-element.202), channel_id=1, source_target_pairs={{0,1},{1,0},{2,3},{3,2},{4,5},{5,4},{6,7},{7,6},{8,9},{9,8},{10,11... | collective-permute-start | bytes 2359304 | tf_op jit(solution)/shard_map/ppermute | solution.py:252
  96.1 31.2 %all-to-all-start = ((bf16[8,192,256]{2,1,0:T(8,128)(2,1)}), bf16[8,192,256]{2,1,0:T(8,128)(2,1)S(1)}, u32[]{:S(2)}, u32[]{:S(2)}) async-start(bf16[8,192,256]{2,1,0:T(8,128)(2,1)} %bitcast.18), calls=%async_computation | async-start | bytes 1572864 | tf_op jit(solution)/shard_map/all_to_all | solution.py:304
  103.8 1.6 %collective-permute-start.28 = (f32[2,2560]{1,0:T(2,128)S(1)}, f32[2,2560]{1,0:T(2,128)S(1)}, u32[]{:S(2)}, u32[]{:S(2)}) collective-permute-start(f32[2,2560]{1,0:T(2,128)S(1)} %get-tuple-element.228), channel_id=1, source_target_pairs={{0,1},{1,0},{2,3},{3,2},{4,5},{5,4},{6,7},{7,6},{8,9},{9,8},{10,11... | collective-permute-start | bytes 61448 | tf_op jit(solution)/shard_map/ppermute | solution.py:252
  105.4 0.7 collective-permute-start.29
  106.1 7.8 %collective-permute-start.30 = (f32[2,2560]{1,0:T(2,128)S(1)}, f32[2,2560]{1,0:T(2,128)S(1)}, u32[]{:S(2)}, u32[]{:S(2)}) collective-permute-start(f32[2,2560]{1,0:T(2,128)S(1)} %add.31), channel_id=1, source_target_pairs={{0,4},{1,5},{2,6},{3,7},{4,0},{5,1},{6,2},{7,3},{8,12},{9,13},{10,... | collective-permute-start | bytes 61448 | tf_op jit(solution)/shard_map/ppermute | solution.py:252
  106.7 27.4 %collective-permute-start.36 = (bf16[192,1024]{1,0:T(8,128)(2,1)S(1)}, bf16[192,1024]{1,0:T(8,128)(2,1)S(1)}, u32[]{:S(2)}, u32[]{:S(2)}) collective-permute-start(bf16[192,1024]{1,0:T(8,128)(2,1)S(1)} %get-tuple-element.199), channel_id=1, source_target_pairs={{128,128},{129,136},{130,130},{131,138},{132,132},{133,140},{134,1... | collective-permute-start | bytes 1179656 | tf_op jit(solution)/shard_map/ppermute | solution.py:252
  108.7 24.7 %collective-permute-start.37 = (bf16[192,1024]{1,0:T(8,128)(2,1)S(1)}, bf16[192,1024]{1,0:T(8,128)(2,1)S(1)}, u32[]{:S(2)}, u32[]{:S(2)}) collective-permute-start(bf16[192,1024]{1,0:T(8,128)(2,1)S(1)} %get-tuple-element.200), channel_id=1, source_target_pairs={{129,136},{131,138},{133,140},{135,142},{136,129},{138,131},{140,1... | collective-permute-start | bytes 1179656 | tf_op jit(solution)/shard_map/ppermute | solution.py:252
  127.4 10.3 %collective-permute-start.39 = (bf16[192,256]{1,0:T(8,128)(2,1)S(1)}, bf16[192,256]{1,0:T(8,128)(2,1)S(1)}, u32[]{:S(2)}, u32[]{:S(2)}) collective-permute-start(bf16[192,256]{1,0:T(8,128)(2,1)S(1)} %reduce_sum.32), channel_id=1, source_target_pairs={{128,128},{129,136},{130,130},{131,138},{132,132},{133,140},{134,1... | collective-permute-start | bytes 294920 | tf_op jit(solution)/shard_map/ppermute | solution.py:252

commit v3 on v2

--- a/solution.py
+++ b/solution.py
@@ -16,7 +16,7 @@
 
 
 def attention_kernel(heads, blk, order_ref, meta_ref, *refs):
-    mine_ref, other_ref, q_ref, do_ref, o_ref, dq_ref, keep_ref, send_ref, kv_ref, kt_s, vt_s, s_s, p_s, dk_s, dv_s = refs
+    mine_ref, other_ref, q_ref, do_ref, out_ref, keep_ref, send_ref, kv_ref, kt_s, vt_s, s_s, p_s, dk_s, dv_s = refs
     total = kv_ref.shape[0]
     toks = q_ref.shape[0]
     gt, kc = TOKENS, KEYS
@@ -30,8 +30,7 @@
 
     @pl.when(learner == 0)
     def _():
-        o_ref[...] = jnp.zeros_like(o_ref)
-        dq_ref[...] = jnp.zeros_like(dq_ref)
+        out_ref[...] = jnp.zeros_like(out_ref)
         keep_ref[...] = jnp.zeros_like(keep_ref)
         send_ref[...] = jnp.zeros_like(send_ref)
 
@@ -53,9 +52,9 @@
         def stacked(ref, base):
             return jnp.concatenate([ref[pl.ds(base, gt), h * HEAD:(h + 1) * HEAD] for h in range(heads)], axis=0)
 
-        def spread(ref, base, value):
+        def spread(which, base, value):
             for h in range(heads):
-                ref[pl.ds(base, gt), h * HEAD:(h + 1) * HEAD] = value[h * gt:(h + 1) * gt]
+                out_ref[which, pl.ds(base, gt), h * HEAD:(h + 1) * HEAD] = value[h * gt:(h + 1) * gt]
 
         def group(g, _):
             base = pl.multiple_of(g * gt, gt)
@@ -99,7 +98,7 @@
             )
             inv = 1.0 / jnp.sum(l, axis=0, keepdims=True)
             ob = (acc * inv).astype(jnp.bfloat16)
-            spread(o_ref, base, ob.T)
+            spread(0, base, ob.T)
             dot_f = dot_t.astype(jnp.float32)
             delta = jnp.sum(dot_f * ob.astype(jnp.float32), axis=0, keepdims=True) * inv
             dots = (dot_f * inv).astype(jnp.bfloat16)
@@ -115,7 +114,7 @@
                 return acc + jnp.dot(kt_s[:, part], ds, preferred_element_type=jnp.float32)
 
             acc = lax.fori_loop(0, last, back, jnp.zeros((HEAD, rows), jnp.float32))
-            spread(dq_ref, base, (acc * scale).astype(jnp.bfloat16).T)
+            spread(1, base, (acc * scale).astype(jnp.bfloat16).T)
             return 0
 
         lax.fori_loop(0, toks // gt, group, 0)
@@ -143,13 +142,12 @@
     return pl.pallas_call(
         functools.partial(attention_kernel, heads, total // order.shape[0]),
         out_shape=(
-            jax.ShapeDtypeStruct(q.shape, jnp.bfloat16),
-            jax.ShapeDtypeStruct(q.shape, jnp.bfloat16),
+            jax.ShapeDtypeStruct((2,) + q.shape, jnp.bfloat16),
             jax.ShapeDtypeStruct((total // 2, 2 * HEAD), jnp.float32),
             jax.ShapeDtypeStruct((total // 2, 2 * HEAD), jnp.bfloat16),
         ),
         in_specs=[smem, smem] + [vmem] * 4,
-        out_specs=(vmem, vmem, vmem, vmem),
+        out_specs=(vmem, vmem, vmem),
         scratch_shapes=[
             pltpu.VMEM((total, 2 * HEAD), jnp.bfloat16),
             pltpu.VMEM((HEAD, total), jnp.bfloat16),
@@ -269,12 +267,10 @@
         def scatter(parts):
             got = parts[0]
             for step in range(1, ring):
-                route = [
-                    (z * 2 + column, (z + step) % ring * 2 + column)
-                    for z in range(first, ring, classes)
-                    for column in range(2)
+                pairs = [
+                    (z * 2 + h, (z + step) % ring * 2 + h) for z in range(first, ring, classes) for h in range(2)
                 ]
-                arrived = lax.ppermute(parts[step], ("grp", "ctx"), route)
+                arrived = lax.ppermute(parts[step], ("grp", "ctx"), pairs)
                 got = jnp.where(distance == step, arrived, got)
             return got
 
@@ -299,13 +295,15 @@
     other = sent(mine, cores)
 
     meta = jnp.stack([z_index * 2 + core, grp_index, core]).astype(jnp.int32)
-    attn_rows, grad_rows, kept, passed = attention(order, meta, mine, other, query_rows, gradient_rows)
+    result_rows, kept, passed = attention(order, meta, mine, other, query_rows, gradient_rows)
     summed = (kept + sent(passed, cores).astype(jnp.float32)).astype(jnp.bfloat16)
     spread = lax.all_to_all(
         summed.reshape(ring, total // ctx_size, width), "ctx", 0, 0, axis_index_groups=columns
     )
-    attn_out = sent(attn_rows, swap_all)
-    grad_query = jnp.where(stays, grad_rows, sent(grad_rows, swap))
+    returned = sent(result_rows, swap)
+    attn_out = jnp.where(stays, result_rows[0], returned[0])
+    grad_query = jnp.where(stays, result_rows[1], returned[1])
+    spread, attn_out, grad_query = lax.optimization_barrier((spread, attn_out, grad_query))
     grads = jnp.sum(spread.astype(jnp.float32), axis=0).astype(jnp.bfloat16)
     grad_pairs = sent(grads, swap_all)
 
@@ -318,8 +316,16 @@
         (cached, new_kv[0], held_query, row_lengths, out_weight[0]),
     )
     partial_out = partial_out + sent(partial_out, cores)
-    partial_out = partial_out + sent(partial_out, route((0,), lambda g, z, h, y, c: (g, z, h, y ^ 1, c)))
-    partial_out = partial_out + sent(partial_out, route((0,), lambda g, z, h, y, c: (g, z, h, y ^ 2, c)))
+    count = tp_size // 2
+    onward = route((0,), lambda g, z, h, y, c: (g, z, h, (y + 1) % count, c))
+    terms = [partial_out]
+    for _ in range(count - 1):
+        terms.append(sent(terms[-1], onward))
+    y_index = lax.axis_index("tp") >> 1
+    partial_out = jnp.zeros_like(partial_out)
+    for y in range(count):
+        back = (y_index - y) & (count - 1)
+        partial_out = partial_out + sum(jnp.where(back == step, terms[step], 0.0) for step in range(count))
     decoded = partial_out.astype(jnp.bfloat16)
     return (decoded[None], attn_out[None], grad_query[None], grad_pairs[None])
 

time: 137 us -> 134 us (0.978); the launches traced: 139 us -> 134 us
  waiting for transfers between devices: 43.6 us -> 50.2 us
  starting transfers between devices: 41.3 us -> 35.2 us
  Pallas kernels: 23.1 us -> 18.4 us
    ppermute x12, waiting for transfers between devices: 30.7 us -> 42.7 us  [sent(): return lax.ppermute(x, ('grp', 'ctx', 'tp'), pairs)]
    ppermute x12, starting transfers between devices: 28.9 us -> 22.7 us  [sent(): return lax.ppermute(x, ('grp', 'ctx', 'tp'), pairs)]
    all_to_all x1, waiting for transfers between devices: 12.8 us -> 7.52 us  [shards(): lax.all_to_all(summed.reshape(ring, total // ctx_size, width), 'ctx', 0,...]
    pallas_call x1, Pallas kernels: 20.3 us -> 15.6 us  [attention(): pl.pallas_call(functools.partial(attention_kernel, heads, total // order....]
  transfers between devices with their start and end apart: 20 -> 20, of which waited for: 7 -> 8; matrix products, arithmetic and copies ran while one was open for 3% -> 4% of each run, Pallas kernels for 0% -> 0%
where the time goes in v3:
time: 134 us
  waiting for transfers between devices  50.2 us (37%)
  starting transfers between devices  35.2 us (26%)
  blocking collectives  21 us (16%)
  Pallas kernels  18.4 us (14%)
  other arithmetic  6.24 us (5%)
  between operations  2.21 us (2%)
    ppermute x12, waiting for transfers between devices, sent(): return lax.ppermute(x, ('grp', 'ctx', 'tp'), pairs)  42.7 us
    ppermute x12, starting transfers between devices, sent(): return lax.ppermute(x, ('grp', 'ctx', 'tp'), pairs)  22.7 us
    all_gather x1, blocking collectives, shards(): lax.all_gather(own, 'ctx', axis=0, tiled=True, axis_index_groups=columns)  21 us
    pallas_call x1, Pallas kernels, attention(): pl.pallas_call(functools.partial(attention_kernel, heads, total // order....  15.6 us
    all_to_all x1, starting transfers between devices, shards(): lax.all_to_all(summed.reshape(ring, total // ctx_size, width), 'ctx', 0,...  7.7 us
    all_to_all x1, waiting for transfers between devices, shards(): lax.all_to_all(summed.reshape(ring, total // ctx_size, width), 'ctx', 0,...  7.52 us
    ppermute x7, starting transfers between devices, scatter(): arrived = lax.ppermute(parts[step], ('grp', 'ctx'), pairs)  4.84 us
    sort x1, other arithmetic, shards(): jnp.argsort(block_plan, stable=True).astype(jnp.int32)  3.17 us
  transfers between devices with their start and end apart: 20, of which 8 were waited for; matrix products, arithmetic and copies ran while one was open for 4% of the time, Pallas kernels for 0%

profile of v3, /device:TPU:11, one launch (start us, length us, event | category | flops | bytes accessed | tf_op | source)
XLA Modules:
  0.0 134.1 jit_solution(6816737031279871458)
XLA Ops:
  0.6 2.8 %shard_map.112 = (s32[1]{0:T(128)}, bf16[384,256]{1,0:T(8,128)(2,1)S(1)}, bf16[384,256]{1,0:T(8,128)(2,1)S(1)}, bf16[384,256]{1,0:T(8,128)(2,1)S(1)}, bf16[384,2...) custom-call(s32[32]{0:T(128)} %lengths_ref.1, ...), custom_call_target="tpu_custom_call" | custom-call | tf_op jit(solution)/shard_map/pallas_call | solution.py:197
  4.1 5.1 %conditional.2 = (bf16[384,256]{1,0:T(8,128)(2,1)S(1)}) conditional(s32[]{:T(128)} %clamp.3, (s32[]{:T(128)}, bf16[384,256]{1,0:T(8,128)(2,1)S(1)}, bf16[384,256]{1,0:T(8,128)(2,1)S(1)}, bf16[384,256]{1,0:T(8,128)(2,1)S(1)}, bf16[384,256]{1,0:T(8,128)(2,1)S(1)}, /*index=5*/bf16[384,256]{1,0:T(8,128)(2,1)S(1)}, ...), branch_computations={%region_0.1_spmd, %region_1.2_spmd, %region_2.3_spmd, %region_3.4_... | conditional | flops 688135 | bytes 7274854 | solution.py:280
  4.1 0.8 collective-permute-start.14
  4.9 0.7 collective-permute-start.15
  5.6 0.7 collective-permute-start.16
  6.3 0.7 collective-permute-start.17
  7.0 0.7 collective-permute-start.18
  7.7 0.7 collective-permute-start.19
  8.4 0.7 collective-permute-start.20
  9.2 4.3 %collective-permute-start.34 = (bf16[192,1024]{1,0:T(8,128)(2,1)S(1)}, bf16[192,1024]{1,0:T(8,128)(2,1)S(1)}, u32[]{:S(2)}, u32[]{:S(2)}) collective-permute-start(bf16[192,1024]{1,0:T(8,128)(2,1)S(1)} %bitcast.46), channel_id=1, source_target_pairs={{129,136},{131,138},{133,140},{135,142},{136,129},{138,131},{140,1... | collective-permute-start | bytes 1179656 | tf_op jit(solution)/shard_map/ppermute | solution.py:250
  13.6 2.8 %collective-permute-start.33 = (bf16[192,1024]{1,0:T(8,128)(2,1)S(1)}, bf16[192,1024]{1,0:T(8,128)(2,1)S(1)}, u32[]{:S(2)}, u32[]{:S(2)}) collective-permute-start(bf16[192,1024]{1,0:T(8,128)(2,1)S(1)} %bitcast.50), channel_id=1, source_target_pairs={{128,128},{129,136},{130,130},{131,138},{132,132},{133,140},{134,1... | collective-permute-start | bytes 1179656 | tf_op jit(solution)/shard_map/ppermute | solution.py:250
  16.3 1.3 collective-permute-start.32
  17.6 3.2 %sort.17 = (s32[192]{0:T(256)}, s32[192]{0:T(256)S(1)}) sort(s32[192]{0:T(256)S(1)} %copy-done.3, s32[192]{0:T(256)S(1)} %iota.17), dimensions={0}, to_apply=%region_9.10 | sort | flops 1536 | bytes 3072 | tf_op jit(solution)/shard_map/jit(argsort)/sort | solution.py:288
  20.9 22.5 %collective-permute-done.32 = bf16[384,256]{1,0:T(8,128)(2,1)S(1)} collective-permute-done((bf16[384,256]{1,0:T(8,128)(2,1)S(1)}, bf16[384,256]{1,0:T(8,128)(2,1)S(1)}, u32[]{:S(2)}, u32[]{:S(2)}) %collective-permute-start.32) | collective-permute-done | bytes 196640 | tf_op jit(solution)/shard_map/ppermute | solution.py:250
  44.2 0.7 collective-permute-done.35
  44.8 21.0 %all_gather.3.refs_0_ = bf16[1536,256]{1,0:T(8,128)(2,1)S(1)} all-gather(bf16[192,256]{1,0:T(8,128)(2,1)S(1)} %select_select_fusion.4), channel_id=1, replica_groups={{0,16,32,48,64,80,96,112},{8,24,40,56,72,88,104,120},{1,17,33,49,65,81,..., dimensions={0}, use_global_device_ids=true | all-gather | bytes 884736 | tf_op jit(solution)/shard_map/all_gather | solution.py:294
  65.8 5.5 %collective-permute-start.36 = (bf16[1536,256]{1,0:T(8,128)(2,1)S(1)}, bf16[1536,256]{1,0:T(8,128)(2,1)S(1)}, u32[]{:S(2)}, u32[]{:S(2)}) collective-permute-start(bf16[1536,256]{1,0:T(8,128)(2,1)S(1)} %all_gather.3.refs_0_), channel_id=1, source_target_pairs={{0,1},{1,0},{2,3},{3,2},{4,5},{5,4},{6,7},{7,6},{8,9},{9,8},{10,11... | collective-permute-start | bytes 2359304 | tf_op jit(solution)/shard_map/ppermute | solution.py:250
  71.4 1.8 %collective-permute-done.36.refs_1_ = bf16[1536,256]{1,0:T(8,128)(2,1)S(1)} collective-permute-done((bf16[1536,256]{1,0:T(8,128)(2,1)S(1)}, bf16[1536,256]{1,0:T(8,128)(2,1)S(1)}, u32[]{:S(2)}, u32[]{:S(2)}) %collective-permute-start.36) | collective-permute-done | bytes 786464 | tf_op jit(solution)/shard_map/ppermute | solution.py:250
  73.2 15.6 %shard_map.113 = (bf16[2,192,1024]{2,1,0:T(8,128)(2,1)S(1)}, f32[1536,256]{1,0:T(8,128)S(1)}, bf16[1536,256]{1,0:T(8,128)(2,1)S(1)}) custom-call(s32[192]{0:T(256)S(1)} %get-tuple-element.197.order_ref, s32[3]{0:T(128)S(1)} %pad_add_fusion.meta_ref, bf16[1536,256]{1,0:T(8,128)(2,1)S(1)} %all_gather.3.refs_0_, ...), custom_call_target="tpu_custom_call" | custom-call | tf_op jit(solution)/shard_map/pallas_call | solution.py:142
  88.8 2.8 %collective-permute-start.37 = (bf16[1536,256]{1,0:T(8,128)(2,1)S(1)}, bf16[1536,256]{1,0:T(8,128)(2,1)S(1)}, u32[]{:S(2)}, u32[]{:S(2)}) collective-permute-start(bf16[1536,256]{1,0:T(8,128)(2,1)S(1)} %get-tuple-element.202), channel_id=1, source_target_pairs={{0,1},{1,0},{2,3},{3,2},{4,5},{5,4},{6,7},{7,6},{8,9},{9,8},{10,11... | collective-permute-start | bytes 2359304 | tf_op jit(solution)/shard_map/ppermute | solution.py:250
  91.6 1.9 %collective-permute-done.37 = bf16[1536,256]{1,0:T(8,128)(2,1)S(1)} collective-permute-done((bf16[1536,256]{1,0:T(8,128)(2,1)S(1)}, bf16[1536,256]{1,0:T(8,128)(2,1)S(1)}, u32[]{:S(2)}, u32[]{:S(2)}) %collective-permute-start.37) | collective-permute-done | bytes 786464 | tf_op jit(solution)/shard_map/ppermute | solution.py:250
  93.6 1.1 add_convert_fusion
  94.6 7.7 %all-to-all-start = ((bf16[8,192,256]{2,1,0:T(8,128)(2,1)}), bf16[8,192,256]{2,1,0:T(8,128)(2,1)S(1)}, u32[]{:S(2)}, u32[]{:S(2)}) async-start(bf16[8,192,256]{2,1,0:T(8,128)(2,1)} %bitcast.16), calls=%async_computation | async-start | bytes 1572864 | tf_op jit(solution)/shard_map/all_to_all | solution.py:300
  102.3 1.9 %collective-permute-start.38 = (bf16[2,192,1024]{2,1,0:T(8,128)(2,1)S(1)}, bf16[2,192,1024]{2,1,0:T(8,128)(2,1)S(1)}, u32[]{:S(2)}, u32[]{:S(2)}) collective-permute-start(bf16[2,192,1024]{2,1,0:T(8,128)(2,1)S(1)} %get-tuple-element.203), channel_id=1, source_target_pairs={{129,136},{131,138},{133,140},{135,142},{136,129},{138,131},{140,1... | collective-permute-start | bytes 2359304 | tf_op jit(solution)/shard_map/ppermute | solution.py:250
  104.4 1.2 collective-permute-done.28
  105.6 0.7 collective-permute-start.29
  107.7 9.7 %collective-permute-done.38 = bf16[2,192,1024]{2,1,0:T(8,128)(2,1)S(1)} collective-permute-done((bf16[2,192,1024]{2,1,0:T(8,128)(2,1)S(1)}, bf16[2,192,1024]{2,1,0:T(8,128)(2,1)S(1)}, u32[]{:S(2)}, u32[]{:S(2)}) %collective-permute-start.38) | collective-permute-done | bytes 786464 | tf_op jit(solution)/shard_map/ppermute | solution.py:250
  117.4 1.0 fusion.36
  118.4 7.5 %all-to-all-done = bf16[8,192,256]{2,1,0:T(8,128)(2,1)S(1)} async-done(((bf16[8,192,256]{2,1,0:T(8,128)(2,1)}), bf16[8,192,256]{2,1,0:T(8,128)(2,1)S(1)}, u32[]{:S(2)}, u32[]{:S(2)}) %all-to-all-start) | async-done | bytes 786464 | tf_op jit(solution)/shard_map/all_to_all | solution.py:300
  126.0 1.9 %collective-permute-start.39 = (bf16[192,256]{1,0:T(8,128)(2,1)S(1)}, bf16[192,256]{1,0:T(8,128)(2,1)S(1)}, u32[]{:S(2)}, u32[]{:S(2)}) collective-permute-start(bf16[192,256]{1,0:T(8,128)(2,1)S(1)} %reduce_sum.32), channel_id=1, source_target_pairs={{128,128},{129,136},{130,130},{131,138},{132,132},{133,140},{134,1... | collective-permute-start | bytes 294920 | tf_op jit(solution)/shard_map/ppermute | solution.py:250
  127.9 0.7 fusion.38
  128.6 4.8 %collective-permute-done.39 = bf16[192,256]{1,0:T(8,128)(2,1)S(1)} collective-permute-done((bf16[192,256]{1,0:T(8,128)(2,1)S(1)}, bf16[192,256]{1,0:T(8,128)(2,1)S(1)}, u32[]{:S(2)}, u32[]{:S(2)}) %collective-permute-start.39) | collective-permute-done | bytes 98336 | tf_op jit(solution)/shard_map/ppermute | solution.py:250
  (39 shorter events, 2.6 us)
Async XLA Ops:
  4.1 5.1 %copy-start = (bf16[1,192,1024]{2,1,0:T(8,128)(2,1)S(1)}, bf16[1,192,1024]{2,1,0:T(8,128)(2,1)}, u32[]{:S(2)}) copy-start(bf16[1,192,1024]{2,1,0:T(8,128)(2,1)} %param.21) | copy-start | bytes 1179652
  4.1 9.5 %copy-start.4 = (bf16[1,192,1024]{2,1,0:T(8,128)(2,1)S(1)}, bf16[1,192,1024]{2,1,0:T(8,128)(2,1)}, u32[]{:S(2)}) copy-start(bf16[1,192,1024]{2,1,0:T(8,128)(2,1)} %param.20) | copy-start | bytes 1179652
  4.1 13.5 %copy-start.3 = (s32[192]{0:T(256)S(1)}, s32[192]{0:T(256)}, u32[]{:S(2)}) copy-start(s32[192]{0:T(256)} %param.19) | copy-start | bytes 2308
  4.1 3.5 %collective-permute-start.14 = (bf16[384,256]{1,0:T(8,128)(2,1)S(1)}, bf16[384,256]{1,0:T(8,128)(2,1)S(1)}, u32[]{:S(2)}, u32[]{:S(2)}) collective-permute-start(bf16[384,256]{1,0:T(8,128)(2,1)S(1)} %get-tuple-element.138), channel_id=1, source_target_pairs={{32,16},{40,24},{96,80},{104,88},{33,17},{41,25},{97,81},{105,89},... | collective-permute-start | bytes 589832 | tf_op jit(solution)/shard_map/cond/branch_2_fun/ppermute | solution.py:273
  4.9 3.4 %collective-permute-start.15 = (bf16[384,256]{1,0:T(8,128)(2,1)S(1)}, bf16[384,256]{1,0:T(8,128)(2,1)S(1)}, u32[]{:S(2)}, u32[]{:S(2)}) collective-permute-start(bf16[384,256]{1,0:T(8,128)(2,1)S(1)} %get-tuple-element.139), channel_id=1, source_target_pairs={{32,0},{40,8},{96,64},{104,72},{33,1},{41,9},{97,65},{105,73},{34,... | collective-permute-start | bytes 589832 | tf_op jit(solution)/shard_map/cond/branch_2_fun/ppermute | solution.py:273
  5.6 3.4 %collective-permute-start.16 = (bf16[384,256]{1,0:T(8,128)(2,1)S(1)}, bf16[384,256]{1,0:T(8,128)(2,1)S(1)}, u32[]{:S(2)}, u32[]{:S(2)}) collective-permute-start(bf16[384,256]{1,0:T(8,128)(2,1)S(1)} %get-tuple-element.140), channel_id=1, source_target_pairs={{32,112},{40,120},{96,48},{104,56},{33,113},{41,121},{97,49},{105,... | collective-permute-start | bytes 589832 | tf_op jit(solution)/shard_map/cond/branch_2_fun/ppermute | solution.py:273
  6.3 2.8 %collective-permute-start.17 = (bf16[384,256]{1,0:T(8,128)(2,1)S(1)}, bf16[384,256]{1,0:T(8,128)(2,1)S(1)}, u32[]{:S(2)}, u32[]{:S(2)}) collective-permute-start(bf16[384,256]{1,0:T(8,128)(2,1)S(1)} %get-tuple-element.141), channel_id=1, source_target_pairs={{32,96},{40,104},{96,32},{104,40},{33,97},{41,105},{97,33},{105,41... | collective-permute-start | bytes 589832 | tf_op jit(solution)/shard_map/cond/branch_2_fun/ppermute | solution.py:273
  7.0 2.1 %collective-permute-start.18 = (bf16[384,256]{1,0:T(8,128)(2,1)S(1)}, bf16[384,256]{1,0:T(8,128)(2,1)S(1)}, u32[]{:S(2)}, u32[]{:S(2)}) collective-permute-start(bf16[384,256]{1,0:T(8,128)(2,1)S(1)} %get-tuple-element.142), channel_id=1, source_target_pairs={{32,80},{40,88},{96,16},{104,24},{33,81},{41,89},{97,17},{105,25},... | collective-permute-start | bytes 589832 | tf_op jit(solution)/shard_map/cond/branch_2_fun/ppermute | solution.py:273
  7.7 1.4 %collective-permute-start.19 = (bf16[384,256]{1,0:T(8,128)(2,1)S(1)}, bf16[384,256]{1,0:T(8,128)(2,1)S(1)}, u32[]{:S(2)}, u32[]{:S(2)}) collective-permute-start(bf16[384,256]{1,0:T(8,128)(2,1)S(1)} %get-tuple-element.143), channel_id=1, source_target_pairs={{32,64},{40,72},{96,0},{104,8},{33,65},{41,73},{97,1},{105,9},{34,... | collective-permute-start | bytes 589832 | tf_op jit(solution)/shard_map/cond/branch_2_fun/ppermute | solution.py:273
  8.4 0.7 collective-permute-start.20
  9.2 11.6 %collective-permute-start.34 = (bf16[192,1024]{1,0:T(8,128)(2,1)S(1)}, bf16[192,1024]{1,0:T(8,128)(2,1)S(1)}, u32[]{:S(2)}, u32[]{:S(2)}) collective-permute-start(bf16[192,1024]{1,0:T(8,128)(2,1)S(1)} %bitcast.46), channel_id=1, source_target_pairs={{129,136},{131,138},{133,140},{135,142},{136,129},{138,131},{140,1... | collective-permute-start | bytes 1179656 | tf_op jit(solution)/shard_map/ppermute | solution.py:250
  13.6 29.9 %collective-permute-start.33 = (bf16[192,1024]{1,0:T(8,128)(2,1)S(1)}, bf16[192,1024]{1,0:T(8,128)(2,1)S(1)}, u32[]{:S(2)}, u32[]{:S(2)}) collective-permute-start(bf16[192,1024]{1,0:T(8,128)(2,1)S(1)} %bitcast.50), channel_id=1, source_target_pairs={{128,128},{129,136},{130,130},{131,138},{132,132},{133,140},{134,1... | collective-permute-start | bytes 1179656 | tf_op jit(solution)/shard_map/ppermute | solution.py:250
  16.3 27.1 %collective-permute-start.32 = (bf16[384,256]{1,0:T(8,128)(2,1)S(1)}, bf16[384,256]{1,0:T(8,128)(2,1)S(1)}, u32[]{:S(2)}, u32[]{:S(2)}) collective-permute-start(bf16[384,256]{1,0:T(8,128)(2,1)S(1)} %get-tuple-element.233), channel_id=1, source_target_pairs={{0,128},{1,136},{2,130},{3,138},{4,132},{5,140},{6,134},{7,142},{8... | collective-permute-start | bytes 589832 | tf_op jit(solution)/shard_map/ppermute | solution.py:250
  43.4 1.4 %collective-permute-start.35 = (bf16[192,256]{1,0:T(8,128)(2,1)S(1)}, bf16[192,256]{1,0:T(8,128)(2,1)S(1)}, u32[]{:S(2)}, u32[]{:S(2)}) collective-permute-start(bf16[192,256]{1,0:T(8,128)(2,1)S(1)} %broadcast_select_fusion.1), channel_id=1, source_target_pairs={{0,1},{1,0},{2,3},{3,2},{4,5},{5,4},{6,7},{7,6},{8,9},{9,8},{10,11... | collective-permute-start | bytes 294920 | tf_op jit(solution)/shard_map/ppermute | solution.py:250
  65.8 7.4 %collective-permute-start.36 = (bf16[1536,256]{1,0:T(8,128)(2,1)S(1)}, bf16[1536,256]{1,0:T(8,128)(2,1)S(1)}, u32[]{:S(2)}, u32[]{:S(2)}) collective-permute-start(bf16[1536,256]{1,0:T(8,128)(2,1)S(1)} %all_gather.3.refs_0_), channel_id=1, source_target_pairs={{0,1},{1,0},{2,3},{3,2},{4,5},{5,4},{6,7},{7,6},{8,9},{9,8},{10,11... | collective-permute-start | bytes 2359304 | tf_op jit(solution)/shard_map/ppermute | solution.py:250
  71.4 32.9 %copy-start.1 = (bf16[1,2,256]{2,1,0:T(2,128)(2,1)S(1)}, bf16[1,2,256]{2,1,0:T(2,128)(2,1)}, u32[]{:S(2)}) copy-start(bf16[1,2,256]{2,1,0:T(2,128)(2,1)} %param.15) | copy-start | bytes 3076
  71.4 32.9 %copy-start.2 = (s32[32]{0:T(128)S(1)}, s32[32]{0:T(128)}, u32[]{:S(2)}) copy-start(s32[32]{0:T(128)} %lengths_ref.1) | copy-start | bytes 388
  71.4 32.9 %copy-start.5 = (bf16[1,2,1024]{2,1,0:T(2,128)(2,1)S(1)}, bf16[1,2,1024]{2,1,0:T(2,128)(2,1)}, u32[]{:S(2)}) copy-start(bf16[1,2,1024]{2,1,0:T(2,128)(2,1)} %param.16) | copy-start | bytes 12292
  88.8 4.7 %collective-permute-start.37 = (bf16[1536,256]{1,0:T(8,128)(2,1)S(1)}, bf16[1536,256]{1,0:T(8,128)(2,1)S(1)}, u32[]{:S(2)}, u32[]{:S(2)}) collective-permute-start(bf16[1536,256]{1,0:T(8,128)(2,1)S(1)} %get-tuple-element.202), channel_id=1, source_target_pairs={{0,1},{1,0},{2,3},{3,2},{4,5},{5,4},{6,7},{7,6},{8,9},{9,8},{10,11... | collective-permute-start | bytes 2359304 | tf_op jit(solution)/shard_map/ppermute | solution.py:250
  94.6 31.3 %all-to-all-start = ((bf16[8,192,256]{2,1,0:T(8,128)(2,1)}), bf16[8,192,256]{2,1,0:T(8,128)(2,1)S(1)}, u32[]{:S(2)}, u32[]{:S(2)}) async-start(bf16[8,192,256]{2,1,0:T(8,128)(2,1)} %bitcast.16), calls=%async_computation | async-start | bytes 1572864 | tf_op jit(solution)/shard_map/all_to_all | solution.py:300
  102.3 15.1 %collective-permute-start.38 = (bf16[2,192,1024]{2,1,0:T(8,128)(2,1)S(1)}, bf16[2,192,1024]{2,1,0:T(8,128)(2,1)S(1)}, u32[]{:S(2)}, u32[]{:S(2)}) collective-permute-start(bf16[2,192,1024]{2,1,0:T(8,128)(2,1)S(1)} %get-tuple-element.203), channel_id=1, source_target_pairs={{129,136},{131,138},{133,140},{135,142},{136,129},{138,131},{140,1... | collective-permute-start | bytes 2359304 | tf_op jit(solution)/shard_map/ppermute | solution.py:250
  104.3 1.3 collective-permute-start.28
  105.6 0.7 collective-permute-start.29
  106.3 0.7 collective-permute-start.30
  107.0 20.9 %collective-permute-start.31 = (f32[2,2560]{1,0:T(2,128)S(1)}, f32[2,2560]{1,0:T(2,128)S(1)}, u32[]{:S(2)}, u32[]{:S(2)}) collective-permute-start(f32[2,2560]{1,0:T(2,128)S(1)} %collective-permute-done.30), channel_id=1, source_target_pairs={{0,2},{1,3},{2,4},{3,5},{4,6},{5,7},{6,0},{7,1},{8,10},{9,11},{10,... | collective-permute-start | bytes 61448 | tf_op jit(solution)/shard_map/ppermute | solution.py:250
  126.0 7.4 %collective-permute-start.39 = (bf16[192,256]{1,0:T(8,128)(2,1)S(1)}, bf16[192,256]{1,0:T(8,128)(2,1)S(1)}, u32[]{:S(2)}, u32[]{:S(2)}) collective-permute-start(bf16[192,256]{1,0:T(8,128)(2,1)S(1)} %reduce_sum.32), channel_id=1, source_target_pairs={{128,128},{129,136},{130,130},{131,138},{132,132},{133,140},{134,1... | collective-permute-start | bytes 294920 | tf_op jit(solution)/shard_map/ppermute | solution.py:250

commit v4 on v3

--- a/solution.py
+++ b/solution.py
@@ -16,7 +16,7 @@
 
 
 def attention_kernel(heads, blk, order_ref, meta_ref, *refs):
-    mine_ref, other_ref, q_ref, do_ref, out_ref, keep_ref, send_ref, kv_ref, kt_s, vt_s, s_s, p_s, dk_s, dv_s = refs
+    mine_ref, other_ref, q_ref, do_ref, out_ref, keep_ref, send_ref, kv_ref, kt_s, vt_s, s_s, p_s, dk_s, dv_s, dq_s, o_s = refs
     total = kv_ref.shape[0]
     toks = q_ref.shape[0]
     gt, kc = TOKENS, KEYS
@@ -84,18 +84,18 @@
             m = jnp.max(m, axis=0, keepdims=True)
 
             def weigh(c, carry):
-                l, acc = carry
+                l = carry
                 part = pl.ds(pl.multiple_of(c * kc, kc), kc)
                 p = jnp.exp2((s_s[part, :] - m) * factor)
                 l = l + jnp.sum(p.reshape(kc // 8, 8, rows), axis=0)
                 pb = p.astype(jnp.bfloat16)
                 p_s[part, :] = pb
-                acc = acc + jnp.dot(vt_s[:, part], pb, preferred_element_type=jnp.float32)
-                return l, acc
-
-            l, acc = lax.fori_loop(
-                0, last, weigh, (jnp.zeros((8, rows), jnp.float32), jnp.zeros((HEAD, rows), jnp.float32))
-            )
+                o_s[...] += jnp.dot(vt_s[:, part], pb, preferred_element_type=jnp.float32)
+                return l
+
+            o_s[...] = jnp.zeros_like(o_s)
+            l = lax.fori_loop(0, last, weigh, jnp.zeros((8, rows), jnp.float32))
+            acc = o_s[...]
             inv = 1.0 / jnp.sum(l, axis=0, keepdims=True)
             ob = (acc * inv).astype(jnp.bfloat16)
             spread(0, base, ob.T)
@@ -111,9 +111,12 @@
                 ds = (pb.astype(jnp.float32) * (dp - delta)).astype(jnp.bfloat16)
                 dv_s[part, :] += jnp.dot(pb, dos, preferred_element_type=jnp.float32)
                 dk_s[part, :] += jnp.dot(ds, q, preferred_element_type=jnp.float32)
-                return acc + jnp.dot(kt_s[:, part], ds, preferred_element_type=jnp.float32)
-
-            acc = lax.fori_loop(0, last, back, jnp.zeros((HEAD, rows), jnp.float32))
+                dq_s[...] += jnp.dot(kt_s[:, part], ds, preferred_element_type=jnp.float32)
+                return acc
+
+            dq_s[...] = jnp.zeros_like(dq_s)
+            lax.fori_loop(0, last, back, 0)
+            acc = dq_s[...]
             spread(1, base, (acc * scale).astype(jnp.bfloat16).T)
             return 0
 
@@ -156,6 +159,8 @@
             pltpu.VMEM((total, rows), jnp.bfloat16),
             pltpu.VMEM((total, HEAD), jnp.float32),
             pltpu.VMEM((total, HEAD), jnp.float32),
+            pltpu.VMEM((HEAD, rows), jnp.float32),
+            pltpu.VMEM((HEAD, rows), jnp.float32),
         ],
         compiler_params=pltpu.CompilerParams(vmem_limit_bytes=48 * 2**20),
     )(order, meta, mine, other, q, do)
@@ -266,7 +271,7 @@
     def scatter_from(first):
         def scatter(parts):
             got = parts[0]
-            for step in range(1, ring):
+            for step in sorted(range(1, ring), key=lambda step: (-abs(step - ring // 2), -step)):
                 pairs = [
                     (z * 2 + h, (z + step) % ring * 2 + h) for z in range(first, ring, classes) for h in range(2)
                 ]

time: 134 us -> 129 us (0.963)
  waiting for transfers between devices: 50.2 us -> 44.9 us
  starting transfers between devices: 35.2 us -> 33.2 us
  Pallas kernels: 18.4 us -> 20.1 us
    ppermute x12, waiting for transfers between devices: 42.7 us -> 37.3 us  [sent(): return lax.ppermute(x, ('grp', 'ctx', 'tp'), pairs)]
    ppermute x12, starting transfers between devices: 22.7 us -> 19.8 us  [sent(): return lax.ppermute(x, ('grp', 'ctx', 'tp'), pairs)]
    pallas_call x1, Pallas kernels: 15.6 us -> 17.3 us  [attention(): pl.pallas_call(functools.partial(attention_kernel, heads, total // order....]
where the time goes in v4:
time: 129 us
  waiting for transfers between devices  44.9 us (35%)
  starting transfers between devices  33.2 us (26%)
  blocking collectives  21.9 us (17%)
  Pallas kernels  20.1 us (16%)
  other arithmetic  6.26 us (5%)
  between operations  2.21 us (2%)
    ppermute x12, waiting for transfers between devices, sent(): return lax.ppermute(x, ('grp', 'ctx', 'tp'), pairs)  37.3 us
    all_gather x1, blocking collectives, shards(): lax.all_gather(own, 'ctx', axis=0, tiled=True, axis_index_groups=columns)  21.9 us
    ppermute x12, starting transfers between devices, sent(): return lax.ppermute(x, ('grp', 'ctx', 'tp'), pairs)  19.8 us
    pallas_call x1, Pallas kernels, attention(): pl.pallas_call(functools.partial(attention_kernel, heads, total // order....  17.3 us
    all_to_all x1, starting transfers between devices, shards(): lax.all_to_all(summed.reshape(ring, total // ctx_size, width), 'ctx', 0,...  8.52 us
    all_to_all x1, waiting for transfers between devices, shards(): lax.all_to_all(summed.reshape(ring, total // ctx_size, width), 'ctx', 0,...  7.58 us
    ppermute x7, starting transfers between devices, scatter(): arrived = lax.ppermute(parts[step], ('grp', 'ctx'), pairs)  4.84 us
    sort x1, other arithmetic, shards(): jnp.argsort(block_plan, stable=True).astype(jnp.int32)  3.17 us
  transfers between devices with their start and end apart: 20, of which 8 were waited for; matrix products, arithmetic and copies ran while one was open for 4% of the time, Pallas kernels for 0%

profile of v4, /device:TPU:11, one launch (start us, length us, event | category | flops | bytes accessed | tf_op | source)
XLA Modules:
  0.0 129.3 jit_solution(14777905382870436689)
XLA Ops:
  0.6 2.8 %shard_map.112 = (s32[1]{0:T(128)}, bf16[384,256]{1,0:T(8,128)(2,1)S(1)}, bf16[384,256]{1,0:T(8,128)(2,1)S(1)}, bf16[384,256]{1,0:T(8,128)(2,1)S(1)}, bf16[384,2...) custom-call(s32[32]{0:T(128)} %lengths_ref.1, ...), custom_call_target="tpu_custom_call" | custom-call | tf_op jit(solution)/shard_map/pallas_call | solution.py:202
  4.1 5.1 %conditional.2 = (bf16[384,256]{1,0:T(8,128)(2,1)S(1)}) conditional(s32[]{:T(128)} %clamp.3, (s32[]{:T(128)}, bf16[384,256]{1,0:T(8,128)(2,1)S(1)}, bf16[384,256]{1,0:T(8,128)(2,1)S(1)}, bf16[384,256]{1,0:T(8,128)(2,1)S(1)}, bf16[384,256]{1,0:T(8,128)(2,1)S(1)}, /*index=5*/bf16[384,256]{1,0:T(8,128)(2,1)S(1)}, ...), branch_computations={%region_0.1_spmd, %region_1.2_spmd, %region_2.3_spmd, %region_3.4_... | conditional | flops 688135 | bytes 7274854 | solution.py:285
  4.1 0.8 collective-permute-start
  4.9 0.7 collective-permute-start.1
  5.6 0.7 collective-permute-start.2
  6.3 0.7 collective-permute-start.3
  7.0 0.7 collective-permute-start.4
  7.7 0.7 collective-permute-start.5
  8.4 0.7 collective-permute-start.6
  9.2 4.3 %collective-permute-start.34 = (bf16[192,1024]{1,0:T(8,128)(2,1)S(1)}, bf16[192,1024]{1,0:T(8,128)(2,1)S(1)}, u32[]{:S(2)}, u32[]{:S(2)}) collective-permute-start(bf16[192,1024]{1,0:T(8,128)(2,1)S(1)} %bitcast.46), channel_id=1, source_target_pairs={{129,136},{131,138},{133,140},{135,142},{136,129},{138,131},{140,1... | collective-permute-start | bytes 1179656 | tf_op jit(solution)/shard_map/ppermute | solution.py:255
  13.6 2.8 %collective-permute-start.33 = (bf16[192,1024]{1,0:T(8,128)(2,1)S(1)}, bf16[192,1024]{1,0:T(8,128)(2,1)S(1)}, u32[]{:S(2)}, u32[]{:S(2)}) collective-permute-start(bf16[192,1024]{1,0:T(8,128)(2,1)S(1)} %bitcast.50), channel_id=1, source_target_pairs={{128,128},{129,136},{130,130},{131,138},{132,132},{133,140},{134,1... | collective-permute-start | bytes 1179656 | tf_op jit(solution)/shard_map/ppermute | solution.py:255
  16.3 1.3 collective-permute-start.32
  17.7 3.2 %sort.17 = (s32[192]{0:T(256)}, s32[192]{0:T(256)S(1)}) sort(s32[192]{0:T(256)S(1)} %copy-done.3, s32[192]{0:T(256)S(1)} %iota.17), dimensions={0}, to_apply=%region_9.10 | sort | flops 1536 | bytes 3072 | tf_op jit(solution)/shard_map/jit(argsort)/sort | solution.py:293
  20.9 17.2 %collective-permute-done.32 = bf16[384,256]{1,0:T(8,128)(2,1)S(1)} collective-permute-done((bf16[384,256]{1,0:T(8,128)(2,1)S(1)}, bf16[384,256]{1,0:T(8,128)(2,1)S(1)}, u32[]{:S(2)}, u32[]{:S(2)}) %collective-permute-start.32) | collective-permute-done | bytes 196640 | tf_op jit(solution)/shard_map/ppermute | solution.py:255
  38.8 0.7 collective-permute-done.35
  39.5 21.9 %all_gather.3.refs_0_ = bf16[1536,256]{1,0:T(8,128)(2,1)S(1)} all-gather(bf16[192,256]{1,0:T(8,128)(2,1)S(1)} %select_select_fusion.4), channel_id=1, replica_groups={{0,16,32,48,64,80,96,112},{8,24,40,56,72,88,104,120},{1,17,33,49,65,81,..., dimensions={0}, use_global_device_ids=true | all-gather | bytes 884736 | tf_op jit(solution)/shard_map/all_gather | solution.py:299
  61.4 5.0 %collective-permute-start.36 = (bf16[1536,256]{1,0:T(8,128)(2,1)S(1)}, bf16[1536,256]{1,0:T(8,128)(2,1)S(1)}, u32[]{:S(2)}, u32[]{:S(2)}) collective-permute-start(bf16[1536,256]{1,0:T(8,128)(2,1)S(1)} %all_gather.3.refs_0_), channel_id=1, source_target_pairs={{0,1},{1,0},{2,3},{3,2},{4,5},{5,4},{6,7},{7,6},{8,9},{9,8},{10,11... | collective-permute-start | bytes 2359304 | tf_op jit(solution)/shard_map/ppermute | solution.py:255
  66.4 1.8 %collective-permute-done.36.refs_1_ = bf16[1536,256]{1,0:T(8,128)(2,1)S(1)} collective-permute-done((bf16[1536,256]{1,0:T(8,128)(2,1)S(1)}, bf16[1536,256]{1,0:T(8,128)(2,1)S(1)}, u32[]{:S(2)}, u32[]{:S(2)}) %collective-permute-start.36) | collective-permute-done | bytes 786464 | tf_op jit(solution)/shard_map/ppermute | solution.py:255
  68.3 17.3 %shard_map.113 = (bf16[2,192,1024]{2,1,0:T(8,128)(2,1)S(1)}, f32[1536,256]{1,0:T(8,128)S(1)}, bf16[1536,256]{1,0:T(8,128)(2,1)S(1)}) custom-call(s32[192]{0:T(256)S(1)} %get-tuple-element.197.order_ref, s32[3]{0:T(128)S(1)} %pad_add_fusion.meta_ref, bf16[1536,256]{1,0:T(8,128)(2,1)S(1)} %all_gather.3.refs_0_, ...), custom_call_target="tpu_custom_call" | custom-call | tf_op jit(solution)/shard_map/pallas_call | solution.py:145
  86.0 1.9 %collective-permute-done.37 = bf16[1536,256]{1,0:T(8,128)(2,1)S(1)} collective-permute-done((bf16[1536,256]{1,0:T(8,128)(2,1)S(1)}, bf16[1536,256]{1,0:T(8,128)(2,1)S(1)}, u32[]{:S(2)}, u32[]{:S(2)}) %collective-permute-start.37) | collective-permute-done | bytes 786464 | tf_op jit(solution)/shard_map/ppermute | solution.py:255
  87.9 1.1 add_convert_fusion
  89.0 8.5 %all-to-all-start = ((bf16[8,192,256]{2,1,0:T(8,128)(2,1)}), bf16[8,192,256]{2,1,0:T(8,128)(2,1)S(1)}, u32[]{:S(2)}, u32[]{:S(2)}) async-start(bf16[8,192,256]{2,1,0:T(8,128)(2,1)} %bitcast.16), calls=%async_computation | async-start | bytes 1572864 | tf_op jit(solution)/shard_map/all_to_all | solution.py:305
  97.5 1.9 %collective-permute-start.38 = (bf16[2,192,1024]{2,1,0:T(8,128)(2,1)S(1)}, bf16[2,192,1024]{2,1,0:T(8,128)(2,1)S(1)}, u32[]{:S(2)}, u32[]{:S(2)}) collective-permute-start(bf16[2,192,1024]{2,1,0:T(8,128)(2,1)S(1)} %get-tuple-element.203), channel_id=1, source_target_pairs={{129,136},{131,138},{133,140},{135,142},{136,129},{138,131},{140,1... | collective-permute-start | bytes 2359304 | tf_op jit(solution)/shard_map/ppermute | solution.py:255
  99.6 1.2 collective-permute-done.28
  100.8 0.7 collective-permute-start.29
  101.5 0.7 collective-permute-start.30
  102.9 9.7 %collective-permute-done.38 = bf16[2,192,1024]{2,1,0:T(8,128)(2,1)S(1)} collective-permute-done((bf16[2,192,1024]{2,1,0:T(8,128)(2,1)S(1)}, bf16[2,192,1024]{2,1,0:T(8,128)(2,1)S(1)}, u32[]{:S(2)}, u32[]{:S(2)}) %collective-permute-start.38) | collective-permute-done | bytes 786464 | tf_op jit(solution)/shard_map/ppermute | solution.py:255
  112.6 1.0 fusion.36
  113.6 7.6 %all-to-all-done = bf16[8,192,256]{2,1,0:T(8,128)(2,1)S(1)} async-done(((bf16[8,192,256]{2,1,0:T(8,128)(2,1)}), bf16[8,192,256]{2,1,0:T(8,128)(2,1)S(1)}, u32[]{:S(2)}, u32[]{:S(2)}) %all-to-all-start) | async-done | bytes 786464 | tf_op jit(solution)/shard_map/all_to_all | solution.py:305
  121.3 1.9 %collective-permute-start.39 = (bf16[192,256]{1,0:T(8,128)(2,1)S(1)}, bf16[192,256]{1,0:T(8,128)(2,1)S(1)}, u32[]{:S(2)}, u32[]{:S(2)}) collective-permute-start(bf16[192,256]{1,0:T(8,128)(2,1)S(1)} %reduce_sum.32), channel_id=1, source_target_pairs={{128,128},{129,136},{130,130},{131,138},{132,132},{133,140},{134,1... | collective-permute-start | bytes 294920 | tf_op jit(solution)/shard_map/ppermute | solution.py:255
  123.2 0.7 fusion.38
  123.9 4.8 %collective-permute-done.39 = bf16[192,256]{1,0:T(8,128)(2,1)S(1)} collective-permute-done((bf16[192,256]{1,0:T(8,128)(2,1)S(1)}, bf16[192,256]{1,0:T(8,128)(2,1)S(1)}, u32[]{:S(2)}, u32[]{:S(2)}) %collective-permute-start.39) | collective-permute-done | bytes 98336 | tf_op jit(solution)/shard_map/ppermute | solution.py:255
  (39 shorter events, 2.4 us)
Async XLA Ops:
  4.1 5.2 %copy-start = (bf16[1,192,1024]{2,1,0:T(8,128)(2,1)S(1)}, bf16[1,192,1024]{2,1,0:T(8,128)(2,1)}, u32[]{:S(2)}) copy-start(bf16[1,192,1024]{2,1,0:T(8,128)(2,1)} %param.21) | copy-start | bytes 1179652
  4.1 9.5 %copy-start.4 = (bf16[1,192,1024]{2,1,0:T(8,128)(2,1)S(1)}, bf16[1,192,1024]{2,1,0:T(8,128)(2,1)}, u32[]{:S(2)}) copy-start(bf16[1,192,1024]{2,1,0:T(8,128)(2,1)} %param.20) | copy-start | bytes 1179652
  4.1 13.6 %copy-start.3 = (s32[192]{0:T(256)S(1)}, s32[192]{0:T(256)}, u32[]{:S(2)}) copy-start(s32[192]{0:T(256)} %param.19) | copy-start | bytes 2308
  4.1 3.5 %collective-permute-start = (bf16[384,256]{1,0:T(8,128)(2,1)S(1)}, bf16[384,256]{1,0:T(8,128)(2,1)S(1)}, u32[]{:S(2)}, u32[]{:S(2)}) collective-permute-start(bf16[384,256]{1,0:T(8,128)(2,1)S(1)} %get-tuple-element.120), channel_id=1, source_target_pairs={{0,64},{8,72},{64,0},{72,8},{1,65},{9,73},{65,1},{73,9},{2,66},{10... | collective-permute-start | bytes 589832 | tf_op jit(solution)/shard_map/cond/branch_0_fun/ppermute | solution.py:278
  4.9 3.4 %collective-permute-start.1 = (bf16[384,256]{1,0:T(8,128)(2,1)S(1)}, bf16[384,256]{1,0:T(8,128)(2,1)S(1)}, u32[]{:S(2)}, u32[]{:S(2)}) collective-permute-start(bf16[384,256]{1,0:T(8,128)(2,1)S(1)} %get-tuple-element.121), channel_id=1, source_target_pairs={{0,48},{8,56},{64,112},{72,120},{1,49},{9,57},{65,113},{73,121},{2... | collective-permute-start | bytes 589832 | tf_op jit(solution)/shard_map/cond/branch_0_fun/ppermute | solution.py:278
  5.6 3.4 %collective-permute-start.2 = (bf16[384,256]{1,0:T(8,128)(2,1)S(1)}, bf16[384,256]{1,0:T(8,128)(2,1)S(1)}, u32[]{:S(2)}, u32[]{:S(2)}) collective-permute-start(bf16[384,256]{1,0:T(8,128)(2,1)S(1)} %get-tuple-element.122), channel_id=1, source_target_pairs={{0,80},{8,88},{64,16},{72,24},{1,81},{9,89},{65,17},{73,25},{2,82}... | collective-permute-start | bytes 589832 | tf_op jit(solution)/shard_map/cond/branch_0_fun/ppermute | solution.py:278
  6.3 2.8 %collective-permute-start.3 = (bf16[384,256]{1,0:T(8,128)(2,1)S(1)}, bf16[384,256]{1,0:T(8,128)(2,1)S(1)}, u32[]{:S(2)}, u32[]{:S(2)}) collective-permute-start(bf16[384,256]{1,0:T(8,128)(2,1)S(1)} %get-tuple-element.123), channel_id=1, source_target_pairs={{0,32},{8,40},{64,96},{72,104},{1,33},{9,41},{65,97},{73,105},{2,3... | collective-permute-start | bytes 589832 | tf_op jit(solution)/shard_map/cond/branch_0_fun/ppermute | solution.py:278
  7.0 2.1 %collective-permute-start.4 = (bf16[384,256]{1,0:T(8,128)(2,1)S(1)}, bf16[384,256]{1,0:T(8,128)(2,1)S(1)}, u32[]{:S(2)}, u32[]{:S(2)}) collective-permute-start(bf16[384,256]{1,0:T(8,128)(2,1)S(1)} %get-tuple-element.124), channel_id=1, source_target_pairs={{0,96},{8,104},{64,32},{72,40},{1,97},{9,105},{65,33},{73,41},{2,9... | collective-permute-start | bytes 589832 | tf_op jit(solution)/shard_map/cond/branch_0_fun/ppermute | solution.py:278
  7.7 1.4 %collective-permute-start.5 = (bf16[384,256]{1,0:T(8,128)(2,1)S(1)}, bf16[384,256]{1,0:T(8,128)(2,1)S(1)}, u32[]{:S(2)}, u32[]{:S(2)}) collective-permute-start(bf16[384,256]{1,0:T(8,128)(2,1)S(1)} %get-tuple-element.125), channel_id=1, source_target_pairs={{0,16},{8,24},{64,80},{72,88},{1,17},{9,25},{65,81},{73,89},{2,18}... | collective-permute-start | bytes 589832 | tf_op jit(solution)/shard_map/cond/branch_0_fun/ppermute | solution.py:278
  8.4 0.7 collective-permute-start.6
  9.2 11.6 %collective-permute-start.34 = (bf16[192,1024]{1,0:T(8,128)(2,1)S(1)}, bf16[192,1024]{1,0:T(8,128)(2,1)S(1)}, u32[]{:S(2)}, u32[]{:S(2)}) collective-permute-start(bf16[192,1024]{1,0:T(8,128)(2,1)S(1)} %bitcast.46), channel_id=1, source_target_pairs={{129,136},{131,138},{133,140},{135,142},{136,129},{138,131},{140,1... | collective-permute-start | bytes 1179656 | tf_op jit(solution)/shard_map/ppermute | solution.py:255
  13.6 24.5 %collective-permute-start.33 = (bf16[192,1024]{1,0:T(8,128)(2,1)S(1)}, bf16[192,1024]{1,0:T(8,128)(2,1)S(1)}, u32[]{:S(2)}, u32[]{:S(2)}) collective-permute-start(bf16[192,1024]{1,0:T(8,128)(2,1)S(1)} %bitcast.50), channel_id=1, source_target_pairs={{128,128},{129,136},{130,130},{131,138},{132,132},{133,140},{134,1... | collective-permute-start | bytes 1179656 | tf_op jit(solution)/shard_map/ppermute | solution.py:255
  16.3 21.8 %collective-permute-start.32 = (bf16[384,256]{1,0:T(8,128)(2,1)S(1)}, bf16[384,256]{1,0:T(8,128)(2,1)S(1)}, u32[]{:S(2)}, u32[]{:S(2)}) collective-permute-start(bf16[384,256]{1,0:T(8,128)(2,1)S(1)} %get-tuple-element.233), channel_id=1, source_target_pairs={{0,128},{1,136},{2,130},{3,138},{4,132},{5,140},{6,134},{7,142},{8... | collective-permute-start | bytes 589832 | tf_op jit(solution)/shard_map/ppermute | solution.py:255
  38.1 1.4 %collective-permute-start.35 = (bf16[192,256]{1,0:T(8,128)(2,1)S(1)}, bf16[192,256]{1,0:T(8,128)(2,1)S(1)}, u32[]{:S(2)}, u32[]{:S(2)}) collective-permute-start(bf16[192,256]{1,0:T(8,128)(2,1)S(1)} %broadcast_select_fusion.1), channel_id=1, source_target_pairs={{0,1},{1,0},{2,3},{3,2},{4,5},{5,4},{6,7},{7,6},{8,9},{9,8},{10,11... | collective-permute-start | bytes 294920 | tf_op jit(solution)/shard_map/ppermute | solution.py:255
  61.4 6.9 %collective-permute-start.36 = (bf16[1536,256]{1,0:T(8,128)(2,1)S(1)}, bf16[1536,256]{1,0:T(8,128)(2,1)S(1)}, u32[]{:S(2)}, u32[]{:S(2)}) collective-permute-start(bf16[1536,256]{1,0:T(8,128)(2,1)S(1)} %all_gather.3.refs_0_), channel_id=1, source_target_pairs={{0,1},{1,0},{2,3},{3,2},{4,5},{5,4},{6,7},{7,6},{8,9},{9,8},{10,11... | collective-permute-start | bytes 2359304 | tf_op jit(solution)/shard_map/ppermute | solution.py:255
  66.4 33.0 %copy-start.1 = (bf16[1,2,256]{2,1,0:T(2,128)(2,1)S(1)}, bf16[1,2,256]{2,1,0:T(2,128)(2,1)}, u32[]{:S(2)}) copy-start(bf16[1,2,256]{2,1,0:T(2,128)(2,1)} %param.15) | copy-start | bytes 3076
  66.4 33.0 %copy-start.2 = (s32[32]{0:T(128)S(1)}, s32[32]{0:T(128)}, u32[]{:S(2)}) copy-start(s32[32]{0:T(128)} %lengths_ref.1) | copy-start | bytes 388
  66.4 33.0 %copy-start.5 = (bf16[1,2,1024]{2,1,0:T(2,128)(2,1)S(1)}, bf16[1,2,1024]{2,1,0:T(2,128)(2,1)}, u32[]{:S(2)}) copy-start(bf16[1,2,1024]{2,1,0:T(2,128)(2,1)} %param.16) | copy-start | bytes 12292
  85.6 2.4 %collective-permute-start.37 = (bf16[1536,256]{1,0:T(8,128)(2,1)S(1)}, bf16[1536,256]{1,0:T(8,128)(2,1)S(1)}, u32[]{:S(2)}, u32[]{:S(2)}) collective-permute-start(bf16[1536,256]{1,0:T(8,128)(2,1)S(1)} %get-tuple-element.202), channel_id=1, source_target_pairs={{0,1},{1,0},{2,3},{3,2},{4,5},{5,4},{6,7},{7,6},{8,9},{9,8},{10,11... | collective-permute-start | bytes 2359304 | tf_op jit(solution)/shard_map/ppermute | solution.py:255
  89.0 32.1 %all-to-all-start = ((bf16[8,192,256]{2,1,0:T(8,128)(2,1)}), bf16[8,192,256]{2,1,0:T(8,128)(2,1)S(1)}, u32[]{:S(2)}, u32[]{:S(2)}) async-start(bf16[8,192,256]{2,1,0:T(8,128)(2,1)} %bitcast.16), calls=%async_computation | async-start | bytes 1572864 | tf_op jit(solution)/shard_map/all_to_all | solution.py:305
  97.5 15.1 %collective-permute-start.38 = (bf16[2,192,1024]{2,1,0:T(8,128)(2,1)S(1)}, bf16[2,192,1024]{2,1,0:T(8,128)(2,1)S(1)}, u32[]{:S(2)}, u32[]{:S(2)}) collective-permute-start(bf16[2,192,1024]{2,1,0:T(8,128)(2,1)S(1)} %get-tuple-element.203), channel_id=1, source_target_pairs={{129,136},{131,138},{133,140},{135,142},{136,129},{138,131},{140,1... | collective-permute-start | bytes 2359304 | tf_op jit(solution)/shard_map/ppermute | solution.py:255
  99.5 1.3 collective-permute-start.28
  100.8 0.7 collective-permute-start.29
  101.5 0.7 collective-permute-start.30
  102.2 21.0 %collective-permute-start.31 = (f32[2,2560]{1,0:T(2,128)S(1)}, f32[2,2560]{1,0:T(2,128)S(1)}, u32[]{:S(2)}, u32[]{:S(2)}) collective-permute-start(f32[2,2560]{1,0:T(2,128)S(1)} %collective-permute-done.30), channel_id=1, source_target_pairs={{0,2},{1,3},{2,4},{3,5},{4,6},{5,7},{6,0},{7,1},{8,10},{9,11},{10,... | collective-permute-start | bytes 61448 | tf_op jit(solution)/shard_map/ppermute | solution.py:255
  121.3 7.4 %collective-permute-start.39 = (bf16[192,256]{1,0:T(8,128)(2,1)S(1)}, bf16[192,256]{1,0:T(8,128)(2,1)S(1)}, u32[]{:S(2)}, u32[]{:S(2)}) collective-permute-start(bf16[192,256]{1,0:T(8,128)(2,1)S(1)} %reduce_sum.32), channel_id=1, source_target_pairs={{128,128},{129,136},{130,130},{131,138},{132,132},{133,140},{134,1... | collective-permute-start | bytes 294920 | tf_op jit(solution)/shard_map/ppermute | solution.py:255

commit v5 on v4

--- a/solution.py
+++ b/solution.py
@@ -37,9 +37,14 @@
     @pl.when(learner == 1)
     def _():
         half = toks
-        for r in range(total // half // 2):
+        ring = total // half // 2
+        z = lax.div(me, 2)
+        for r in range(ring):
+            run = lax.rem(z + ring + (r // 2 if r % 2 == 0 else -(r + 1) // 2), ring)
+            if r == ring - 1:
+                run = lax.rem(z + ring // 2, ring)
             for ref, which in ((mine_ref, core), (other_ref, 1 - core)):
-                start = pl.multiple_of((2 * r + which) * half, half)
+                start = pl.multiple_of((2 * run + which) * half, half)
                 kv_ref[pl.ds(start, half), :] = ref[r * half:(r + 1) * half, :]
 
         for c in range(total // 256):
@@ -296,7 +301,16 @@
     handed = sent(jnp.where(core == 0, high, low), cores)
     own = jnp.where(core == (owner & 1), jnp.where(core == 0, low, high), handed)
     columns = [list(range(h, ctx_size, 2)) for h in range(2)]
-    mine = lax.all_gather(own, "ctx", axis=0, tiled=True, axis_index_groups=columns)
+
+    def turned(x, step):
+        return lax.ppermute(x, "ctx", [(z * 2 + h, (z + step) % ring * 2 + h) for z in range(ring) for h in range(2)])
+
+    on, back, parts = own, own, [own]
+    for _ in range(ring // 2 - 1):
+        on, back = turned(on, 1), turned(back, -1)
+        parts += [on, back]
+    parts += [turned(on[:half // 2], 1), turned(back[half // 2:], -1)]
+    mine = jnp.concatenate(parts, axis=0)
     other = sent(mine, cores)
 
     meta = jnp.stack([z_index * 2 + core, grp_index, core]).astype(jnp.int32)

time: 129 us -> 126 us (0.977)
  blocking collectives: 21.9 us -> 0 us
  waiting for transfers between devices: 44.9 us -> 55.2 us
  starting transfers between devices: 33.2 us -> 42.4 us
    all_gather x1 -> x0, blocking collectives: 21.9 us -> none  [shards(): lax.all_gather(own, 'ctx', axis=0, tiled=True, axis_index_groups=columns)]
    ppermute x0 -> x8, starting transfers between devices: none -> 10.9 us  [turned(): lax.ppermute(x, 'ctx', [(z * 2 + h, (z + step) % ring * 2 + h) for z in r...]
    ppermute x0 -> x8, waiting for transfers between devices: none -> 10.3 us  [turned(): lax.ppermute(x, 'ctx', [(z * 2 + h, (z + step) % ring * 2 + h) for z in r...]
    all_to_all x1, starting transfers between devices: 8.52 us -> 4.67 us  [shards(): lax.all_to_all(summed.reshape(ring, total // ctx_size, width), 'ctx', 0,...]
    ppermute x12, starting transfers between devices: 19.8 us -> 21.9 us  [sent(): return lax.ppermute(x, ('grp', 'ctx', 'tp'), pairs)]
  transfers between devices with their start and end apart: 20 -> 28, of which waited for: 8 -> 12; matrix products, arithmetic and copies ran while one was open for 4% -> 4% of each run, Pallas kernels for 0% -> 0%
where the time goes in v5:
time: 126 us; the launch traced here: 127 us
  waiting for transfers between devices  55.2 us (44%)
  starting transfers between devices  42.4 us (34%)
  Pallas kernels  20.3 us (16%)
  other arithmetic  6.3 us (5%)
  between operations  2.13 us (2%)
    ppermute x12, waiting for transfers between devices, sent(): return lax.ppermute(x, ('grp', 'ctx', 'tp'), pairs)  37.4 us
    ppermute x12, starting transfers between devices, sent(): return lax.ppermute(x, ('grp', 'ctx', 'tp'), pairs)  21.9 us
    pallas_call x1, Pallas kernels, attention(): pl.pallas_call(functools.partial(attention_kernel, heads, total // order....  17.5 us
    ppermute x8, starting transfers between devices, turned(): lax.ppermute(x, 'ctx', [(z * 2 + h, (z + step) % ring * 2 + h) for z in r...  10.9 us
    ppermute x8, waiting for transfers between devices, turned(): lax.ppermute(x, 'ctx', [(z * 2 + h, (z + step) % ring * 2 + h) for z in r...  10.3 us
    all_to_all x1, waiting for transfers between devices, shards(): lax.all_to_all(summed.reshape(ring, total // ctx_size, width), 'ctx', 0,...  7.52 us
    ppermute x7, starting transfers between devices, scatter(): arrived = lax.ppermute(parts[step], ('grp', 'ctx'), pairs)  4.84 us
    all_to_all x1, starting transfers between devices, shards(): lax.all_to_all(summed.reshape(ring, total // ctx_size, width), 'ctx', 0,...  4.67 us
  transfers between devices with their start and end apart: 28, of which 12 were waited for; matrix products, arithmetic and copies ran while one was open for 4% of the time, Pallas kernels for 0%

profile of v5, /device:TPU:11, one launch (start us, length us, event | category | flops | bytes accessed | tf_op | source)
XLA Modules:
  0.0 127.2 jit_solution(12789541602065723317)
XLA Ops:
  0.6 2.8 %shard_map.112 = (s32[1]{0:T(128)}, bf16[384,256]{1,0:T(8,128)(2,1)S(1)}, bf16[384,256]{1,0:T(8,128)(2,1)S(1)}, bf16[384,256]{1,0:T(8,128)(2,1)S(1)}, bf16[384,2...) custom-call(s32[32]{0:T(128)} %lengths_ref.1, ...), custom_call_target="tpu_custom_call" | custom-call | tf_op jit(solution)/shard_map/pallas_call | solution.py:207
  4.0 5.1 %conditional.2 = (bf16[384,256]{1,0:T(8,128)(2,1)S(1)}) conditional(s32[]{:T(128)} %clamp.3, (s32[]{:T(128)}, bf16[384,256]{1,0:T(8,128)(2,1)S(1)}, bf16[384,256]{1,0:T(8,128)(2,1)S(1)}, bf16[384,256]{1,0:T(8,128)(2,1)S(1)}, bf16[384,256]{1,0:T(8,128)(2,1)S(1)}, /*index=5*/bf16[384,256]{1,0:T(8,128)(2,1)S(1)}, ...), branch_computations={%region_0.1_spmd, %region_1.2_spmd, %region_2.3_spmd, %region_3.4_... | conditional | flops 688135 | bytes 7274854 | solution.py:290
  4.0 0.8 collective-permute-start
  9.2 4.3 %collective-permute-start.34 = (bf16[192,1024]{1,0:T(8,128)(2,1)S(1)}, bf16[192,1024]{1,0:T(8,128)(2,1)S(1)}, u32[]{:S(2)}, u32[]{:S(2)}) collective-permute-start(bf16[192,1024]{1,0:T(8,128)(2,1)S(1)} %bitcast.46), channel_id=1, source_target_pairs={{129,136},{131,138},{133,140},{135,142},{136,129},{138,131},{140,1... | collective-permute-start | bytes 1179656 | tf_op jit(solution)/shard_map/ppermute | solution.py:260
  13.5 2.8 %collective-permute-start.33 = (bf16[192,1024]{1,0:T(8,128)(2,1)S(1)}, bf16[192,1024]{1,0:T(8,128)(2,1)S(1)}, u32[]{:S(2)}, u32[]{:S(2)}) collective-permute-start(bf16[192,1024]{1,0:T(8,128)(2,1)S(1)} %bitcast.50), channel_id=1, source_target_pairs={{128,128},{129,136},{130,130},{131,138},{132,132},{133,140},{134,1... | collective-permute-start | bytes 1179656 | tf_op jit(solution)/shard_map/ppermute | solution.py:260
  16.3 1.3 %collective-permute-start.32 = (bf16[384,256]{1,0:T(8,128)(2,1)S(1)}, bf16[384,256]{1,0:T(8,128)(2,1)S(1)}, u32[]{:S(2)}, u32[]{:S(2)}) collective-permute-start(bf16[384,256]{1,0:T(8,128)(2,1)S(1)} %get-tuple-element.235), channel_id=1, source_target_pairs={{0,128},{1,136},{2,130},{3,138},{4,132},{5,140},{6,134},{7,142},{8... | collective-permute-start | bytes 589832 | tf_op jit(solution)/shard_map/ppermute | solution.py:260
  17.6 3.2 %sort.17 = (s32[192]{0:T(256)}, s32[192]{0:T(256)S(1)}) sort(s32[192]{0:T(256)S(1)} %copy-done.3, s32[192]{0:T(256)S(1)} %iota.17), dimensions={0}, to_apply=%region_9.10 | sort | flops 1536 | bytes 3072 | tf_op jit(solution)/shard_map/jit(argsort)/sort | solution.py:298
  20.8 17.2 %collective-permute-done.32 = bf16[384,256]{1,0:T(8,128)(2,1)S(1)} collective-permute-done((bf16[384,256]{1,0:T(8,128)(2,1)S(1)}, bf16[384,256]{1,0:T(8,128)(2,1)S(1)}, u32[]{:S(2)}, u32[]{:S(2)}) %collective-permute-start.32) | collective-permute-done | bytes 196640 | tf_op jit(solution)/shard_map/ppermute | solution.py:260
  38.7 0.7 collective-permute-done.35
  39.5 2.3 %collective-permute-start.37 = (bf16[192,256]{1,0:T(8,128)(2,1)S(1)}, bf16[192,256]{1,0:T(8,128)(2,1)S(1)}, u32[]{:S(2)}, u32[]{:S(2)}) collective-permute-start(bf16[192,256]{1,0:T(8,128)(2,1)S(1)} %get-tuple-element.216), channel_id=1, source_target_pairs={{0,112},{8,120},{16,0},{24,8},{32,16},{40,24},{48,32},{56,40},{64,... | collective-permute-start | bytes 294920 | tf_op jit(solution)/shard_map/ppermute | solution.py:306
  41.8 2.9 %collective-permute-done.37 = bf16[192,256]{1,0:T(8,128)(2,1)S(1)} collective-permute-done((bf16[192,256]{1,0:T(8,128)(2,1)S(1)}, bf16[192,256]{1,0:T(8,128)(2,1)S(1)}, u32[]{:S(2)}, u32[]{:S(2)}) %collective-permute-start.37) | collective-permute-done | bytes 98336 | tf_op jit(solution)/shard_map/ppermute | solution.py:306
  44.8 2.4 %collective-permute-start.39 = (bf16[192,256]{1,0:T(8,128)(2,1)S(1)}, bf16[192,256]{1,0:T(8,128)(2,1)S(1)}, u32[]{:S(2)}, u32[]{:S(2)}) collective-permute-start(bf16[192,256]{1,0:T(8,128)(2,1)S(1)} %collective-permute-done.37), channel_id=1, source_target_pairs={{0,112},{8,120},{16,0},{24,8},{32,16},{40,24},{48,32},{56,40},{64,... | collective-permute-start | bytes 294920 | tf_op jit(solution)/shard_map/ppermute | solution.py:306
  47.2 1.6 %collective-permute-done.39 = bf16[192,256]{1,0:T(8,128)(2,1)S(1)} collective-permute-done((bf16[192,256]{1,0:T(8,128)(2,1)S(1)}, bf16[192,256]{1,0:T(8,128)(2,1)S(1)}, u32[]{:S(2)}, u32[]{:S(2)}) %collective-permute-start.39) | collective-permute-done | bytes 98336 | tf_op jit(solution)/shard_map/ppermute | solution.py:306
  48.8 3.0 %collective-permute-start.41 = (bf16[192,256]{1,0:T(8,128)(2,1)S(1)}, bf16[192,256]{1,0:T(8,128)(2,1)S(1)}, u32[]{:S(2)}, u32[]{:S(2)}) collective-permute-start(bf16[192,256]{1,0:T(8,128)(2,1)S(1)} %collective-permute-done.39), channel_id=1, source_target_pairs={{0,112},{8,120},{16,0},{24,8},{32,16},{40,24},{48,32},{56,40},{64,... | collective-permute-start | bytes 294920 | tf_op jit(solution)/shard_map/ppermute | solution.py:306
  51.9 1.6 %collective-permute-done.41 = bf16[192,256]{1,0:T(8,128)(2,1)S(1)} collective-permute-done((bf16[192,256]{1,0:T(8,128)(2,1)S(1)}, bf16[192,256]{1,0:T(8,128)(2,1)S(1)}, u32[]{:S(2)}, u32[]{:S(2)}) %collective-permute-start.41) | collective-permute-done | bytes 98336 | tf_op jit(solution)/shard_map/ppermute | solution.py:306
  53.5 3.0 %collective-permute-start.43 = (bf16[96,256]{1,0:T(8,128)(2,1)S(1)}, bf16[96,256]{1,0:T(8,128)(2,1)S(1)}, u32[]{:S(2)}, u32[]{:S(2)}) collective-permute-start(bf16[96,256]{1,0:T(8,128)(2,1)S(1)} %slice.49), channel_id=1, source_target_pairs={{0,112},{8,120},{16,0},{24,8},{32,16},{40,24},{48,32},{56,40},{64,... | collective-permute-start | bytes 147464 | tf_op jit(solution)/shard_map/ppermute | solution.py:306
  56.7 4.1 %collective-permute-done.42 = bf16[96,256]{1,0:T(8,128)(2,1)S(1)} collective-permute-done((bf16[96,256]{1,0:T(8,128)(2,1)S(1)}, bf16[96,256]{1,0:T(8,128)(2,1)S(1)}, u32[]{:S(2)}, u32[]{:S(2)}) %collective-permute-start.42) | collective-permute-done | bytes 49184 | tf_op jit(solution)/shard_map/ppermute | solution.py:306
  60.8 4.8 %collective-permute-start.44 = (bf16[1536,256]{1,0:T(8,128)(2,1)S(1)}, bf16[1536,256]{1,0:T(8,128)(2,1)S(1)}, u32[]{:S(2)}, u32[]{:S(2)}) collective-permute-start(bf16[1536,256]{1,0:T(8,128)(2,1)S(1)} %constant_dynamic-update-slice_fusion.refs_0_), channel_id=1, source_target_pairs={{0,1},{1,0},{2,3},{3,2},{4,5},{5,4},{6,7},{7,6},{8,9},{9,8},{10,11... | collective-permute-start | bytes 2359304 | tf_op jit(solution)/shard_map/ppermute | solution.py:260
  65.7 1.8 %collective-permute-done.44.refs_1_ = bf16[1536,256]{1,0:T(8,128)(2,1)S(1)} collective-permute-done((bf16[1536,256]{1,0:T(8,128)(2,1)S(1)}, bf16[1536,256]{1,0:T(8,128)(2,1)S(1)}, u32[]{:S(2)}, u32[]{:S(2)}) %collective-permute-start.44) | collective-permute-done | bytes 786464 | tf_op jit(solution)/shard_map/ppermute | solution.py:260
  67.5 17.5 %shard_map.113 = (bf16[2,192,1024]{2,1,0:T(8,128)(2,1)S(1)}, f32[1536,256]{1,0:T(8,128)S(1)}, bf16[1536,256]{1,0:T(8,128)(2,1)S(1)}) custom-call(s32[192]{0:T(256)S(1)} %get-tuple-element.197.order_ref, s32[3]{0:T(128)S(1)} %pad_add_fusion.meta_ref, bf16[1536,256]{1,0:T(8,128)(2,1)S(1)} %constant_dynamic-update-slice_fusion.refs_0_, ...), custom_call_target="tpu_custom_call" | custom-call | tf_op jit(solution)/shard_map/pallas_call | solution.py:150
  85.0 2.7 %collective-permute-start.45 = (bf16[1536,256]{1,0:T(8,128)(2,1)S(1)}, bf16[1536,256]{1,0:T(8,128)(2,1)S(1)}, u32[]{:S(2)}, u32[]{:S(2)}) collective-permute-start(bf16[1536,256]{1,0:T(8,128)(2,1)S(1)} %get-tuple-element.202), channel_id=1, source_target_pairs={{0,1},{1,0},{2,3},{3,2},{4,5},{5,4},{6,7},{7,6},{8,9},{9,8},{10,11... | collective-permute-start | bytes 2359304 | tf_op jit(solution)/shard_map/ppermute | solution.py:260
  87.7 1.9 %collective-permute-done.45 = bf16[1536,256]{1,0:T(8,128)(2,1)S(1)} collective-permute-done((bf16[1536,256]{1,0:T(8,128)(2,1)S(1)}, bf16[1536,256]{1,0:T(8,128)(2,1)S(1)}, u32[]{:S(2)}, u32[]{:S(2)}) %collective-permute-start.45) | collective-permute-done | bytes 786464 | tf_op jit(solution)/shard_map/ppermute | solution.py:260
  89.6 1.1 add_convert_fusion
  90.7 4.7 %all-to-all-start = ((bf16[8,192,256]{2,1,0:T(8,128)(2,1)}), bf16[8,192,256]{2,1,0:T(8,128)(2,1)S(1)}, u32[]{:S(2)}, u32[]{:S(2)}) async-start(bf16[8,192,256]{2,1,0:T(8,128)(2,1)} %bitcast.16), calls=%async_computation | async-start | bytes 1572864 | tf_op jit(solution)/shard_map/all_to_all | solution.py:319
  95.4 1.9 %collective-permute-start.46 = (bf16[2,192,1024]{2,1,0:T(8,128)(2,1)S(1)}, bf16[2,192,1024]{2,1,0:T(8,128)(2,1)S(1)}, u32[]{:S(2)}, u32[]{:S(2)}) collective-permute-start(bf16[2,192,1024]{2,1,0:T(8,128)(2,1)S(1)} %get-tuple-element.203), channel_id=1, source_target_pairs={{129,136},{131,138},{133,140},{135,142},{136,129},{138,131},{140,1... | collective-permute-start | bytes 2359304 | tf_op jit(solution)/shard_map/ppermute | solution.py:260
  97.5 1.2 collective-permute-done.28
  100.8 9.7 %collective-permute-done.46 = bf16[2,192,1024]{2,1,0:T(8,128)(2,1)S(1)} collective-permute-done((bf16[2,192,1024]{2,1,0:T(8,128)(2,1)S(1)}, bf16[2,192,1024]{2,1,0:T(8,128)(2,1)S(1)}, u32[]{:S(2)}, u32[]{:S(2)}) %collective-permute-start.46) | collective-permute-done | bytes 786464 | tf_op jit(solution)/shard_map/ppermute | solution.py:260
  110.5 1.0 fusion.36
  111.5 7.5 %all-to-all-done = bf16[8,192,256]{2,1,0:T(8,128)(2,1)S(1)} async-done(((bf16[8,192,256]{2,1,0:T(8,128)(2,1)}), bf16[8,192,256]{2,1,0:T(8,128)(2,1)S(1)}, u32[]{:S(2)}, u32[]{:S(2)}) %all-to-all-start) | async-done | bytes 786464 | tf_op jit(solution)/shard_map/all_to_all | solution.py:319
  119.1 1.9 %collective-permute-start.47 = (bf16[192,256]{1,0:T(8,128)(2,1)S(1)}, bf16[192,256]{1,0:T(8,128)(2,1)S(1)}, u32[]{:S(2)}, u32[]{:S(2)}) collective-permute-start(bf16[192,256]{1,0:T(8,128)(2,1)S(1)} %reduce_sum.32), channel_id=1, source_target_pairs={{128,128},{129,136},{130,130},{131,138},{132,132},{133,140},{134,1... | collective-permute-start | bytes 294920 | tf_op jit(solution)/shard_map/ppermute | solution.py:260
  121.0 0.7 fusion.38
  121.7 4.8 %collective-permute-done.47 = bf16[192,256]{1,0:T(8,128)(2,1)S(1)} collective-permute-done((bf16[192,256]{1,0:T(8,128)(2,1)S(1)}, bf16[192,256]{1,0:T(8,128)(2,1)S(1)}, u32[]{:S(2)}, u32[]{:S(2)}) %collective-permute-start.47) | collective-permute-done | bytes 98336 | tf_op jit(solution)/shard_map/ppermute | solution.py:260
  (64 shorter events, 7.6 us)
Async XLA Ops:
  4.0 13.6 %copy-start.3 = (s32[192]{0:T(256)S(1)}, s32[192]{0:T(256)}, u32[]{:S(2)}) copy-start(s32[192]{0:T(256)} %param.19) | copy-start | bytes 2308
  4.0 3.5 %collective-permute-start = (bf16[384,256]{1,0:T(8,128)(2,1)S(1)}, bf16[384,256]{1,0:T(8,128)(2,1)S(1)}, u32[]{:S(2)}, u32[]{:S(2)}) collective-permute-start(bf16[384,256]{1,0:T(8,128)(2,1)S(1)} %get-tuple-element.120), channel_id=1, source_target_pairs={{0,64},{8,72},{64,0},{72,8},{1,65},{9,73},{65,1},{73,9},{2,66},{10... | collective-permute-start | bytes 589832 | tf_op jit(solution)/shard_map/cond/branch_0_fun/ppermute | solution.py:283
  4.9 3.4 %collective-permute-start.1 = (bf16[384,256]{1,0:T(8,128)(2,1)S(1)}, bf16[384,256]{1,0:T(8,128)(2,1)S(1)}, u32[]{:S(2)}, u32[]{:S(2)}) collective-permute-start(bf16[384,256]{1,0:T(8,128)(2,1)S(1)} %get-tuple-element.121), channel_id=1, source_target_pairs={{0,48},{8,56},{64,112},{72,120},{1,49},{9,57},{65,113},{73,121},{2... | collective-permute-start | bytes 589832 | tf_op jit(solution)/shard_map/cond/branch_0_fun/ppermute | solution.py:283
  5.5 3.4 %collective-permute-start.2 = (bf16[384,256]{1,0:T(8,128)(2,1)S(1)}, bf16[384,256]{1,0:T(8,128)(2,1)S(1)}, u32[]{:S(2)}, u32[]{:S(2)}) collective-permute-start(bf16[384,256]{1,0:T(8,128)(2,1)S(1)} %get-tuple-element.122), channel_id=1, source_target_pairs={{0,80},{8,88},{64,16},{72,24},{1,81},{9,89},{65,17},{73,25},{2,82}... | collective-permute-start | bytes 589832 | tf_op jit(solution)/shard_map/cond/branch_0_fun/ppermute | solution.py:283
  6.2 2.8 %collective-permute-start.3 = (bf16[384,256]{1,0:T(8,128)(2,1)S(1)}, bf16[384,256]{1,0:T(8,128)(2,1)S(1)}, u32[]{:S(2)}, u32[]{:S(2)}) collective-permute-start(bf16[384,256]{1,0:T(8,128)(2,1)S(1)} %get-tuple-element.123), channel_id=1, source_target_pairs={{0,32},{8,40},{64,96},{72,104},{1,33},{9,41},{65,97},{73,105},{2,3... | collective-permute-start | bytes 589832 | tf_op jit(solution)/shard_map/cond/branch_0_fun/ppermute | solution.py:283
  6.9 2.1 %collective-permute-start.4 = (bf16[384,256]{1,0:T(8,128)(2,1)S(1)}, bf16[384,256]{1,0:T(8,128)(2,1)S(1)}, u32[]{:S(2)}, u32[]{:S(2)}) collective-permute-start(bf16[384,256]{1,0:T(8,128)(2,1)S(1)} %get-tuple-element.124), channel_id=1, source_target_pairs={{0,96},{8,104},{64,32},{72,40},{1,97},{9,105},{65,33},{73,41},{2,9... | collective-permute-start | bytes 589832 | tf_op jit(solution)/shard_map/cond/branch_0_fun/ppermute | solution.py:283
  7.6 1.4 %collective-permute-start.5 = (bf16[384,256]{1,0:T(8,128)(2,1)S(1)}, bf16[384,256]{1,0:T(8,128)(2,1)S(1)}, u32[]{:S(2)}, u32[]{:S(2)}) collective-permute-start(bf16[384,256]{1,0:T(8,128)(2,1)S(1)} %get-tuple-element.125), channel_id=1, source_target_pairs={{0,16},{8,24},{64,80},{72,88},{1,17},{9,25},{65,81},{73,89},{2,18}... | collective-permute-start | bytes 589832 | tf_op jit(solution)/shard_map/cond/branch_0_fun/ppermute | solution.py:283
  8.3 0.7 collective-permute-start.6
  9.2 11.6 %collective-permute-start.34 = (bf16[192,1024]{1,0:T(8,128)(2,1)S(1)}, bf16[192,1024]{1,0:T(8,128)(2,1)S(1)}, u32[]{:S(2)}, u32[]{:S(2)}) collective-permute-start(bf16[192,1024]{1,0:T(8,128)(2,1)S(1)} %bitcast.46), channel_id=1, source_target_pairs={{129,136},{131,138},{133,140},{135,142},{136,129},{138,131},{140,1... | collective-permute-start | bytes 1179656 | tf_op jit(solution)/shard_map/ppermute | solution.py:260
  13.5 24.5 %collective-permute-start.33 = (bf16[192,1024]{1,0:T(8,128)(2,1)S(1)}, bf16[192,1024]{1,0:T(8,128)(2,1)S(1)}, u32[]{:S(2)}, u32[]{:S(2)}) collective-permute-start(bf16[192,1024]{1,0:T(8,128)(2,1)S(1)} %bitcast.50), channel_id=1, source_target_pairs={{128,128},{129,136},{130,130},{131,138},{132,132},{133,140},{134,1... | collective-permute-start | bytes 1179656 | tf_op jit(solution)/shard_map/ppermute | solution.py:260
  16.3 21.8 %collective-permute-start.32 = (bf16[384,256]{1,0:T(8,128)(2,1)S(1)}, bf16[384,256]{1,0:T(8,128)(2,1)S(1)}, u32[]{:S(2)}, u32[]{:S(2)}) collective-permute-start(bf16[384,256]{1,0:T(8,128)(2,1)S(1)} %get-tuple-element.235), channel_id=1, source_target_pairs={{0,128},{1,136},{2,130},{3,138},{4,132},{5,140},{6,134},{7,142},{8... | collective-permute-start | bytes 589832 | tf_op jit(solution)/shard_map/ppermute | solution.py:260
  38.0 1.4 %collective-permute-start.35 = (bf16[192,256]{1,0:T(8,128)(2,1)S(1)}, bf16[192,256]{1,0:T(8,128)(2,1)S(1)}, u32[]{:S(2)}, u32[]{:S(2)}) collective-permute-start(bf16[192,256]{1,0:T(8,128)(2,1)S(1)} %broadcast_select_fusion.1), channel_id=1, source_target_pairs={{0,1},{1,0},{2,3},{3,2},{4,5},{5,4},{6,7},{7,6},{8,9},{9,8},{10,11... | collective-permute-start | bytes 294920 | tf_op jit(solution)/shard_map/ppermute | solution.py:260
  39.5 5.3 %collective-permute-start.37 = (bf16[192,256]{1,0:T(8,128)(2,1)S(1)}, bf16[192,256]{1,0:T(8,128)(2,1)S(1)}, u32[]{:S(2)}, u32[]{:S(2)}) collective-permute-start(bf16[192,256]{1,0:T(8,128)(2,1)S(1)} %get-tuple-element.216), channel_id=1, source_target_pairs={{0,112},{8,120},{16,0},{24,8},{32,16},{40,24},{48,32},{56,40},{64,... | collective-permute-start | bytes 294920 | tf_op jit(solution)/shard_map/ppermute | solution.py:306
  41.7 5.5 %collective-permute-start.36 = (bf16[192,256]{1,0:T(8,128)(2,1)S(1)}, bf16[192,256]{1,0:T(8,128)(2,1)S(1)}, u32[]{:S(2)}, u32[]{:S(2)}) collective-permute-start(bf16[192,256]{1,0:T(8,128)(2,1)S(1)} %get-tuple-element.216), channel_id=1, source_target_pairs={{0,16},{8,24},{16,32},{24,40},{32,48},{40,56},{48,64},{56,72},{64,... | collective-permute-start | bytes 294920 | tf_op jit(solution)/shard_map/ppermute | solution.py:306
  44.8 4.1 %collective-permute-start.39 = (bf16[192,256]{1,0:T(8,128)(2,1)S(1)}, bf16[192,256]{1,0:T(8,128)(2,1)S(1)}, u32[]{:S(2)}, u32[]{:S(2)}) collective-permute-start(bf16[192,256]{1,0:T(8,128)(2,1)S(1)} %collective-permute-done.37), channel_id=1, source_target_pairs={{0,112},{8,120},{16,0},{24,8},{32,16},{40,24},{48,32},{56,40},{64,... | collective-permute-start | bytes 294920 | tf_op jit(solution)/shard_map/ppermute | solution.py:306
  47.2 4.7 %collective-permute-start.38 = (bf16[192,256]{1,0:T(8,128)(2,1)S(1)}, bf16[192,256]{1,0:T(8,128)(2,1)S(1)}, u32[]{:S(2)}, u32[]{:S(2)}) collective-permute-start(bf16[192,256]{1,0:T(8,128)(2,1)S(1)} %collective-permute-done.36), channel_id=1, source_target_pairs={{0,16},{8,24},{16,32},{24,40},{32,48},{40,56},{48,64},{56,72},{64,... | collective-permute-start | bytes 294920 | tf_op jit(solution)/shard_map/ppermute | solution.py:306
  48.8 4.7 %collective-permute-start.41 = (bf16[192,256]{1,0:T(8,128)(2,1)S(1)}, bf16[192,256]{1,0:T(8,128)(2,1)S(1)}, u32[]{:S(2)}, u32[]{:S(2)}) collective-permute-start(bf16[192,256]{1,0:T(8,128)(2,1)S(1)} %collective-permute-done.39), channel_id=1, source_target_pairs={{0,112},{8,120},{16,0},{24,8},{32,16},{40,24},{48,32},{56,40},{64,... | collective-permute-start | bytes 294920 | tf_op jit(solution)/shard_map/ppermute | solution.py:306
  51.9 4.7 %collective-permute-start.40 = (bf16[192,256]{1,0:T(8,128)(2,1)S(1)}, bf16[192,256]{1,0:T(8,128)(2,1)S(1)}, u32[]{:S(2)}, u32[]{:S(2)}) collective-permute-start(bf16[192,256]{1,0:T(8,128)(2,1)S(1)} %collective-permute-done.38), channel_id=1, source_target_pairs={{0,16},{8,24},{16,32},{24,40},{32,48},{40,56},{48,64},{56,72},{64,... | collective-permute-start | bytes 294920 | tf_op jit(solution)/shard_map/ppermute | solution.py:306
  53.5 7.3 %collective-permute-start.43 = (bf16[96,256]{1,0:T(8,128)(2,1)S(1)}, bf16[96,256]{1,0:T(8,128)(2,1)S(1)}, u32[]{:S(2)}, u32[]{:S(2)}) collective-permute-start(bf16[96,256]{1,0:T(8,128)(2,1)S(1)} %slice.49), channel_id=1, source_target_pairs={{0,112},{8,120},{16,0},{24,8},{32,16},{40,24},{48,32},{56,40},{64,... | collective-permute-start | bytes 147464 | tf_op jit(solution)/shard_map/ppermute | solution.py:306
  56.6 4.2 %collective-permute-start.42 = (bf16[96,256]{1,0:T(8,128)(2,1)S(1)}, bf16[96,256]{1,0:T(8,128)(2,1)S(1)}, u32[]{:S(2)}, u32[]{:S(2)}) collective-permute-start(bf16[96,256]{1,0:T(8,128)(2,1)S(1)} %slice.48), channel_id=1, source_target_pairs={{0,16},{8,24},{16,32},{24,40},{32,48},{40,56},{48,64},{56,72},{64,... | collective-permute-start | bytes 147464 | tf_op jit(solution)/shard_map/ppermute | solution.py:306
  60.8 6.7 %collective-permute-start.44 = (bf16[1536,256]{1,0:T(8,128)(2,1)S(1)}, bf16[1536,256]{1,0:T(8,128)(2,1)S(1)}, u32[]{:S(2)}, u32[]{:S(2)}) collective-permute-start(bf16[1536,256]{1,0:T(8,128)(2,1)S(1)} %constant_dynamic-update-slice_fusion.refs_0_), channel_id=1, source_target_pairs={{0,1},{1,0},{2,3},{3,2},{4,5},{5,4},{6,7},{7,6},{8,9},{9,8},{10,11... | collective-permute-start | bytes 2359304 | tf_op jit(solution)/shard_map/ppermute | solution.py:260
  65.7 31.7 %copy-start.1 = (bf16[1,2,256]{2,1,0:T(2,128)(2,1)S(1)}, bf16[1,2,256]{2,1,0:T(2,128)(2,1)}, u32[]{:S(2)}) copy-start(bf16[1,2,256]{2,1,0:T(2,128)(2,1)} %param.15) | copy-start | bytes 3076
  65.7 31.7 %copy-start.2 = (s32[32]{0:T(128)S(1)}, s32[32]{0:T(128)}, u32[]{:S(2)}) copy-start(s32[32]{0:T(128)} %lengths_ref.1) | copy-start | bytes 388
  65.7 31.7 %copy-start.5 = (bf16[1,2,1024]{2,1,0:T(2,128)(2,1)S(1)}, bf16[1,2,1024]{2,1,0:T(2,128)(2,1)}, u32[]{:S(2)}) copy-start(bf16[1,2,1024]{2,1,0:T(2,128)(2,1)} %param.16) | copy-start | bytes 12292
  85.0 4.7 %collective-permute-start.45 = (bf16[1536,256]{1,0:T(8,128)(2,1)S(1)}, bf16[1536,256]{1,0:T(8,128)(2,1)S(1)}, u32[]{:S(2)}, u32[]{:S(2)}) collective-permute-start(bf16[1536,256]{1,0:T(8,128)(2,1)S(1)} %get-tuple-element.202), channel_id=1, source_target_pairs={{0,1},{1,0},{2,3},{3,2},{4,5},{5,4},{6,7},{7,6},{8,9},{9,8},{10,11... | collective-permute-start | bytes 2359304 | tf_op jit(solution)/shard_map/ppermute | solution.py:260
  90.7 28.2 %all-to-all-start = ((bf16[8,192,256]{2,1,0:T(8,128)(2,1)}), bf16[8,192,256]{2,1,0:T(8,128)(2,1)S(1)}, u32[]{:S(2)}, u32[]{:S(2)}) async-start(bf16[8,192,256]{2,1,0:T(8,128)(2,1)} %bitcast.16), calls=%async_computation | async-start | bytes 1572864 | tf_op jit(solution)/shard_map/all_to_all | solution.py:319
  95.4 15.1 %collective-permute-start.46 = (bf16[2,192,1024]{2,1,0:T(8,128)(2,1)S(1)}, bf16[2,192,1024]{2,1,0:T(8,128)(2,1)S(1)}, u32[]{:S(2)}, u32[]{:S(2)}) collective-permute-start(bf16[2,192,1024]{2,1,0:T(8,128)(2,1)S(1)} %get-tuple-element.203), channel_id=1, source_target_pairs={{129,136},{131,138},{133,140},{135,142},{136,129},{138,131},{140,1... | collective-permute-start | bytes 2359304 | tf_op jit(solution)/shard_map/ppermute | solution.py:260
  97.4 1.3 %collective-permute-start.28 = (f32[2,2560]{1,0:T(2,128)S(1)}, f32[2,2560]{1,0:T(2,128)S(1)}, u32[]{:S(2)}, u32[]{:S(2)}) collective-permute-start(f32[2,2560]{1,0:T(2,128)S(1)} %get-tuple-element.236), channel_id=1, source_target_pairs={{0,1},{1,0},{2,3},{3,2},{4,5},{5,4},{6,7},{7,6},{8,9},{9,8},{10,11... | collective-permute-start | bytes 61448 | tf_op jit(solution)/shard_map/ppermute | solution.py:260
  98.7 0.7 collective-permute-start.29
  99.4 0.7 collective-permute-start.30
  100.1 20.9 %collective-permute-start.31 = (f32[2,2560]{1,0:T(2,128)S(1)}, f32[2,2560]{1,0:T(2,128)S(1)}, u32[]{:S(2)}, u32[]{:S(2)}) collective-permute-start(f32[2,2560]{1,0:T(2,128)S(1)} %collective-permute-done.30), channel_id=1, source_target_pairs={{0,2},{1,3},{2,4},{3,5},{4,6},{5,7},{6,0},{7,1},{8,10},{9,11},{10,... | collective-permute-start | bytes 61448 | tf_op jit(solution)/shard_map/ppermute | solution.py:260
  119.1 7.4 %collective-permute-start.47 = (bf16[192,256]{1,0:T(8,128)(2,1)S(1)}, bf16[192,256]{1,0:T(8,128)(2,1)S(1)}, u32[]{:S(2)}, u32[]{:S(2)}) collective-permute-start(bf16[192,256]{1,0:T(8,128)(2,1)S(1)} %reduce_sum.32), channel_id=1, source_target_pairs={{128,128},{129,136},{130,130},{131,138},{132,132},{133,140},{134,1... | collective-permute-start | bytes 294920 | tf_op jit(solution)/shard_map/ppermute | solution.py:260
  (2 other events, 14.6 us)

commit v6 on v5

--- a/solution.py
+++ b/solution.py
@@ -61,8 +61,8 @@
             for h in range(heads):
                 out_ref[which, pl.ds(base, gt), h * HEAD:(h + 1) * HEAD] = value[h * gt:(h + 1) * gt]
 
-        def group(g, _):
-            base = pl.multiple_of(g * gt, gt)
+        def prepare(g):
+            base = g * gt
             firsts = [order_ref[me * (toks // blk) + g * sub + s] * blk for s in range(sub)]
             lane = lax.rem(lax.broadcasted_iota(jnp.int32, (1, rows), 1), gt)
             pos = firsts[0] + lane
@@ -71,61 +71,82 @@
             full = lax.div(firsts[0] + 1, kc)
             last = lax.div(firsts[-1] + blk + kc - 1, kc)
             q = stacked(q_ref, base)
-            qt = q.T
-            dot_t = stacked(do_ref, base).T
-
-            def scores(masked, c, m):
-                part = pl.ds(pl.multiple_of(c * kc, kc), kc)
-                s = jnp.dot(kv_ref[part, :HEAD], qt, preferred_element_type=jnp.float32)
-                if masked:
-                    kpos = c * kc + lax.broadcasted_iota(jnp.int32, (kc, rows), 0)
-                    s = jnp.where(kpos <= pos, s, neg_big)
-                s_s[part, :] = s
-                return jnp.maximum(m, jnp.max(s.reshape(kc // 8, 8, rows), axis=0))
-
-            m = jnp.full((8, rows), neg_big, jnp.float32)
-            m = lax.fori_loop(0, full, functools.partial(scores, False), m)
-            m = lax.fori_loop(full, last, functools.partial(scores, True), m)
-            m = jnp.max(m, axis=0, keepdims=True)
-
-            def weigh(c, carry):
-                l = carry
-                part = pl.ds(pl.multiple_of(c * kc, kc), kc)
-                p = jnp.exp2((s_s[part, :] - m) * factor)
-                l = l + jnp.sum(p.reshape(kc // 8, 8, rows), axis=0)
-                pb = p.astype(jnp.bfloat16)
-                p_s[part, :] = pb
-                o_s[...] += jnp.dot(vt_s[:, part], pb, preferred_element_type=jnp.float32)
-                return l
-
-            o_s[...] = jnp.zeros_like(o_s)
-            l = lax.fori_loop(0, last, weigh, jnp.zeros((8, rows), jnp.float32))
-            acc = o_s[...]
+            o_s[g] = jnp.zeros_like(o_s[g])
+            dq_s[g] = jnp.zeros_like(dq_s[g])
+            return pos, full, last, q, q.T, stacked(do_ref, base).T
+
+        def keys_of(c):
+            return pl.ds(pl.multiple_of(c * kc, kc), kc)
+
+        def scores(g, masked, c, m):
+            pos, qt = state[g][0], state[g][4]
+            s = jnp.dot(kv_ref[keys_of(c), :HEAD], qt, preferred_element_type=jnp.float32)
+            if masked:
+                kpos = c * kc + lax.broadcasted_iota(jnp.int32, (kc, rows), 0)
+                s = jnp.where(kpos <= pos, s, neg_big)
+            s_s[g, keys_of(c), :] = s
+            return jnp.maximum(m, jnp.max(s.reshape(kc // 8, 8, rows), axis=0))
+
+        def weigh(g, m, c, l):
+            p = jnp.exp2((s_s[g, keys_of(c), :] - m) * factor)
+            l = l + jnp.sum(p.reshape(kc // 8, 8, rows), axis=0)
+            pb = p.astype(jnp.bfloat16)
+            p_s[g, keys_of(c), :] = pb
+            o_s[g] += jnp.dot(vt_s[:, keys_of(c)], pb, preferred_element_type=jnp.float32)
+            return l
+
+        def settle(g, l):
             inv = 1.0 / jnp.sum(l, axis=0, keepdims=True)
-            ob = (acc * inv).astype(jnp.bfloat16)
-            spread(0, base, ob.T)
-            dot_f = dot_t.astype(jnp.float32)
+            ob = (o_s[g] * inv).astype(jnp.bfloat16)
+            spread(0, g * gt, ob.T)
+            dot_f = state[g][5].astype(jnp.float32)
             delta = jnp.sum(dot_f * ob.astype(jnp.float32), axis=0, keepdims=True) * inv
             dots = (dot_f * inv).astype(jnp.bfloat16)
-            dos = dots.T
-
-            def back(c, acc):
-                part = pl.ds(pl.multiple_of(c * kc, kc), kc)
-                dp = jnp.dot(kv_ref[part, HEAD:], dots, preferred_element_type=jnp.float32)
-                pb = p_s[part, :]
-                ds = (pb.astype(jnp.float32) * (dp - delta)).astype(jnp.bfloat16)
-                dv_s[part, :] += jnp.dot(pb, dos, preferred_element_type=jnp.float32)
-                dk_s[part, :] += jnp.dot(ds, q, preferred_element_type=jnp.float32)
-                dq_s[...] += jnp.dot(kt_s[:, part], ds, preferred_element_type=jnp.float32)
-                return acc
-
-            dq_s[...] = jnp.zeros_like(dq_s)
-            lax.fori_loop(0, last, back, 0)
-            acc = dq_s[...]
-            spread(1, base, (acc * scale).astype(jnp.bfloat16).T)
+            return delta, dots, dots.T
+
+        def back(g, settled, c):
+            delta, dots, dos = settled
+            dp = jnp.dot(kv_ref[keys_of(c), HEAD:], dots, preferred_element_type=jnp.float32)
+            pb = p_s[g, keys_of(c), :]
+            ds = (pb.astype(jnp.float32) * (dp - delta)).astype(jnp.bfloat16)
+            dv_s[keys_of(c), :] += jnp.dot(pb, dos, preferred_element_type=jnp.float32)
+            dk_s[keys_of(c), :] += jnp.dot(ds, state[g][3], preferred_element_type=jnp.float32)
+            dq_s[g] += jnp.dot(kt_s[:, keys_of(c)], ds, preferred_element_type=jnp.float32)
+
+        def topmost(m):
+            return jnp.max(m, axis=0, keepdims=True)
+
+        state = [prepare(0), prepare(1)]
+        full0, last0 = state[0][1:3]
+        full1, last1 = state[1][1:3]
+        low = jnp.full((8, rows), neg_big, jnp.float32)
+        none = jnp.zeros((8, rows), jnp.float32)
+        m0 = lax.fori_loop(0, full0, functools.partial(scores, 0, False), low)
+        m0 = topmost(lax.fori_loop(full0, last0, functools.partial(scores, 0, True), m0))
+
+        def both_forward(c, carry):
+            return weigh(0, m0, c, carry[0]), scores(1, True, c, carry[1])
+
+        l0, m1 = lax.fori_loop(0, last0, both_forward, (none, low))
+        m1 = lax.fori_loop(last0, full1, functools.partial(scores, 1, False), m1)
+        m1 = topmost(lax.fori_loop(jnp.maximum(last0, full1), last1, functools.partial(scores, 1, True), m1))
+        settled0 = settle(0, l0)
+
+        def both_ways(c, l):
+            back(0, settled0, c)
+            return weigh(1, m1, c, l)
+
+        l1 = lax.fori_loop(0, last0, both_ways, none)
+        l1 = lax.fori_loop(last0, last1, functools.partial(weigh, 1, m1), l1)
+        settled1 = settle(1, l1)
+        spread(1, 0, (dq_s[0] * scale).astype(jnp.bfloat16).T)
+
+        def rest(c, _):
+            back(1, settled1, c)
             return 0
 
-        lax.fori_loop(0, toks // gt, group, 0)
+        lax.fori_loop(0, last1, rest, 0)
+        spread(1, gt, (dq_s[1] * scale).astype(jnp.bfloat16).T)
 
         per = toks // blk
 
@@ -160,14 +181,14 @@
             pltpu.VMEM((total, 2 * HEAD), jnp.bfloat16),
             pltpu.VMEM((HEAD, total), jnp.bfloat16),
             pltpu.VMEM((HEAD, total), jnp.bfloat16),
-            pltpu.VMEM((total, rows), jnp.float32),
-            pltpu.VMEM((total, rows), jnp.bfloat16),
+            pltpu.VMEM((2, total, rows), jnp.float32),
+            pltpu.VMEM((2, total, rows), jnp.bfloat16),
             pltpu.VMEM((total, HEAD), jnp.float32),
             pltpu.VMEM((total, HEAD), jnp.float32),
-            pltpu.VMEM((HEAD, rows), jnp.float32),
-            pltpu.VMEM((HEAD, rows), jnp.float32),
+            pltpu.VMEM((2, HEAD, rows), jnp.float32),
+            pltpu.VMEM((2, HEAD, rows), jnp.float32),
         ],
-        compiler_params=pltpu.CompilerParams(vmem_limit_bytes=48 * 2**20),
+        compiler_params=pltpu.CompilerParams(vmem_limit_bytes=52 * 2**20),
     )(order, meta, mine, other, q, do)
 
 

time: 126 us -> 130 us (1.032); the launches traced: 127 us -> 129 us
  waiting for transfers between devices: 55.2 us -> 53.6 us
  other arithmetic: 6.3 us -> 7.69 us
    ppermute x12, waiting for transfers between devices: 37.4 us -> 34.6 us  [sent(): return lax.ppermute(x, ('grp', 'ctx', 'tp'), pairs)]
    convert_element_type x1, other arithmetic: 1.08 us -> 2.47 us  [shards(): (kept + sent(passed, cores).astype(jnp.float32)).astype(jnp.bfloat16)]
  transfers between devices with their start and end apart: 28 -> 28, of which waited for: 12 -> 15; matrix products, arithmetic and copies ran while one was open for 4% -> 4% of each run, Pallas kernels for 0% -> 0%
where the time goes in v6:
time: 130 us; the launch traced here: 129 us
  waiting for transfers between devices  53.6 us (41%)
  starting transfers between devices  43.6 us (34%)
  Pallas kernels  19.9 us (15%)
  other arithmetic  7.69 us (6%)
  between operations  2.28 us (2%)
  local copies, waits for them, and re-layouts  1.63 us (1%)
    ppermute x12, waiting for transfers between devices, sent(): return lax.ppermute(x, ('grp', 'ctx', 'tp'), pairs)  34.6 us
    ppermute x12, starting transfers between devices, sent(): return lax.ppermute(x, ('grp', 'ctx', 'tp'), pairs)  21.1 us
    pallas_call x1, Pallas kernels, attention(): pl.pallas_call(functools.partial(attention_kernel, heads, total // order....  17.1 us
    ppermute x8, starting transfers between devices, turned(): lax.ppermute(x, 'ctx', [(z * 2 + h, (z + step) % ring * 2 + h) for z in r...  11.6 us
    ppermute x8, waiting for transfers between devices, turned(): lax.ppermute(x, 'ctx', [(z * 2 + h, (z + step) % ring * 2 + h) for z in r...  11.5 us
    all_to_all x1, waiting for transfers between devices, shards(): lax.all_to_all(summed.reshape(ring, total // ctx_size, width), 'ctx', 0,...  7.52 us
    all_to_all x1, starting transfers between devices, shards(): lax.all_to_all(summed.reshape(ring, total // ctx_size, width), 'ctx', 0,...  5.97 us
    ppermute x7, starting transfers between devices, scatter(): arrived = lax.ppermute(parts[step], ('grp', 'ctx'), pairs)  4.84 us
  transfers between devices with their start and end apart: 28, of which 15 were waited for; matrix products, arithmetic and copies ran while one was open for 4% of the time, Pallas kernels for 0%

profile of v6, /device:TPU:11, one launch (start us, length us, event | category | flops | bytes accessed | tf_op | source)
XLA Modules:
  0.0 128.8 jit_solution(7787362783264207619)
XLA Ops:
  0.6 2.8 %shard_map.112 = (s32[1]{0:T(128)}, bf16[384,256]{1,0:T(8,128)(2,1)S(1)}, bf16[384,256]{1,0:T(8,128)(2,1)S(1)}, bf16[384,256]{1,0:T(8,128)(2,1)S(1)}, bf16[384,2...) custom-call(s32[32]{0:T(128)} %lengths_ref.1, ...), custom_call_target="tpu_custom_call" | custom-call | tf_op jit(solution)/shard_map/pallas_call | solution.py:228
  4.1 5.1 %conditional.2 = (bf16[384,256]{1,0:T(8,128)(2,1)S(1)}) conditional(s32[]{:T(128)} %clamp.3, (s32[]{:T(128)}, bf16[384,256]{1,0:T(8,128)(2,1)S(1)}, bf16[384,256]{1,0:T(8,128)(2,1)S(1)}, bf16[384,256]{1,0:T(8,128)(2,1)S(1)}, bf16[384,256]{1,0:T(8,128)(2,1)S(1)}, /*index=5*/bf16[384,256]{1,0:T(8,128)(2,1)S(1)}, ...), branch_computations={%region_0.1_spmd, %region_1.2_spmd, %region_2.3_spmd, %region_3.4_... | conditional | flops 688135 | bytes 7274854 | solution.py:311
  4.1 0.8 collective-permute-start.14
  9.2 4.3 %collective-permute-start.34 = (bf16[192,1024]{1,0:T(8,128)(2,1)S(1)}, bf16[192,1024]{1,0:T(8,128)(2,1)S(1)}, u32[]{:S(2)}, u32[]{:S(2)}) collective-permute-start(bf16[192,1024]{1,0:T(8,128)(2,1)S(1)} %bitcast.46), channel_id=1, source_target_pairs={{129,136},{131,138},{133,140},{135,142},{136,129},{138,131},{140,1... | collective-permute-start | bytes 1179656 | tf_op jit(solution)/shard_map/ppermute | solution.py:281
  13.6 2.8 %collective-permute-start.33 = (bf16[192,1024]{1,0:T(8,128)(2,1)S(1)}, bf16[192,1024]{1,0:T(8,128)(2,1)S(1)}, u32[]{:S(2)}, u32[]{:S(2)}) collective-permute-start(bf16[192,1024]{1,0:T(8,128)(2,1)S(1)} %bitcast.50), channel_id=1, source_target_pairs={{128,128},{129,136},{130,130},{131,138},{132,132},{133,140},{134,1... | collective-permute-start | bytes 1179656 | tf_op jit(solution)/shard_map/ppermute | solution.py:281
  16.3 1.3 %collective-permute-start.32 = (bf16[384,256]{1,0:T(8,128)(2,1)S(1)}, bf16[384,256]{1,0:T(8,128)(2,1)S(1)}, u32[]{:S(2)}, u32[]{:S(2)}) collective-permute-start(bf16[384,256]{1,0:T(8,128)(2,1)S(1)} %get-tuple-element.235), channel_id=1, source_target_pairs={{0,128},{1,136},{2,130},{3,138},{4,132},{5,140},{6,134},{7,142},{8... | collective-permute-start | bytes 589832 | tf_op jit(solution)/shard_map/ppermute | solution.py:281
  17.7 3.2 %sort.17 = (s32[192]{0:T(256)}, s32[192]{0:T(256)S(1)}) sort(s32[192]{0:T(256)S(1)} %copy-done.5, s32[192]{0:T(256)S(1)} %iota.17), dimensions={0}, to_apply=%region_9.10 | sort | flops 1536 | bytes 3072 | tf_op jit(solution)/shard_map/jit(argsort)/sort | solution.py:319
  20.9 14.2 %collective-permute-done.32 = bf16[384,256]{1,0:T(8,128)(2,1)S(1)} collective-permute-done((bf16[384,256]{1,0:T(8,128)(2,1)S(1)}, bf16[384,256]{1,0:T(8,128)(2,1)S(1)}, u32[]{:S(2)}, u32[]{:S(2)}) %collective-permute-start.32) | collective-permute-done | bytes 196640 | tf_op jit(solution)/shard_map/ppermute | solution.py:281
  36.6 3.4 %collective-permute-start.37 = (bf16[192,256]{1,0:T(8,128)(2,1)S(1)}, bf16[192,256]{1,0:T(8,128)(2,1)S(1)}, u32[]{:S(2)}, u32[]{:S(2)}) collective-permute-start(bf16[192,256]{1,0:T(8,128)(2,1)S(1)} %get-tuple-element.216), channel_id=1, source_target_pairs={{0,112},{8,120},{16,0},{24,8},{32,16},{40,24},{48,32},{56,40},{64,... | collective-permute-start | bytes 294920 | tf_op jit(solution)/shard_map/ppermute | solution.py:327
  40.0 1.3 collective-permute-start.36
  41.3 2.9 %collective-permute-done.37 = bf16[192,256]{1,0:T(8,128)(2,1)S(1)} collective-permute-done((bf16[192,256]{1,0:T(8,128)(2,1)S(1)}, bf16[192,256]{1,0:T(8,128)(2,1)S(1)}, u32[]{:S(2)}, u32[]{:S(2)}) %collective-permute-start.37) | collective-permute-done | bytes 98336 | tf_op jit(solution)/shard_map/ppermute | solution.py:327
  44.2 1.4 %collective-permute-start.39 = (bf16[192,256]{1,0:T(8,128)(2,1)S(1)}, bf16[192,256]{1,0:T(8,128)(2,1)S(1)}, u32[]{:S(2)}, u32[]{:S(2)}) collective-permute-start(bf16[192,256]{1,0:T(8,128)(2,1)S(1)} %collective-permute-done.37), channel_id=1, source_target_pairs={{0,112},{8,120},{16,0},{24,8},{32,16},{40,24},{48,32},{56,40},{64,... | collective-permute-start | bytes 294920 | tf_op jit(solution)/shard_map/ppermute | solution.py:327
  46.3 1.3 %collective-permute-done.39 = bf16[192,256]{1,0:T(8,128)(2,1)S(1)} collective-permute-done((bf16[192,256]{1,0:T(8,128)(2,1)S(1)}, bf16[192,256]{1,0:T(8,128)(2,1)S(1)}, u32[]{:S(2)}, u32[]{:S(2)}) %collective-permute-start.39) | collective-permute-done | bytes 98336 | tf_op jit(solution)/shard_map/ppermute | solution.py:327
  47.6 2.6 %collective-permute-start.41 = (bf16[192,256]{1,0:T(8,128)(2,1)S(1)}, bf16[192,256]{1,0:T(8,128)(2,1)S(1)}, u32[]{:S(2)}, u32[]{:S(2)}) collective-permute-start(bf16[192,256]{1,0:T(8,128)(2,1)S(1)} %collective-permute-done.39), channel_id=1, source_target_pairs={{0,112},{8,120},{16,0},{24,8},{32,16},{40,24},{48,32},{56,40},{64,... | collective-permute-start | bytes 294920 | tf_op jit(solution)/shard_map/ppermute | solution.py:327
  51.0 0.9 collective-permute-done.41
  51.9 3.0 %collective-permute-start.43 = (bf16[96,256]{1,0:T(8,128)(2,1)S(1)}, bf16[96,256]{1,0:T(8,128)(2,1)S(1)}, u32[]{:S(2)}, u32[]{:S(2)}) collective-permute-start(bf16[96,256]{1,0:T(8,128)(2,1)S(1)} %slice.49), channel_id=1, source_target_pairs={{0,112},{8,120},{16,0},{24,8},{32,16},{40,24},{48,32},{56,40},{64,... | collective-permute-start | bytes 147464 | tf_op jit(solution)/shard_map/ppermute | solution.py:327
  55.7 4.1 %collective-permute-done.42 = bf16[96,256]{1,0:T(8,128)(2,1)S(1)} collective-permute-done((bf16[96,256]{1,0:T(8,128)(2,1)S(1)}, bf16[96,256]{1,0:T(8,128)(2,1)S(1)}, u32[]{:S(2)}, u32[]{:S(2)}) %collective-permute-start.42) | collective-permute-done | bytes 49184 | tf_op jit(solution)/shard_map/ppermute | solution.py:327
  59.8 4.5 %collective-permute-start.44 = (bf16[1536,256]{1,0:T(8,128)(2,1)S(1)}, bf16[1536,256]{1,0:T(8,128)(2,1)S(1)}, u32[]{:S(2)}, u32[]{:S(2)}) collective-permute-start(bf16[1536,256]{1,0:T(8,128)(2,1)S(1)} %constant_dynamic-update-slice_fusion.refs_0_), channel_id=1, source_target_pairs={{0,1},{1,0},{2,3},{3,2},{4,5},{5,4},{6,7},{7,6},{8,9},{9,8},{10,11... | collective-permute-start | bytes 2359304 | tf_op jit(solution)/shard_map/ppermute | solution.py:281
  64.4 1.8 %collective-permute-done.44.refs_1_ = bf16[1536,256]{1,0:T(8,128)(2,1)S(1)} collective-permute-done((bf16[1536,256]{1,0:T(8,128)(2,1)S(1)}, bf16[1536,256]{1,0:T(8,128)(2,1)S(1)}, u32[]{:S(2)}, u32[]{:S(2)}) %collective-permute-start.44) | collective-permute-done | bytes 786464 | tf_op jit(solution)/shard_map/ppermute | solution.py:281
  66.2 0.9 copy-done.1
  67.1 17.1 %shard_map.113 = (bf16[2,192,1024]{2,1,0:T(8,128)(2,1)S(1)}, f32[1536,256]{1,0:T(8,128)}, bf16[1536,256]{1,0:T(8,128)(2,1)}) custom-call(s32[192]{0:T(256)S(1)} %get-tuple-element.197.order_ref, s32[3]{0:T(128)S(1)} %pad_add_fusion.meta_ref, bf16[1536,256]{1,0:T(8,128)(2,1)} %copy-done, bf16[1536,256]{1,0:T(8,128)(2,1)} %copy-done.1, ...), custom_call_target="tpu_custom_call" | custom-call | tf_op jit(solution)/shard_map/pallas_call | solution.py:171
  84.2 2.2 %collective-permute-start.45 = (bf16[1536,256]{1,0:T(8,128)(2,1)}, bf16[1536,256]{1,0:T(8,128)(2,1)S(1)}, u32[]{:S(2)}, u32[]{:S(2)}) collective-permute-start(bf16[1536,256]{1,0:T(8,128)(2,1)} %get-tuple-element.202), channel_id=1, source_target_pairs={{0,1},{1,0},{2,3},{3,2},{4,5},{5,4},{6,7},{7,6},{8,9},{9,8},{10,11... | collective-permute-start | bytes 2359304 | tf_op jit(solution)/shard_map/ppermute | solution.py:281
  86.5 2.1 %collective-permute-done.45 = bf16[1536,256]{1,0:T(8,128)(2,1)S(1)} collective-permute-done((bf16[1536,256]{1,0:T(8,128)(2,1)}, bf16[1536,256]{1,0:T(8,128)(2,1)S(1)}, u32[]{:S(2)}, u32[]{:S(2)}) %collective-permute-start.45) | collective-permute-done | bytes 786464 | tf_op jit(solution)/shard_map/ppermute | solution.py:281
  88.6 2.5 %add_convert_fusion = bf16[1536,256]{1,0:T(8,128)(2,1)} fusion(f32[1536,256]{1,0:T(8,128)} %get-tuple-element.201, bf16[1536,256]{1,0:T(8,128)(2,1)S(1)} %collective-permute-done.45), kind=kLoop, calls=%fused_computation.39 | loop fusion | flops 1179648 | bytes 3145728 | tf_op jit(solution)/shard_map/convert_element_type | solution.py:339
  91.1 6.0 %all-to-all-start = ((bf16[8,192,256]{2,1,0:T(8,128)(2,1)}), bf16[8,192,256]{2,1,0:T(8,128)(2,1)S(1)}, u32[]{:S(2)}, u32[]{:S(2)}) async-start(bf16[8,192,256]{2,1,0:T(8,128)(2,1)} %bitcast.16), calls=%async_computation | async-start | bytes 1572864 | tf_op jit(solution)/shard_map/all_to_all | solution.py:340
  97.1 1.9 %collective-permute-start.46 = (bf16[2,192,1024]{2,1,0:T(8,128)(2,1)S(1)}, bf16[2,192,1024]{2,1,0:T(8,128)(2,1)S(1)}, u32[]{:S(2)}, u32[]{:S(2)}) collective-permute-start(bf16[2,192,1024]{2,1,0:T(8,128)(2,1)S(1)} %get-tuple-element.203), channel_id=1, source_target_pairs={{129,136},{131,138},{133,140},{135,142},{136,129},{138,131},{140,1... | collective-permute-start | bytes 2359304 | tf_op jit(solution)/shard_map/ppermute | solution.py:281
  99.1 1.2 collective-permute-done.28
  102.4 9.7 %collective-permute-done.46 = bf16[2,192,1024]{2,1,0:T(8,128)(2,1)S(1)} collective-permute-done((bf16[2,192,1024]{2,1,0:T(8,128)(2,1)S(1)}, bf16[2,192,1024]{2,1,0:T(8,128)(2,1)S(1)}, u32[]{:S(2)}, u32[]{:S(2)}) %collective-permute-start.46) | collective-permute-done | bytes 786464 | tf_op jit(solution)/shard_map/ppermute | solution.py:281
  112.2 1.0 fusion.36
  113.1 7.5 %all-to-all-done = bf16[8,192,256]{2,1,0:T(8,128)(2,1)S(1)} async-done(((bf16[8,192,256]{2,1,0:T(8,128)(2,1)}), bf16[8,192,256]{2,1,0:T(8,128)(2,1)S(1)}, u32[]{:S(2)}, u32[]{:S(2)}) %all-to-all-start) | async-done | bytes 786464 | tf_op jit(solution)/shard_map/all_to_all | solution.py:340
  120.8 1.9 %collective-permute-start.47 = (bf16[192,256]{1,0:T(8,128)(2,1)S(1)}, bf16[192,256]{1,0:T(8,128)(2,1)S(1)}, u32[]{:S(2)}, u32[]{:S(2)}) collective-permute-start(bf16[192,256]{1,0:T(8,128)(2,1)S(1)} %reduce_sum.32), channel_id=1, source_target_pairs={{128,128},{129,136},{130,130},{131,138},{132,132},{133,140},{134,1... | collective-permute-start | bytes 294920 | tf_op jit(solution)/shard_map/ppermute | solution.py:281
  123.4 4.8 %collective-permute-done.47 = bf16[192,256]{1,0:T(8,128)(2,1)S(1)} collective-permute-done((bf16[192,256]{1,0:T(8,128)(2,1)S(1)}, bf16[192,256]{1,0:T(8,128)(2,1)S(1)}, u32[]{:S(2)}, u32[]{:S(2)}) %collective-permute-start.47) | collective-permute-done | bytes 98336 | tf_op jit(solution)/shard_map/ppermute | solution.py:281
  (68 shorter events, 11.0 us)
Async XLA Ops:
  4.1 13.6 %copy-start.5 = (s32[192]{0:T(256)S(1)}, s32[192]{0:T(256)}, u32[]{:S(2)}) copy-start(s32[192]{0:T(256)} %param.19) | copy-start | bytes 2308
  4.1 3.5 %collective-permute-start.14 = (bf16[384,256]{1,0:T(8,128)(2,1)S(1)}, bf16[384,256]{1,0:T(8,128)(2,1)S(1)}, u32[]{:S(2)}, u32[]{:S(2)}) collective-permute-start(bf16[384,256]{1,0:T(8,128)(2,1)S(1)} %get-tuple-element.138), channel_id=1, source_target_pairs={{32,96},{40,104},{96,32},{104,40},{33,97},{41,105},{97,33},{105,41... | collective-permute-start | bytes 589832 | tf_op jit(solution)/shard_map/cond/branch_2_fun/ppermute | solution.py:304
  4.9 3.4 %collective-permute-start.15 = (bf16[384,256]{1,0:T(8,128)(2,1)S(1)}, bf16[384,256]{1,0:T(8,128)(2,1)S(1)}, u32[]{:S(2)}, u32[]{:S(2)}) collective-permute-start(bf16[384,256]{1,0:T(8,128)(2,1)S(1)} %get-tuple-element.139), channel_id=1, source_target_pairs={{32,80},{40,88},{96,16},{104,24},{33,81},{41,89},{97,17},{105,25},... | collective-permute-start | bytes 589832 | tf_op jit(solution)/shard_map/cond/branch_2_fun/ppermute | solution.py:304
  5.6 3.4 %collective-permute-start.16 = (bf16[384,256]{1,0:T(8,128)(2,1)S(1)}, bf16[384,256]{1,0:T(8,128)(2,1)S(1)}, u32[]{:S(2)}, u32[]{:S(2)}) collective-permute-start(bf16[384,256]{1,0:T(8,128)(2,1)S(1)} %get-tuple-element.140), channel_id=1, source_target_pairs={{32,112},{40,120},{96,48},{104,56},{33,113},{41,121},{97,49},{105,... | collective-permute-start | bytes 589832 | tf_op jit(solution)/shard_map/cond/branch_2_fun/ppermute | solution.py:304
  6.3 2.8 %collective-permute-start.17 = (bf16[384,256]{1,0:T(8,128)(2,1)S(1)}, bf16[384,256]{1,0:T(8,128)(2,1)S(1)}, u32[]{:S(2)}, u32[]{:S(2)}) collective-permute-start(bf16[384,256]{1,0:T(8,128)(2,1)S(1)} %get-tuple-element.141), channel_id=1, source_target_pairs={{32,64},{40,72},{96,0},{104,8},{33,65},{41,73},{97,1},{105,9},{34,... | collective-permute-start | bytes 589832 | tf_op jit(solution)/shard_map/cond/branch_2_fun/ppermute | solution.py:304
  7.0 2.1 %collective-permute-start.18 = (bf16[384,256]{1,0:T(8,128)(2,1)S(1)}, bf16[384,256]{1,0:T(8,128)(2,1)S(1)}, u32[]{:S(2)}, u32[]{:S(2)}) collective-permute-start(bf16[384,256]{1,0:T(8,128)(2,1)S(1)} %get-tuple-element.142), channel_id=1, source_target_pairs={{32,0},{40,8},{96,64},{104,72},{33,1},{41,9},{97,65},{105,73},{34,... | collective-permute-start | bytes 589832 | tf_op jit(solution)/shard_map/cond/branch_2_fun/ppermute | solution.py:304
  7.7 1.4 %collective-permute-start.19 = (bf16[384,256]{1,0:T(8,128)(2,1)S(1)}, bf16[384,256]{1,0:T(8,128)(2,1)S(1)}, u32[]{:S(2)}, u32[]{:S(2)}) collective-permute-start(bf16[384,256]{1,0:T(8,128)(2,1)S(1)} %get-tuple-element.143), channel_id=1, source_target_pairs={{32,48},{40,56},{96,112},{104,120},{33,49},{41,57},{97,113},{105,1... | collective-permute-start | bytes 589832 | tf_op jit(solution)/shard_map/cond/branch_2_fun/ppermute | solution.py:304
  8.4 0.7 collective-permute-start.20
  9.2 11.6 %collective-permute-start.34 = (bf16[192,1024]{1,0:T(8,128)(2,1)S(1)}, bf16[192,1024]{1,0:T(8,128)(2,1)S(1)}, u32[]{:S(2)}, u32[]{:S(2)}) collective-permute-start(bf16[192,1024]{1,0:T(8,128)(2,1)S(1)} %bitcast.46), channel_id=1, source_target_pairs={{129,136},{131,138},{133,140},{135,142},{136,129},{138,131},{140,1... | collective-permute-start | bytes 1179656 | tf_op jit(solution)/shard_map/ppermute | solution.py:281
  13.6 21.6 %collective-permute-start.33 = (bf16[192,1024]{1,0:T(8,128)(2,1)S(1)}, bf16[192,1024]{1,0:T(8,128)(2,1)S(1)}, u32[]{:S(2)}, u32[]{:S(2)}) collective-permute-start(bf16[192,1024]{1,0:T(8,128)(2,1)S(1)} %bitcast.50), channel_id=1, source_target_pairs={{128,128},{129,136},{130,130},{131,138},{132,132},{133,140},{134,1... | collective-permute-start | bytes 1179656 | tf_op jit(solution)/shard_map/ppermute | solution.py:281
  16.3 18.8 %collective-permute-start.32 = (bf16[384,256]{1,0:T(8,128)(2,1)S(1)}, bf16[384,256]{1,0:T(8,128)(2,1)S(1)}, u32[]{:S(2)}, u32[]{:S(2)}) collective-permute-start(bf16[384,256]{1,0:T(8,128)(2,1)S(1)} %get-tuple-element.235), channel_id=1, source_target_pairs={{0,128},{1,136},{2,130},{3,138},{4,132},{5,140},{6,134},{7,142},{8... | collective-permute-start | bytes 589832 | tf_op jit(solution)/shard_map/ppermute | solution.py:281
  35.1 1.4 %collective-permute-start.35 = (bf16[192,256]{1,0:T(8,128)(2,1)S(1)}, bf16[192,256]{1,0:T(8,128)(2,1)S(1)}, u32[]{:S(2)}, u32[]{:S(2)}) collective-permute-start(bf16[192,256]{1,0:T(8,128)(2,1)S(1)} %broadcast_select_fusion.1), channel_id=1, source_target_pairs={{0,1},{1,0},{2,3},{3,2},{4,5},{5,4},{6,7},{7,6},{8,9},{9,8},{10,11... | collective-permute-start | bytes 294920 | tf_op jit(solution)/shard_map/ppermute | solution.py:281
  36.6 7.6 %collective-permute-start.37 = (bf16[192,256]{1,0:T(8,128)(2,1)S(1)}, bf16[192,256]{1,0:T(8,128)(2,1)S(1)}, u32[]{:S(2)}, u32[]{:S(2)}) collective-permute-start(bf16[192,256]{1,0:T(8,128)(2,1)S(1)} %get-tuple-element.216), channel_id=1, source_target_pairs={{0,112},{8,120},{16,0},{24,8},{32,16},{40,24},{48,32},{56,40},{64,... | collective-permute-start | bytes 294920 | tf_op jit(solution)/shard_map/ppermute | solution.py:327
  40.0 6.3 %collective-permute-start.36 = (bf16[192,256]{1,0:T(8,128)(2,1)S(1)}, bf16[192,256]{1,0:T(8,128)(2,1)S(1)}, u32[]{:S(2)}, u32[]{:S(2)}) collective-permute-start(bf16[192,256]{1,0:T(8,128)(2,1)S(1)} %get-tuple-element.216), channel_id=1, source_target_pairs={{0,16},{8,24},{16,32},{24,40},{32,48},{40,56},{48,64},{56,72},{64,... | collective-permute-start | bytes 294920 | tf_op jit(solution)/shard_map/ppermute | solution.py:327
  44.2 3.5 %collective-permute-start.39 = (bf16[192,256]{1,0:T(8,128)(2,1)S(1)}, bf16[192,256]{1,0:T(8,128)(2,1)S(1)}, u32[]{:S(2)}, u32[]{:S(2)}) collective-permute-start(bf16[192,256]{1,0:T(8,128)(2,1)S(1)} %collective-permute-done.37), channel_id=1, source_target_pairs={{0,112},{8,120},{16,0},{24,8},{32,16},{40,24},{48,32},{56,40},{64,... | collective-permute-start | bytes 294920 | tf_op jit(solution)/shard_map/ppermute | solution.py:327
  46.3 4.7 %collective-permute-start.38 = (bf16[192,256]{1,0:T(8,128)(2,1)S(1)}, bf16[192,256]{1,0:T(8,128)(2,1)S(1)}, u32[]{:S(2)}, u32[]{:S(2)}) collective-permute-start(bf16[192,256]{1,0:T(8,128)(2,1)S(1)} %collective-permute-done.36), channel_id=1, source_target_pairs={{0,16},{8,24},{16,32},{24,40},{32,48},{40,56},{48,64},{56,72},{64,... | collective-permute-start | bytes 294920 | tf_op jit(solution)/shard_map/ppermute | solution.py:327
  47.6 4.2 %collective-permute-start.41 = (bf16[192,256]{1,0:T(8,128)(2,1)S(1)}, bf16[192,256]{1,0:T(8,128)(2,1)S(1)}, u32[]{:S(2)}, u32[]{:S(2)}) collective-permute-start(bf16[192,256]{1,0:T(8,128)(2,1)S(1)} %collective-permute-done.39), channel_id=1, source_target_pairs={{0,112},{8,120},{16,0},{24,8},{32,16},{40,24},{48,32},{56,40},{64,... | collective-permute-start | bytes 294920 | tf_op jit(solution)/shard_map/ppermute | solution.py:327
  51.0 4.7 %collective-permute-start.40 = (bf16[192,256]{1,0:T(8,128)(2,1)S(1)}, bf16[192,256]{1,0:T(8,128)(2,1)S(1)}, u32[]{:S(2)}, u32[]{:S(2)}) collective-permute-start(bf16[192,256]{1,0:T(8,128)(2,1)S(1)} %collective-permute-done.38), channel_id=1, source_target_pairs={{0,16},{8,24},{16,32},{24,40},{32,48},{40,56},{48,64},{56,72},{64,... | collective-permute-start | bytes 294920 | tf_op jit(solution)/shard_map/ppermute | solution.py:327
  51.9 7.9 %collective-permute-start.43 = (bf16[96,256]{1,0:T(8,128)(2,1)S(1)}, bf16[96,256]{1,0:T(8,128)(2,1)S(1)}, u32[]{:S(2)}, u32[]{:S(2)}) collective-permute-start(bf16[96,256]{1,0:T(8,128)(2,1)S(1)} %slice.49), channel_id=1, source_target_pairs={{0,112},{8,120},{16,0},{24,8},{32,16},{40,24},{48,32},{56,40},{64,... | collective-permute-start | bytes 147464 | tf_op jit(solution)/shard_map/ppermute | solution.py:327
  55.6 4.2 %collective-permute-start.42 = (bf16[96,256]{1,0:T(8,128)(2,1)S(1)}, bf16[96,256]{1,0:T(8,128)(2,1)S(1)}, u32[]{:S(2)}, u32[]{:S(2)}) collective-permute-start(bf16[96,256]{1,0:T(8,128)(2,1)S(1)} %slice.48), channel_id=1, source_target_pairs={{0,16},{8,24},{16,32},{24,40},{32,48},{40,56},{48,64},{56,72},{64,... | collective-permute-start | bytes 147464 | tf_op jit(solution)/shard_map/ppermute | solution.py:327
  59.8 6.4 %collective-permute-start.44 = (bf16[1536,256]{1,0:T(8,128)(2,1)S(1)}, bf16[1536,256]{1,0:T(8,128)(2,1)S(1)}, u32[]{:S(2)}, u32[]{:S(2)}) collective-permute-start(bf16[1536,256]{1,0:T(8,128)(2,1)S(1)} %constant_dynamic-update-slice_fusion.refs_0_), channel_id=1, source_target_pairs={{0,1},{1,0},{2,3},{3,2},{4,5},{5,4},{6,7},{7,6},{8,9},{9,8},{10,11... | collective-permute-start | bytes 2359304 | tf_op jit(solution)/shard_map/ppermute | solution.py:281
  64.4 34.6 %copy-start.3 = (bf16[1,2,256]{2,1,0:T(2,128)(2,1)S(1)}, bf16[1,2,256]{2,1,0:T(2,128)(2,1)}, u32[]{:S(2)}) copy-start(bf16[1,2,256]{2,1,0:T(2,128)(2,1)} %param.15) | copy-start | bytes 3076
  64.4 34.6 %copy-start.4 = (s32[32]{0:T(128)S(1)}, s32[32]{0:T(128)}, u32[]{:S(2)}) copy-start(s32[32]{0:T(128)} %lengths_ref.1) | copy-start | bytes 388
  64.4 34.6 %copy-start.7 = (bf16[1,2,1024]{2,1,0:T(2,128)(2,1)S(1)}, bf16[1,2,1024]{2,1,0:T(2,128)(2,1)}, u32[]{:S(2)}) copy-start(bf16[1,2,1024]{2,1,0:T(2,128)(2,1)} %param.16) | copy-start | bytes 12292
  84.2 4.4 %collective-permute-start.45 = (bf16[1536,256]{1,0:T(8,128)(2,1)}, bf16[1536,256]{1,0:T(8,128)(2,1)S(1)}, u32[]{:S(2)}, u32[]{:S(2)}) collective-permute-start(bf16[1536,256]{1,0:T(8,128)(2,1)} %get-tuple-element.202), channel_id=1, source_target_pairs={{0,1},{1,0},{2,3},{3,2},{4,5},{5,4},{6,7},{7,6},{8,9},{9,8},{10,11... | collective-permute-start | bytes 2359304 | tf_op jit(solution)/shard_map/ppermute | solution.py:281
  91.1 29.5 %all-to-all-start = ((bf16[8,192,256]{2,1,0:T(8,128)(2,1)}), bf16[8,192,256]{2,1,0:T(8,128)(2,1)S(1)}, u32[]{:S(2)}, u32[]{:S(2)}) async-start(bf16[8,192,256]{2,1,0:T(8,128)(2,1)} %bitcast.16), calls=%async_computation | async-start | bytes 1572864 | tf_op jit(solution)/shard_map/all_to_all | solution.py:340
  97.1 15.1 %collective-permute-start.46 = (bf16[2,192,1024]{2,1,0:T(8,128)(2,1)S(1)}, bf16[2,192,1024]{2,1,0:T(8,128)(2,1)S(1)}, u32[]{:S(2)}, u32[]{:S(2)}) collective-permute-start(bf16[2,192,1024]{2,1,0:T(8,128)(2,1)S(1)} %get-tuple-element.203), channel_id=1, source_target_pairs={{129,136},{131,138},{133,140},{135,142},{136,129},{138,131},{140,1... | collective-permute-start | bytes 2359304 | tf_op jit(solution)/shard_map/ppermute | solution.py:281
  99.0 1.3 collective-permute-start.28
  100.3 0.7 collective-permute-start.29
  101.0 0.7 collective-permute-start.30
  101.7 20.9 %collective-permute-start.31 = (f32[2,2560]{1,0:T(2,128)S(1)}, f32[2,2560]{1,0:T(2,128)S(1)}, u32[]{:S(2)}, u32[]{:S(2)}) collective-permute-start(f32[2,2560]{1,0:T(2,128)S(1)} %collective-permute-done.30), channel_id=1, source_target_pairs={{0,2},{1,3},{2,4},{3,5},{4,6},{5,7},{6,0},{7,1},{8,10},{9,11},{10,... | collective-permute-start | bytes 61448 | tf_op jit(solution)/shard_map/ppermute | solution.py:281
  120.8 7.4 %collective-permute-start.47 = (bf16[192,256]{1,0:T(8,128)(2,1)S(1)}, bf16[192,256]{1,0:T(8,128)(2,1)S(1)}, u32[]{:S(2)}, u32[]{:S(2)}) collective-permute-start(bf16[192,256]{1,0:T(8,128)(2,1)S(1)} %reduce_sum.32), channel_id=1, source_target_pairs={{128,128},{129,136},{130,130},{131,138},{132,132},{133,140},{134,1... | collective-permute-start | bytes 294920 | tf_op jit(solution)/shard_map/ppermute | solution.py:281
  (4 other events, 21.9 us)

commit v7 on v6

--- a/solution.py
+++ b/solution.py
@@ -84,14 +84,14 @@
             if masked:
                 kpos = c * kc + lax.broadcasted_iota(jnp.int32, (kc, rows), 0)
                 s = jnp.where(kpos <= pos, s, neg_big)
-            s_s[g, keys_of(c), :] = s
+            s_s[keys_of(c), :] = s
             return jnp.maximum(m, jnp.max(s.reshape(kc // 8, 8, rows), axis=0))
 
         def weigh(g, m, c, l):
-            p = jnp.exp2((s_s[g, keys_of(c), :] - m) * factor)
+            p = jnp.exp2((s_s[keys_of(c), :] - m) * factor)
             l = l + jnp.sum(p.reshape(kc // 8, 8, rows), axis=0)
             pb = p.astype(jnp.bfloat16)
-            p_s[g, keys_of(c), :] = pb
+            p_s[keys_of(c), :] = pb
             o_s[g] += jnp.dot(vt_s[:, keys_of(c)], pb, preferred_element_type=jnp.float32)
             return l
 
@@ -107,7 +107,7 @@
         def back(g, settled, c):
             delta, dots, dos = settled
             dp = jnp.dot(kv_ref[keys_of(c), HEAD:], dots, preferred_element_type=jnp.float32)
-            pb = p_s[g, keys_of(c), :]
+            pb = p_s[keys_of(c), :]
             ds = (pb.astype(jnp.float32) * (dp - delta)).astype(jnp.bfloat16)
             dv_s[keys_of(c), :] += jnp.dot(pb, dos, preferred_element_type=jnp.float32)
             dk_s[keys_of(c), :] += jnp.dot(ds, state[g][3], preferred_element_type=jnp.float32)
@@ -181,14 +181,14 @@
             pltpu.VMEM((total, 2 * HEAD), jnp.bfloat16),
             pltpu.VMEM((HEAD, total), jnp.bfloat16),
             pltpu.VMEM((HEAD, total), jnp.bfloat16),
-            pltpu.VMEM((2, total, rows), jnp.float32),
-            pltpu.VMEM((2, total, rows), jnp.bfloat16),
+            pltpu.VMEM((total, rows), jnp.float32),
+            pltpu.VMEM((total, rows), jnp.bfloat16),
             pltpu.VMEM((total, HEAD), jnp.float32),
             pltpu.VMEM((total, HEAD), jnp.float32),
             pltpu.VMEM((2, HEAD, rows), jnp.float32),
             pltpu.VMEM((2, HEAD, rows), jnp.float32),
         ],
-        compiler_params=pltpu.CompilerParams(vmem_limit_bytes=52 * 2**20),
+        compiler_params=pltpu.CompilerParams(vmem_limit_bytes=40 * 2**20),
     )(order, meta, mine, other, q, do)
 
 

time: 130 us -> 125 us (0.962)
  starting transfers between devices: 43.6 us -> 37.9 us
  other arithmetic: 7.69 us -> 6.3 us
  Pallas kernels: 19.9 us -> 21.2 us
    all_to_all x1, starting transfers between devices: 5.97 us -> 3.55 us  [shards(): lax.all_to_all(summed.reshape(ring, total // ctx_size, width), 'ctx', 0,...]
    ppermute x8, starting transfers between devices: 11.6 us -> 9.9 us  [turned(): lax.ppermute(x, 'ctx', [(z * 2 + h, (z + step) % ring * 2 + h) for z in r...]
    ppermute x12, starting transfers between devices: 21.1 us -> 19.6 us  [sent(): return lax.ppermute(x, ('grp', 'ctx', 'tp'), pairs)]
    convert_element_type x1, other arithmetic: 2.47 us -> 1.08 us  [shards(): (kept + sent(passed, cores).astype(jnp.float32)).astype(jnp.bfloat16)]
    ppermute x12, waiting for transfers between devices: 34.6 us -> 35.9 us  [sent(): return lax.ppermute(x, ('grp', 'ctx', 'tp'), pairs)]
    pallas_call x1, Pallas kernels: 17.1 us -> 18.4 us  [attention(): pl.pallas_call(functools.partial(attention_kernel, heads, total // order....]
  transfers between devices with their start and end apart: 28 -> 28, of which waited for: 15 -> 12; matrix products, arithmetic and copies ran while one was open for 4% -> 4% of each run, Pallas kernels for 0% -> 0%
where the time goes in v7:
time: 125 us; the launch traced here: 123 us
  waiting for transfers between devices  54.3 us (43%)
  starting transfers between devices  37.9 us (30%)
  Pallas kernels  21.2 us (17%)
  other arithmetic  6.3 us (5%)
  between operations  2.12 us (2%)
    ppermute x12, waiting for transfers between devices, sent(): return lax.ppermute(x, ('grp', 'ctx', 'tp'), pairs)  35.9 us
    ppermute x12, starting transfers between devices, sent(): return lax.ppermute(x, ('grp', 'ctx', 'tp'), pairs)  19.6 us
    pallas_call x1, Pallas kernels, attention(): pl.pallas_call(functools.partial(attention_kernel, heads, total // order....  18.4 us
    ppermute x8, waiting for transfers between devices, turned(): lax.ppermute(x, 'ctx', [(z * 2 + h, (z + step) % ring * 2 + h) for z in r...  10.9 us
    ppermute x8, starting transfers between devices, turned(): lax.ppermute(x, 'ctx', [(z * 2 + h, (z + step) % ring * 2 + h) for z in r...  9.9 us
    all_to_all x1, waiting for transfers between devices, shards(): lax.all_to_all(summed.reshape(ring, total // ctx_size, width), 'ctx', 0,...  7.48 us
    ppermute x7, starting transfers between devices, scatter(): arrived = lax.ppermute(parts[step], ('grp', 'ctx'), pairs)  4.84 us
    all_to_all x1, starting transfers between devices, shards(): lax.all_to_all(summed.reshape(ring, total // ctx_size, width), 'ctx', 0,...  3.55 us
  transfers between devices with their start and end apart: 28, of which 12 were waited for; matrix products, arithmetic and copies ran while one was open for 4% of the time, Pallas kernels for 0%

profile of v7, /device:TPU:11, one launch (start us, length us, event | category | flops | bytes accessed | tf_op | source)
XLA Modules:
  0.0 122.8 jit_solution(5475716392840016462)
XLA Ops:
  0.6 2.8 %shard_map.112 = (s32[1]{0:T(128)}, bf16[384,256]{1,0:T(8,128)(2,1)S(1)}, bf16[384,256]{1,0:T(8,128)(2,1)S(1)}, bf16[384,256]{1,0:T(8,128)(2,1)S(1)}, bf16[384,2...) custom-call(s32[32]{0:T(128)} %lengths_ref.1, ...), custom_call_target="tpu_custom_call" | custom-call | tf_op jit(solution)/shard_map/pallas_call | solution.py:228
  4.0 5.1 %conditional.2 = (bf16[384,256]{1,0:T(8,128)(2,1)S(1)}) conditional(s32[]{:T(128)} %clamp.3, (s32[]{:T(128)}, bf16[384,256]{1,0:T(8,128)(2,1)S(1)}, bf16[384,256]{1,0:T(8,128)(2,1)S(1)}, bf16[384,256]{1,0:T(8,128)(2,1)S(1)}, bf16[384,256]{1,0:T(8,128)(2,1)S(1)}, /*index=5*/bf16[384,256]{1,0:T(8,128)(2,1)S(1)}, ...), branch_computations={%region_0.1_spmd, %region_1.2_spmd, %region_2.3_spmd, %region_3.4_... | conditional | flops 688135 | bytes 7274854 | solution.py:311
  4.1 0.8 collective-permute-start.21
  4.9 0.7 collective-permute-start.22
  9.2 4.3 %collective-permute-start.34 = (bf16[192,1024]{1,0:T(8,128)(2,1)S(1)}, bf16[192,1024]{1,0:T(8,128)(2,1)S(1)}, u32[]{:S(2)}, u32[]{:S(2)}) collective-permute-start(bf16[192,1024]{1,0:T(8,128)(2,1)S(1)} %bitcast.46), channel_id=1, source_target_pairs={{129,136},{131,138},{133,140},{135,142},{136,129},{138,131},{140,1... | collective-permute-start | bytes 1179656 | tf_op jit(solution)/shard_map/ppermute | solution.py:281
  13.5 2.8 %collective-permute-start.33 = (bf16[192,1024]{1,0:T(8,128)(2,1)S(1)}, bf16[192,1024]{1,0:T(8,128)(2,1)S(1)}, u32[]{:S(2)}, u32[]{:S(2)}) collective-permute-start(bf16[192,1024]{1,0:T(8,128)(2,1)S(1)} %bitcast.50), channel_id=1, source_target_pairs={{128,128},{129,136},{130,130},{131,138},{132,132},{133,140},{134,1... | collective-permute-start | bytes 1179656 | tf_op jit(solution)/shard_map/ppermute | solution.py:281
  16.3 1.3 %collective-permute-start.32 = (bf16[384,256]{1,0:T(8,128)(2,1)S(1)}, bf16[384,256]{1,0:T(8,128)(2,1)S(1)}, u32[]{:S(2)}, u32[]{:S(2)}) collective-permute-start(bf16[384,256]{1,0:T(8,128)(2,1)S(1)} %get-tuple-element.235), channel_id=1, source_target_pairs={{0,128},{1,136},{2,130},{3,138},{4,132},{5,140},{6,134},{7,142},{8... | collective-permute-start | bytes 589832 | tf_op jit(solution)/shard_map/ppermute | solution.py:281
  17.6 3.2 %sort.17 = (s32[192]{0:T(256)}, s32[192]{0:T(256)S(1)}) sort(s32[192]{0:T(256)S(1)} %copy-done.3, s32[192]{0:T(256)S(1)} %iota.17), dimensions={0}, to_apply=%region_9.10 | sort | flops 1536 | bytes 3072 | tf_op jit(solution)/shard_map/jit(argsort)/sort | solution.py:319
  20.8 15.7 %collective-permute-done.32 = bf16[384,256]{1,0:T(8,128)(2,1)S(1)} collective-permute-done((bf16[384,256]{1,0:T(8,128)(2,1)S(1)}, bf16[384,256]{1,0:T(8,128)(2,1)S(1)}, u32[]{:S(2)}, u32[]{:S(2)}) %collective-permute-start.32) | collective-permute-done | bytes 196640 | tf_op jit(solution)/shard_map/ppermute | solution.py:281
  37.2 0.7 collective-permute-done.35
  38.0 1.8 %collective-permute-start.37 = (bf16[192,256]{1,0:T(8,128)(2,1)S(1)}, bf16[192,256]{1,0:T(8,128)(2,1)S(1)}, u32[]{:S(2)}, u32[]{:S(2)}) collective-permute-start(bf16[192,256]{1,0:T(8,128)(2,1)S(1)} %get-tuple-element.216), channel_id=1, source_target_pairs={{0,112},{8,120},{16,0},{24,8},{32,16},{40,24},{48,32},{56,40},{64,... | collective-permute-start | bytes 294920 | tf_op jit(solution)/shard_map/ppermute | solution.py:327
  39.8 2.5 %collective-permute-done.37 = bf16[192,256]{1,0:T(8,128)(2,1)S(1)} collective-permute-done((bf16[192,256]{1,0:T(8,128)(2,1)S(1)}, bf16[192,256]{1,0:T(8,128)(2,1)S(1)}, u32[]{:S(2)}, u32[]{:S(2)}) %collective-permute-start.37) | collective-permute-done | bytes 98336 | tf_op jit(solution)/shard_map/ppermute | solution.py:327
  42.3 2.9 %collective-permute-start.39 = (bf16[192,256]{1,0:T(8,128)(2,1)S(1)}, bf16[192,256]{1,0:T(8,128)(2,1)S(1)}, u32[]{:S(2)}, u32[]{:S(2)}) collective-permute-start(bf16[192,256]{1,0:T(8,128)(2,1)S(1)} %collective-permute-done.37), channel_id=1, source_target_pairs={{0,112},{8,120},{16,0},{24,8},{32,16},{40,24},{48,32},{56,40},{64,... | collective-permute-start | bytes 294920 | tf_op jit(solution)/shard_map/ppermute | solution.py:327
  45.6 2.4 %collective-permute-done.39 = bf16[192,256]{1,0:T(8,128)(2,1)S(1)} collective-permute-done((bf16[192,256]{1,0:T(8,128)(2,1)S(1)}, bf16[192,256]{1,0:T(8,128)(2,1)S(1)}, u32[]{:S(2)}, u32[]{:S(2)}) %collective-permute-start.39) | collective-permute-done | bytes 98336 | tf_op jit(solution)/shard_map/ppermute | solution.py:327
  48.0 1.9 %collective-permute-start.41 = (bf16[192,256]{1,0:T(8,128)(2,1)S(1)}, bf16[192,256]{1,0:T(8,128)(2,1)S(1)}, u32[]{:S(2)}, u32[]{:S(2)}) collective-permute-start(bf16[192,256]{1,0:T(8,128)(2,1)S(1)} %collective-permute-done.39), channel_id=1, source_target_pairs={{0,112},{8,120},{16,0},{24,8},{32,16},{40,24},{48,32},{56,40},{64,... | collective-permute-start | bytes 294920 | tf_op jit(solution)/shard_map/ppermute | solution.py:327
  50.0 1.8 %collective-permute-done.41 = bf16[192,256]{1,0:T(8,128)(2,1)S(1)} collective-permute-done((bf16[192,256]{1,0:T(8,128)(2,1)S(1)}, bf16[192,256]{1,0:T(8,128)(2,1)S(1)}, u32[]{:S(2)}, u32[]{:S(2)}) %collective-permute-start.41) | collective-permute-done | bytes 98336 | tf_op jit(solution)/shard_map/ppermute | solution.py:327
  51.8 2.8 %collective-permute-start.43 = (bf16[96,256]{1,0:T(8,128)(2,1)S(1)}, bf16[96,256]{1,0:T(8,128)(2,1)S(1)}, u32[]{:S(2)}, u32[]{:S(2)}) collective-permute-start(bf16[96,256]{1,0:T(8,128)(2,1)S(1)} %slice.49), channel_id=1, source_target_pairs={{0,112},{8,120},{16,0},{24,8},{32,16},{40,24},{48,32},{56,40},{64,... | collective-permute-start | bytes 147464 | tf_op jit(solution)/shard_map/ppermute | solution.py:327
  54.7 4.1 %collective-permute-done.42 = bf16[96,256]{1,0:T(8,128)(2,1)S(1)} collective-permute-done((bf16[96,256]{1,0:T(8,128)(2,1)S(1)}, bf16[96,256]{1,0:T(8,128)(2,1)S(1)}, u32[]{:S(2)}, u32[]{:S(2)}) %collective-permute-start.42) | collective-permute-done | bytes 49184 | tf_op jit(solution)/shard_map/ppermute | solution.py:327
  58.9 4.8 %collective-permute-start.44 = (bf16[1536,256]{1,0:T(8,128)(2,1)S(1)}, bf16[1536,256]{1,0:T(8,128)(2,1)S(1)}, u32[]{:S(2)}, u32[]{:S(2)}) collective-permute-start(bf16[1536,256]{1,0:T(8,128)(2,1)S(1)} %constant_dynamic-update-slice_fusion.refs_0_), channel_id=1, source_target_pairs={{0,1},{1,0},{2,3},{3,2},{4,5},{5,4},{6,7},{7,6},{8,9},{9,8},{10,11... | collective-permute-start | bytes 2359304 | tf_op jit(solution)/shard_map/ppermute | solution.py:281
  63.7 1.8 %collective-permute-done.44.refs_1_ = bf16[1536,256]{1,0:T(8,128)(2,1)S(1)} collective-permute-done((bf16[1536,256]{1,0:T(8,128)(2,1)S(1)}, bf16[1536,256]{1,0:T(8,128)(2,1)S(1)}, u32[]{:S(2)}, u32[]{:S(2)}) %collective-permute-start.44) | collective-permute-done | bytes 786464 | tf_op jit(solution)/shard_map/ppermute | solution.py:281
  65.6 18.4 %shard_map.113 = (bf16[2,192,1024]{2,1,0:T(8,128)(2,1)S(1)}, f32[1536,256]{1,0:T(8,128)S(1)}, bf16[1536,256]{1,0:T(8,128)(2,1)S(1)}) custom-call(s32[192]{0:T(256)S(1)} %get-tuple-element.197.order_ref, s32[3]{0:T(128)S(1)} %pad_add_fusion.meta_ref, bf16[1536,256]{1,0:T(8,128)(2,1)S(1)} %constant_dynamic-update-slice_fusion.refs_0_, ...), custom_call_target="tpu_custom_call" | custom-call | tf_op jit(solution)/shard_map/pallas_call | solution.py:171
  84.5 1.9 %collective-permute-done.45 = bf16[1536,256]{1,0:T(8,128)(2,1)S(1)} collective-permute-done((bf16[1536,256]{1,0:T(8,128)(2,1)S(1)}, bf16[1536,256]{1,0:T(8,128)(2,1)S(1)}, u32[]{:S(2)}, u32[]{:S(2)}) %collective-permute-start.45) | collective-permute-done | bytes 786464 | tf_op jit(solution)/shard_map/ppermute | solution.py:281
  86.4 1.1 add_convert_fusion
  87.5 3.5 %all-to-all-start = ((bf16[8,192,256]{2,1,0:T(8,128)(2,1)}), bf16[8,192,256]{2,1,0:T(8,128)(2,1)S(1)}, u32[]{:S(2)}, u32[]{:S(2)}) async-start(bf16[8,192,256]{2,1,0:T(8,128)(2,1)} %bitcast.16), calls=%async_computation | async-start | bytes 1572864 | tf_op jit(solution)/shard_map/all_to_all | solution.py:340
  91.0 1.9 %collective-permute-start.46 = (bf16[2,192,1024]{2,1,0:T(8,128)(2,1)S(1)}, bf16[2,192,1024]{2,1,0:T(8,128)(2,1)S(1)}, u32[]{:S(2)}, u32[]{:S(2)}) collective-permute-start(bf16[2,192,1024]{2,1,0:T(8,128)(2,1)S(1)} %get-tuple-element.203), channel_id=1, source_target_pairs={{129,136},{131,138},{133,140},{135,142},{136,129},{138,131},{140,1... | collective-permute-start | bytes 2359304 | tf_op jit(solution)/shard_map/ppermute | solution.py:281
  93.1 1.2 collective-permute-done.28
  96.4 9.7 %collective-permute-done.46 = bf16[2,192,1024]{2,1,0:T(8,128)(2,1)S(1)} collective-permute-done((bf16[2,192,1024]{2,1,0:T(8,128)(2,1)S(1)}, bf16[2,192,1024]{2,1,0:T(8,128)(2,1)S(1)}, u32[]{:S(2)}, u32[]{:S(2)}) %collective-permute-start.46) | collective-permute-done | bytes 786464 | tf_op jit(solution)/shard_map/ppermute | solution.py:281
  106.1 1.0 fusion.36
  107.1 7.5 %all-to-all-done = bf16[8,192,256]{2,1,0:T(8,128)(2,1)S(1)} async-done(((bf16[8,192,256]{2,1,0:T(8,128)(2,1)}), bf16[8,192,256]{2,1,0:T(8,128)(2,1)S(1)}, u32[]{:S(2)}, u32[]{:S(2)}) %all-to-all-start) | async-done | bytes 786464 | tf_op jit(solution)/shard_map/all_to_all | solution.py:340
  114.7 1.9 %collective-permute-start.47 = (bf16[192,256]{1,0:T(8,128)(2,1)S(1)}, bf16[192,256]{1,0:T(8,128)(2,1)S(1)}, u32[]{:S(2)}, u32[]{:S(2)}) collective-permute-start(bf16[192,256]{1,0:T(8,128)(2,1)S(1)} %reduce_sum.32), channel_id=1, source_target_pairs={{128,128},{129,136},{130,130},{131,138},{132,132},{133,140},{134,1... | collective-permute-start | bytes 294920 | tf_op jit(solution)/shard_map/ppermute | solution.py:281
  116.6 0.7 fusion.38
  117.3 4.8 %collective-permute-done.47 = bf16[192,256]{1,0:T(8,128)(2,1)S(1)} collective-permute-done((bf16[192,256]{1,0:T(8,128)(2,1)S(1)}, bf16[192,256]{1,0:T(8,128)(2,1)S(1)}, u32[]{:S(2)}, u32[]{:S(2)}) %collective-permute-start.47) | collective-permute-done | bytes 98336 | tf_op jit(solution)/shard_map/ppermute | solution.py:281
  (64 shorter events, 7.6 us)
Async XLA Ops:
  4.0 13.6 %copy-start.3 = (s32[192]{0:T(256)S(1)}, s32[192]{0:T(256)}, u32[]{:S(2)}) copy-start(s32[192]{0:T(256)} %param.19) | copy-start | bytes 2308
  4.1 3.5 %collective-permute-start.21 = (bf16[384,256]{1,0:T(8,128)(2,1)S(1)}, bf16[384,256]{1,0:T(8,128)(2,1)S(1)}, u32[]{:S(2)}, u32[]{:S(2)}) collective-permute-start(bf16[384,256]{1,0:T(8,128)(2,1)S(1)} %get-tuple-element.147), channel_id=1, source_target_pairs={{48,112},{56,120},{112,48},{120,56},{49,113},{57,121},{113,49},{12... | collective-permute-start | bytes 589832 | tf_op jit(solution)/shard_map/cond/branch_3_fun/ppermute | solution.py:304
  4.9 3.4 %collective-permute-start.22 = (bf16[384,256]{1,0:T(8,128)(2,1)S(1)}, bf16[384,256]{1,0:T(8,128)(2,1)S(1)}, u32[]{:S(2)}, u32[]{:S(2)}) collective-permute-start(bf16[384,256]{1,0:T(8,128)(2,1)S(1)} %get-tuple-element.148), channel_id=1, source_target_pairs={{48,96},{56,104},{112,32},{120,40},{49,97},{57,105},{113,33},{121,... | collective-permute-start | bytes 589832 | tf_op jit(solution)/shard_map/cond/branch_3_fun/ppermute | solution.py:304
  5.6 3.4 %collective-permute-start.23 = (bf16[384,256]{1,0:T(8,128)(2,1)S(1)}, bf16[384,256]{1,0:T(8,128)(2,1)S(1)}, u32[]{:S(2)}, u32[]{:S(2)}) collective-permute-start(bf16[384,256]{1,0:T(8,128)(2,1)S(1)} %get-tuple-element.149), channel_id=1, source_target_pairs={{48,0},{56,8},{112,64},{120,72},{49,1},{57,9},{113,65},{121,73},{5... | collective-permute-start | bytes 589832 | tf_op jit(solution)/shard_map/cond/branch_3_fun/ppermute | solution.py:304
  6.2 2.8 %collective-permute-start.24 = (bf16[384,256]{1,0:T(8,128)(2,1)S(1)}, bf16[384,256]{1,0:T(8,128)(2,1)S(1)}, u32[]{:S(2)}, u32[]{:S(2)}) collective-permute-start(bf16[384,256]{1,0:T(8,128)(2,1)S(1)} %get-tuple-element.150), channel_id=1, source_target_pairs={{48,80},{56,88},{112,16},{120,24},{49,81},{57,89},{113,17},{121,25... | collective-permute-start | bytes 589832 | tf_op jit(solution)/shard_map/cond/branch_3_fun/ppermute | solution.py:304
  6.9 2.1 %collective-permute-start.25 = (bf16[384,256]{1,0:T(8,128)(2,1)S(1)}, bf16[384,256]{1,0:T(8,128)(2,1)S(1)}, u32[]{:S(2)}, u32[]{:S(2)}) collective-permute-start(bf16[384,256]{1,0:T(8,128)(2,1)S(1)} %get-tuple-element.151), channel_id=1, source_target_pairs={{48,16},{56,24},{112,80},{120,88},{49,17},{57,25},{113,81},{121,89... | collective-permute-start | bytes 589832 | tf_op jit(solution)/shard_map/cond/branch_3_fun/ppermute | solution.py:304
  7.6 1.4 %collective-permute-start.26 = (bf16[384,256]{1,0:T(8,128)(2,1)S(1)}, bf16[384,256]{1,0:T(8,128)(2,1)S(1)}, u32[]{:S(2)}, u32[]{:S(2)}) collective-permute-start(bf16[384,256]{1,0:T(8,128)(2,1)S(1)} %get-tuple-element.152), channel_id=1, source_target_pairs={{48,64},{56,72},{112,0},{120,8},{49,65},{57,73},{113,1},{121,9},{5... | collective-permute-start | bytes 589832 | tf_op jit(solution)/shard_map/cond/branch_3_fun/ppermute | solution.py:304
  8.3 0.7 collective-permute-start.27
  9.2 11.6 %collective-permute-start.34 = (bf16[192,1024]{1,0:T(8,128)(2,1)S(1)}, bf16[192,1024]{1,0:T(8,128)(2,1)S(1)}, u32[]{:S(2)}, u32[]{:S(2)}) collective-permute-start(bf16[192,1024]{1,0:T(8,128)(2,1)S(1)} %bitcast.46), channel_id=1, source_target_pairs={{129,136},{131,138},{133,140},{135,142},{136,129},{138,131},{140,1... | collective-permute-start | bytes 1179656 | tf_op jit(solution)/shard_map/ppermute | solution.py:281
  13.5 23.0 %collective-permute-start.33 = (bf16[192,1024]{1,0:T(8,128)(2,1)S(1)}, bf16[192,1024]{1,0:T(8,128)(2,1)S(1)}, u32[]{:S(2)}, u32[]{:S(2)}) collective-permute-start(bf16[192,1024]{1,0:T(8,128)(2,1)S(1)} %bitcast.50), channel_id=1, source_target_pairs={{128,128},{129,136},{130,130},{131,138},{132,132},{133,140},{134,1... | collective-permute-start | bytes 1179656 | tf_op jit(solution)/shard_map/ppermute | solution.py:281
  16.3 20.3 %collective-permute-start.32 = (bf16[384,256]{1,0:T(8,128)(2,1)S(1)}, bf16[384,256]{1,0:T(8,128)(2,1)S(1)}, u32[]{:S(2)}, u32[]{:S(2)}) collective-permute-start(bf16[384,256]{1,0:T(8,128)(2,1)S(1)} %get-tuple-element.235), channel_id=1, source_target_pairs={{0,128},{1,136},{2,130},{3,138},{4,132},{5,140},{6,134},{7,142},{8... | collective-permute-start | bytes 589832 | tf_op jit(solution)/shard_map/ppermute | solution.py:281
  36.5 1.4 %collective-permute-start.35 = (bf16[192,256]{1,0:T(8,128)(2,1)S(1)}, bf16[192,256]{1,0:T(8,128)(2,1)S(1)}, u32[]{:S(2)}, u32[]{:S(2)}) collective-permute-start(bf16[192,256]{1,0:T(8,128)(2,1)S(1)} %broadcast_select_fusion.1), channel_id=1, source_target_pairs={{0,1},{1,0},{2,3},{3,2},{4,5},{5,4},{6,7},{7,6},{8,9},{9,8},{10,11... | collective-permute-start | bytes 294920 | tf_op jit(solution)/shard_map/ppermute | solution.py:281
  38.0 4.3 %collective-permute-start.37 = (bf16[192,256]{1,0:T(8,128)(2,1)S(1)}, bf16[192,256]{1,0:T(8,128)(2,1)S(1)}, u32[]{:S(2)}, u32[]{:S(2)}) collective-permute-start(bf16[192,256]{1,0:T(8,128)(2,1)S(1)} %get-tuple-element.216), channel_id=1, source_target_pairs={{0,112},{8,120},{16,0},{24,8},{32,16},{40,24},{48,32},{56,40},{64,... | collective-permute-start | bytes 294920 | tf_op jit(solution)/shard_map/ppermute | solution.py:327
  39.8 5.5 %collective-permute-start.36 = (bf16[192,256]{1,0:T(8,128)(2,1)S(1)}, bf16[192,256]{1,0:T(8,128)(2,1)S(1)}, u32[]{:S(2)}, u32[]{:S(2)}) collective-permute-start(bf16[192,256]{1,0:T(8,128)(2,1)S(1)} %get-tuple-element.216), channel_id=1, source_target_pairs={{0,16},{8,24},{16,32},{24,40},{32,48},{40,56},{48,64},{56,72},{64,... | collective-permute-start | bytes 294920 | tf_op jit(solution)/shard_map/ppermute | solution.py:327
  42.3 5.7 %collective-permute-start.39 = (bf16[192,256]{1,0:T(8,128)(2,1)S(1)}, bf16[192,256]{1,0:T(8,128)(2,1)S(1)}, u32[]{:S(2)}, u32[]{:S(2)}) collective-permute-start(bf16[192,256]{1,0:T(8,128)(2,1)S(1)} %collective-permute-done.37), channel_id=1, source_target_pairs={{0,112},{8,120},{16,0},{24,8},{32,16},{40,24},{48,32},{56,40},{64,... | collective-permute-start | bytes 294920 | tf_op jit(solution)/shard_map/ppermute | solution.py:327
  45.2 4.7 %collective-permute-start.38 = (bf16[192,256]{1,0:T(8,128)(2,1)S(1)}, bf16[192,256]{1,0:T(8,128)(2,1)S(1)}, u32[]{:S(2)}, u32[]{:S(2)}) collective-permute-start(bf16[192,256]{1,0:T(8,128)(2,1)S(1)} %collective-permute-done.36), channel_id=1, source_target_pairs={{0,16},{8,24},{16,32},{24,40},{32,48},{40,56},{48,64},{56,72},{64,... | collective-permute-start | bytes 294920 | tf_op jit(solution)/shard_map/ppermute | solution.py:327
  48.0 3.8 %collective-permute-start.41 = (bf16[192,256]{1,0:T(8,128)(2,1)S(1)}, bf16[192,256]{1,0:T(8,128)(2,1)S(1)}, u32[]{:S(2)}, u32[]{:S(2)}) collective-permute-start(bf16[192,256]{1,0:T(8,128)(2,1)S(1)} %collective-permute-done.39), channel_id=1, source_target_pairs={{0,112},{8,120},{16,0},{24,8},{32,16},{40,24},{48,32},{56,40},{64,... | collective-permute-start | bytes 294920 | tf_op jit(solution)/shard_map/ppermute | solution.py:327
  49.9 4.7 %collective-permute-start.40 = (bf16[192,256]{1,0:T(8,128)(2,1)S(1)}, bf16[192,256]{1,0:T(8,128)(2,1)S(1)}, u32[]{:S(2)}, u32[]{:S(2)}) collective-permute-start(bf16[192,256]{1,0:T(8,128)(2,1)S(1)} %collective-permute-done.38), channel_id=1, source_target_pairs={{0,16},{8,24},{16,32},{24,40},{32,48},{40,56},{48,64},{56,72},{64,... | collective-permute-start | bytes 294920 | tf_op jit(solution)/shard_map/ppermute | solution.py:327
  51.8 7.1 %collective-permute-start.43 = (bf16[96,256]{1,0:T(8,128)(2,1)S(1)}, bf16[96,256]{1,0:T(8,128)(2,1)S(1)}, u32[]{:S(2)}, u32[]{:S(2)}) collective-permute-start(bf16[96,256]{1,0:T(8,128)(2,1)S(1)} %slice.49), channel_id=1, source_target_pairs={{0,112},{8,120},{16,0},{24,8},{32,16},{40,24},{48,32},{56,40},{64,... | collective-permute-start | bytes 147464 | tf_op jit(solution)/shard_map/ppermute | solution.py:327
  54.6 4.2 %collective-permute-start.42 = (bf16[96,256]{1,0:T(8,128)(2,1)S(1)}, bf16[96,256]{1,0:T(8,128)(2,1)S(1)}, u32[]{:S(2)}, u32[]{:S(2)}) collective-permute-start(bf16[96,256]{1,0:T(8,128)(2,1)S(1)} %slice.48), channel_id=1, source_target_pairs={{0,16},{8,24},{16,32},{24,40},{32,48},{40,56},{48,64},{56,72},{64,... | collective-permute-start | bytes 147464 | tf_op jit(solution)/shard_map/ppermute | solution.py:327
  58.9 6.7 %collective-permute-start.44 = (bf16[1536,256]{1,0:T(8,128)(2,1)S(1)}, bf16[1536,256]{1,0:T(8,128)(2,1)S(1)}, u32[]{:S(2)}, u32[]{:S(2)}) collective-permute-start(bf16[1536,256]{1,0:T(8,128)(2,1)S(1)} %constant_dynamic-update-slice_fusion.refs_0_), channel_id=1, source_target_pairs={{0,1},{1,0},{2,3},{3,2},{4,5},{5,4},{6,7},{7,6},{8,9},{9,8},{10,11... | collective-permute-start | bytes 2359304 | tf_op jit(solution)/shard_map/ppermute | solution.py:281
  63.7 29.2 %copy-start.1 = (bf16[1,2,256]{2,1,0:T(2,128)(2,1)S(1)}, bf16[1,2,256]{2,1,0:T(2,128)(2,1)}, u32[]{:S(2)}) copy-start(bf16[1,2,256]{2,1,0:T(2,128)(2,1)} %param.15) | copy-start | bytes 3076
  63.7 29.2 %copy-start.2 = (s32[32]{0:T(128)S(1)}, s32[32]{0:T(128)}, u32[]{:S(2)}) copy-start(s32[32]{0:T(128)} %lengths_ref.1) | copy-start | bytes 388
  63.7 29.3 %copy-start.5 = (bf16[1,2,1024]{2,1,0:T(2,128)(2,1)S(1)}, bf16[1,2,1024]{2,1,0:T(2,128)(2,1)}, u32[]{:S(2)}) copy-start(bf16[1,2,1024]{2,1,0:T(2,128)(2,1)} %param.16) | copy-start | bytes 12292
  84.0 2.4 %collective-permute-start.45 = (bf16[1536,256]{1,0:T(8,128)(2,1)S(1)}, bf16[1536,256]{1,0:T(8,128)(2,1)S(1)}, u32[]{:S(2)}, u32[]{:S(2)}) collective-permute-start(bf16[1536,256]{1,0:T(8,128)(2,1)S(1)} %get-tuple-element.202), channel_id=1, source_target_pairs={{0,1},{1,0},{2,3},{3,2},{4,5},{5,4},{6,7},{7,6},{8,9},{9,8},{10,11... | collective-permute-start | bytes 2359304 | tf_op jit(solution)/shard_map/ppermute | solution.py:281
  87.5 27.1 %all-to-all-start = ((bf16[8,192,256]{2,1,0:T(8,128)(2,1)}), bf16[8,192,256]{2,1,0:T(8,128)(2,1)S(1)}, u32[]{:S(2)}, u32[]{:S(2)}) async-start(bf16[8,192,256]{2,1,0:T(8,128)(2,1)} %bitcast.16), calls=%async_computation | async-start | bytes 1572864 | tf_op jit(solution)/shard_map/all_to_all | solution.py:340
  91.0 15.1 %collective-permute-start.46 = (bf16[2,192,1024]{2,1,0:T(8,128)(2,1)S(1)}, bf16[2,192,1024]{2,1,0:T(8,128)(2,1)S(1)}, u32[]{:S(2)}, u32[]{:S(2)}) collective-permute-start(bf16[2,192,1024]{2,1,0:T(8,128)(2,1)S(1)} %get-tuple-element.203), channel_id=1, source_target_pairs={{129,136},{131,138},{133,140},{135,142},{136,129},{138,131},{140,1... | collective-permute-start | bytes 2359304 | tf_op jit(solution)/shard_map/ppermute | solution.py:281
  93.0 1.3 %collective-permute-start.28 = (f32[2,2560]{1,0:T(2,128)S(1)}, f32[2,2560]{1,0:T(2,128)S(1)}, u32[]{:S(2)}, u32[]{:S(2)}) collective-permute-start(f32[2,2560]{1,0:T(2,128)S(1)} %get-tuple-element.236), channel_id=1, source_target_pairs={{0,1},{1,0},{2,3},{3,2},{4,5},{5,4},{6,7},{7,6},{8,9},{9,8},{10,11... | collective-permute-start | bytes 61448 | tf_op jit(solution)/shard_map/ppermute | solution.py:281
  94.3 0.7 collective-permute-start.29
  95.0 0.7 collective-permute-start.30
  95.7 20.9 %collective-permute-start.31 = (f32[2,2560]{1,0:T(2,128)S(1)}, f32[2,2560]{1,0:T(2,128)S(1)}, u32[]{:S(2)}, u32[]{:S(2)}) collective-permute-start(f32[2,2560]{1,0:T(2,128)S(1)} %collective-permute-done.30), channel_id=1, source_target_pairs={{0,2},{1,3},{2,4},{3,5},{4,6},{5,7},{6,0},{7,1},{8,10},{9,11},{10,... | collective-permute-start | bytes 61448 | tf_op jit(solution)/shard_map/ppermute | solution.py:281
  114.7 7.4 %collective-permute-start.47 = (bf16[192,256]{1,0:T(8,128)(2,1)S(1)}, bf16[192,256]{1,0:T(8,128)(2,1)S(1)}, u32[]{:S(2)}, u32[]{:S(2)}) collective-permute-start(bf16[192,256]{1,0:T(8,128)(2,1)S(1)} %reduce_sum.32), channel_id=1, source_target_pairs={{128,128},{129,136},{130,130},{131,138},{132,132},{133,140},{134,1... | collective-permute-start | bytes 294920 | tf_op jit(solution)/shard_map/ppermute | solution.py:281
  (2 other events, 14.6 us)
